TPU v7x, 32 devices: a whole 2x2x4 slice. The times are simulated.
32 devices in a mesh: member: 2 (over x), gx: 16 (over z, y, core).
Axes of the slice: x: 2, y: 2, z: 4, core: 2. Of those that a mesh axis runs over, the one named last changes fastest.
Arguments:
- thermal_state: float32 [16, 1024, 1024], P('member', 'gx'), parts along dimension 0, may hold values from -6 to 6
- seawater_drift: float32 [4, 1024, 1024], P('member', 'gx'), parts along dimension 0, may hold values from -3 to 3
- sea_site_indicator: int32 [1024, 1024], P('gx'), may hold values 0 or 1
- chosen_tile_numbers: int32 [128], P(('member', 'gx')), parts along dimension 0, may hold values from 0 to 255, as said below
- chosen_floe_indicator: int32 [128, 4096], P(('member', 'gx')), parts along dimension 0, may hold values 0 or 1
- areal_fraction: float32 [128, 5, 4096], P(('member', 'gx')), parts along dimension 0, may hold values from 0 to 0.2
- thickness_amount: float32 [128, 5, 4096], P(('member', 'gx')), parts along dimension 0, may hold values from 0.1 to 1.5
- floe_motion: float32 [128, 2, 4096], P(('member', 'gx')), parts along dimension 0, may hold values from -3 to 3
- internal_traction: float32 [128, 3, 4096], P(('member', 'gx')), parts along dimension 0, may hold values from -6 to 6
- wind_traction: float32 [128, 2, 4096], P(('member', 'gx')), parts along dimension 0, may hold values from -3 to 3
Outputs:
- sea_warmth_later: float32 [16, 1024, 1024], P('member', 'gx'), parts along dimension 0
- topmost_drift_later: float32 [4, 1024, 1024], P('member', 'gx'), parts along dimension 0
- floe_drift_later: float32 [128, 2, 4096], P(('member', 'gx')), parts along dimension 0
- floe_traction_later: float32 [128, 3, 4096], P(('member', 'gx')), parts along dimension 0
- thickness_class_amount_later: float32 [128, 5, 4096], P(('member', 'gx')), parts along dimension 0
There are 2 independent parts, one for each index of `member`. A program takes and returns all parts, laid end to end along the dimension named above; an argument that names none is the same for every part. Nothing has to cross between parts.
Inputs may be any that keep to these rules, and one draw needn't show every extreme that they name: `chosen_tile_numbers`: distinct block numbers, listed in no particular order; row q is owned by index q // 4 of gx. No tile column (block number // 16) holds more than 8 listed blocks, and some column holds exactly 8.
All inputs are finite; a program needn't handle non-finite values. No bound on the sum of `sea_site_indicator` or of `chosen_floe_indicator` on one device may be relied on, other than what follows from the above.
Results may differ from a plain program's by a relative error of at most 0.0017.
Values may be sent and summed in bfloat16 or wider, within the bound.
No kernel may reach another device: no remote copies, remote signals or barrier semaphores. Data moves between devices by JAX's collectives and lax.ppermute only.
A program may use at most 128 MiB of HBM per device.

v0:
```python
import jax
import jax.numpy as jnp
from jax import lax
from jax.sharding import PartitionSpec as P

BS = 64
SUBCYCLES = 4
KMAX = 8


step_evp = 1.0
damping = 1.0
drag_water = 1.0
coriolis = 0.5
strength_scale = 2.0
strength_decay = 5.0
ecc_square = 4.0
delta_floor = 0.1
growth_rate = 0.5
freezing = -1.8
sideways_spreading_coefficient = 0.2
depthwise_spreading_coefficient = 0.2
heat_gain = 1.0
stress_gain = 1.0


def extended(cells, sides, width):
    for axis, dim in sides:
        count = lax.axis_size(axis)
        head = lax.slice_in_dim(cells, 0, width, axis=dim)
        tail = lax.slice_in_dim(cells, cells.shape[dim] - width, cells.shape[dim], axis=dim)
        cells = jnp.concatenate(
            [
                lax.ppermute(tail, axis, [(i, (i + 1) % count) for i in range(count)]),
                cells,
                lax.ppermute(head, axis, [((i + 1) % count, i) for i in range(count)]),
            ],
            axis=dim,
        )
    return cells


def edge_rims(field, tile_span):
    return jnp.stack(
        [
            field[..., :tile_span],
            field[..., -tile_span:],
            field[..., 0::tile_span],
            field[..., tile_span - 1 :: tile_span],
        ],
        1,
    )


def locate(all_ids, target, allowed):
    matches = all_ids[None, :] == target[:, None]
    present = (jnp.any(matches, 1) & allowed).astype(jnp.float32)
    positions = jnp.arange(all_ids.shape[0], dtype=jnp.int32)[None, :]
    row_index = jnp.sum(jnp.where(matches, positions, 0), 1)
    return (row_index, present)


def pick_halos(gathered, lookups, tile_span):
    rim_table = gathered.reshape(gathered.shape[0], 4, -1, tile_span)
    halo_list = []
    for rim_number, lookup in zip((1, 0, 3, 2), lookups):
        row_index, present = lookup
        taken = jnp.take(rim_table[:, rim_number], row_index, axis=1)
        halo_list.append(taken * present[None, :, None])
    return halo_list


def neighbour_values(field, halo_list, tile_span):
    cells = field.shape[-1]
    west_halo, east_halo, south_halo, north_halo = halo_list
    at_west = jnp.concatenate([west_halo, field[..., : cells - tile_span]], -1)
    at_east = jnp.concatenate([field[..., tile_span:], east_halo], -1)
    position = jnp.arange(cells) % tile_span
    blank = jnp.zeros_like(field[..., :1])
    below = jnp.concatenate([blank, field[..., :-1]], -1)
    above = jnp.concatenate([field[..., 1:], blank], -1)
    at_south = jnp.where(position == 0, jnp.repeat(south_halo, tile_span, axis=-1), below)
    at_north = jnp.where(
        position == tile_span - 1, jnp.repeat(north_halo, tile_span, axis=-1), above
    )
    return (at_east, at_west, at_north, at_south)


def local(
    thermal_state,
    seawater_drift,
    sea_site_indicator,
    chosen_tile_numbers,
    chosen_floe_indicator,
    areal_fraction,
    thickness_amount,
    floe_motion,
    internal_traction,
    wind_traction,
):
    columns_total = lax.axis_size("gx")
    my_column = lax.axis_index("gx")
    tile_span = BS
    cells = tile_span * tile_span
    owned_blocks = chosen_tile_numbers.shape[0]
    tiles_across = thermal_state.shape[2] // tile_span
    all_ids = lax.all_gather(chosen_tile_numbers, "gx", axis=0, tiled=True)
    listed = all_ids.shape[0]
    block_column = all_ids // tiles_across
    same_column = block_column[None, :] == block_column[:, None]
    column_rank = jnp.sum(
        (same_column & (all_ids[None, :] < all_ids[:, None])).astype(jnp.int32), 1
    )
    slot_number = jnp.arange(KMAX, dtype=jnp.int32)
    slot_match = (block_column[None, :] == my_column) & (
        column_rank[None, :] == slot_number[:, None]
    )
    slot_live = jnp.any(slot_match, 1)
    positions = jnp.arange(listed, dtype=jnp.int32)
    slot_row = jnp.sum(jnp.where(slot_match, positions[None, :], 0), 1)
    slot_block = jnp.clip(
        jnp.take(all_ids, slot_row) - my_column * tiles_across, 0, tiles_across - 1
    )
    topmost_region = jnp.stack([thermal_state[0], seawater_drift[0], seawater_drift[1]]).astype(
        jnp.bfloat16
    )

    def cut_block(block_row):
        block_piece = lax.dynamic_slice_in_dim(topmost_region, block_row * tile_span, tile_span, 2)
        return block_piece.reshape(3, cells)

    slot_fields = jax.vmap(cut_block)(slot_block) * slot_live[:, None, None].astype(jnp.bfloat16)
    my_columns = chosen_tile_numbers // tiles_across
    my_rows = chosen_tile_numbers % tiles_across
    my_global_rows = my_column * owned_blocks + jnp.arange(owned_blocks, dtype=jnp.int32)
    my_slots = my_columns * KMAX + jnp.take(column_rank, my_global_rows)
    shard_piece = lax.all_gather(slot_fields, "gx", axis=0, tiled=True)
    selector = (
        my_slots[:, None] == jnp.arange(shard_piece.shape[0], dtype=jnp.int32)[None, :]
    ).astype(jnp.bfloat16)
    surface = jnp.einsum("br,rfc->bfc", selector, shard_piece, preferred_element_type=jnp.float32)
    sea_temp, ocean_u, ocean_v = (surface[:, 0], surface[:, 1], surface[:, 2])
    sea_water_indicator = sea_site_indicator.astype(jnp.float32)
    state_group = jnp.concatenate([thermal_state, seawater_drift], 0)
    padded = extended(state_group, (("gx", 1),), 1)
    blank_row = jnp.zeros_like(state_group[..., :1])
    lateral = (
        padded[:, 2:]
        + padded[:, :-2]
        + jnp.concatenate([state_group[..., 1:], blank_row], -1)
        + jnp.concatenate([blank_row, state_group[..., :-1]], -1)
        - 4.0 * state_group
    )
    sea_slabs = thermal_state.shape[0]
    topmost_slab = thermal_state[1:] - thermal_state[:-1]
    vacant_slab = jnp.zeros_like(thermal_state[:1])
    depthwise_blending = jnp.concatenate([topmost_slab, vacant_slab], 0) - jnp.concatenate(
        [vacant_slab, topmost_slab], 0
    )
    change_speed = (
        sideways_spreading_coefficient * lateral[:sea_slabs]
        + depthwise_spreading_coefficient * depthwise_blending
    )
    ice_cells = chosen_floe_indicator.astype(jnp.float32)
    ice_cover = jnp.sum(areal_fraction, 1)
    thickness = jnp.sum(thickness_amount, 1)
    strength = strength_scale * thickness * jnp.exp(-strength_decay * (1.0 - ice_cover))
    inertia = thickness / step_evp
    always = jnp.ones((owned_blocks,), bool)
    lookups = (
        locate(all_ids, (my_columns - 1) % columns_total * tiles_across + my_rows, always),
        locate(all_ids, (my_columns + 1) % columns_total * tiles_across + my_rows, always),
        locate(all_ids, chosen_tile_numbers - 1, my_rows > 0),
        locate(all_ids, chosen_tile_numbers + 1, my_rows < tiles_across - 1),
    )
    ice_u, ice_v = (floe_motion[:, 0], floe_motion[:, 1])
    sigma_one, sigma_two, sigma_shear = (
        internal_traction[:, 0],
        internal_traction[:, 1],
        internal_traction[:, 2],
    )
    for subcycle in range(SUBCYCLES):
        stress_stack = jnp.stack([sigma_one, sigma_two, sigma_shear])
        stress_edges = edge_rims(stress_stack, tile_span).reshape(3, 4, owned_blocks * tile_span)
        stress_gathered = lax.all_gather(stress_edges, "gx", axis=2, tiled=True)
        at_east, at_west, at_north, at_south = neighbour_values(
            stress_stack, pick_halos(stress_gathered, lookups, tile_span), tile_span
        )
        force_x = 0.5 * (
            0.5 * (at_east[0] + at_east[1]) - 0.5 * (at_west[0] + at_west[1])
        ) + 0.5 * (at_north[2] - at_south[2])
        force_y = 0.5 * (at_east[2] - at_west[2]) + 0.5 * (
            0.5 * (at_north[0] - at_north[1]) - 0.5 * (at_south[0] - at_south[1])
        )
        denominator = inertia + drag_water
        new_u = (
            (
                inertia * ice_u
                + force_x
                + wind_traction[:, 0]
                + drag_water * ocean_u
                + coriolis * thickness * ice_v
            )
            / denominator
            * ice_cells
        )
        new_v = (
            (
                inertia * ice_v
                + force_y
                + wind_traction[:, 1]
                + drag_water * ocean_v
                - coriolis * thickness * ice_u
            )
            / denominator
            * ice_cells
        )
        ice_u, ice_v = (new_u, new_v)
        motion = jnp.stack([ice_u, ice_v])
        motion_edges = edge_rims(motion, tile_span).reshape(2, 4, owned_blocks * tile_span)
        motion_gathered = lax.all_gather(motion_edges, "gx", axis=2, tiled=True)
        at_east, at_west, at_north, at_south = neighbour_values(
            motion, pick_halos(motion_gathered, lookups, tile_span), tile_span
        )
        grad_ux = 0.5 * (at_east[0] - at_west[0])
        grad_vy = 0.5 * (at_north[1] - at_south[1])
        grad_uy = 0.5 * (at_north[0] - at_south[0])
        grad_vx = 0.5 * (at_east[1] - at_west[1])
        divergence = grad_ux + grad_vy
        tension = grad_ux - grad_vy
        shearing = grad_uy + grad_vx
        deform = jnp.sqrt(
            divergence * divergence
            + (tension * tension + shearing * shearing) / ecc_square
            + delta_floor * delta_floor
        )
        sigma_one = (
            (sigma_one + damping * strength * (divergence / deform - 1.0))
            / (1.0 + damping)
            * ice_cells
        )
        sigma_two = (
            (sigma_two + damping * strength * tension / (ecc_square * deform))
            / (1.0 + damping)
            * ice_cells
        )
        sigma_shear = (
            (sigma_shear + damping * strength * shearing / (2.0 * ecc_square * deform))
            / (1.0 + damping)
            * ice_cells
        )
    heat_excess = sea_temp - freezing
    category_bias = 1.5 - 0.5 * jnp.arange(thickness_amount.shape[1], dtype=jnp.float32)
    growth = (
        growth_rate
        * areal_fraction
        * (category_bias[None, :, None] - heat_excess[:, None, :])
        / (1.0 + thickness_amount)
        * ice_cells[:, None, :]
    )
    volume_updated = jnp.maximum(thickness_amount + growth, 0.0)
    heat_flux = jnp.sum(volume_updated - thickness_amount, 1)
    tau_x = drag_water * ice_cover * (ice_u - ocean_u) * ice_cells
    tau_y = drag_water * ice_cover * (ice_v - ocean_v) * ice_cells
    flux_blocks = jnp.stack([heat_flux, tau_x, tau_y], 1).astype(jnp.bfloat16)
    shard_piece = lax.all_gather(flux_blocks, "gx", axis=0, tiled=True)
    row_range = jnp.arange(shard_piece.shape[0], dtype=jnp.int32)
    selector = ((slot_row[:, None] == row_range[None, :]) & slot_live[:, None]).astype(jnp.bfloat16)
    slot_flux = jnp.einsum("kr,rfc->kfc", selector, shard_piece, preferred_element_type=jnp.float32)
    placement = (
        (slot_block[:, None] == jnp.arange(tiles_across, dtype=jnp.int32)[None, :])
        & slot_live[:, None]
    ).astype(jnp.float32)
    tile_flux = jnp.einsum(
        "kr,kfab->farb",
        placement,
        slot_flux.reshape(KMAX, 3, tile_span, tile_span),
        precision=lax.Precision.HIGHEST,
    )
    tile_flux = tile_flux.reshape(3, tile_span, tiles_across * tile_span)
    change_speed = change_speed.at[0].add(heat_gain * tile_flux[0])
    sea_warmth_later = thermal_state + sea_water_indicator * change_speed
    topmost_drift_later = seawater_drift + sea_water_indicator * (
        sideways_spreading_coefficient * lateral[sea_slabs:] + stress_gain * tile_flux[1:]
    )
    floe_drift_later = jnp.stack([ice_u, ice_v], 1)
    floe_traction_later = jnp.stack([sigma_one, sigma_two, sigma_shear], 1)
    return (
        sea_warmth_later,
        topmost_drift_later,
        floe_drift_later,
        floe_traction_later,
        volume_updated,
    )


def solution(mesh):
    return jax.shard_map(
        local,
        mesh=mesh,
        in_specs=(
            P("member", "gx", None),
            P("member", "gx", None),
            P("gx", None),
            P(("member", "gx")),
            P(("member", "gx"), None),
            P(("member", "gx"), None, None),
            P(("member", "gx"), None, None),
            P(("member", "gx"), None, None),
            P(("member", "gx"), None, None),
            P(("member", "gx"), None, None),
        ),
        out_specs=(
            P("member", "gx", None),
            P("member", "gx", None),
            P(("member", "gx"), None, None),
            P(("member", "gx"), None, None),
            P(("member", "gx"), None, None),
        ),
        check_vma=False,
    )
```

profile of v0, /device:TPU:0, one launch (start us, length us, event | category | flops | bytes accessed | tf_op | source)
XLA Modules:
  0.0 302.7 jit_solution(1861696435521379513)
XLA Ops:
  7.2 1.8 constant_dynamic-update-slice_fusion.1
  10.3 5.0 %collective-permute-start = (f32[10,1,1024]{2,1,0:T(1,128)}, f32[10,1,1024]{2,1,0:T(1,128)}, u32[]{:S(2)}, u32[]{:S(2)}) collective-permute-start(f32[10,1,1024]{2,1,0:T(1,128)} %get-tuple-element.84), channel_id=1, source_target_pairs={{1,0},{2,1},{3,2},{4,3},{5,4},{6,5},{7,6},{8,7},{9,8},{10,9},{11,1... | collective-permute-start | bytes 122888 | tf_op jit(solution)/shard_map/ppermute | solution.py:36
  15.3 1.0 slice.1867
  17.7 10.3 %all-reduce.21 = s32[64]{0:T(128)S(1)} all-reduce(s32[64]{0:T(128)S(1)} %dynamic-update-slice.3), channel_id=1, replica_groups=mesh['member'=2,'gx'=16] {'gx'}, use_global_device_ids=true, to_apply=%add.21 | all-reduce | flops 64 | bytes 512
  28.5 1.4 copy.366
  30.6 2.2 gather_fusion.2
  32.8 1.0 copy.367
  33.8 1.4 reshape.445
  36.1 3.8 %slice_subtract_fusion = f32[7,64,1024]{2,1,0:T(8,128)} fusion(f32[8,64,1024]{2,1,0:T(8,128)} %param.16), kind=kLoop, calls=%fused_computation.44 | loop fusion | flops 458752 | bytes 5505024 | tf_op jit(solution)/shard_map/sub | solution.py:155
  45.9 20.3 %all_gather.35 = f32[3,4,4096]{2,0,1:T(4,128)S(1)} all-gather(f32[3,4,256]{2,0,1:T(4,128)S(1)} %pad_maximum_fusion.30), channel_id=1, replica_groups=mesh['member'=2,'gx'=16] {'gx'}, dimensions={2}, use_global_device_ids=true | all-gather | bytes 208896 | tf_op jit(solution)/shard_map/all_gather | solution.py:185
  69.7 1.5 gather_fusion.5
  72.3 1.1 copy_bitcast_fusion.14
  80.0 2.2 fusion.3
  82.2 1.5 copy-done.2
  83.7 1.8 fusion.4
  85.6 2.5 fusion.240
  88.2 1.7 subtract_reduce_fusion
  91.5 18.0 %all_gather.36 = f32[2,4,4096]{2,1,0:T(4,128)S(1)} all-gather(f32[2,4,256]{2,1,0:T(4,128)S(1)} %pad_maximum_fusion.34), channel_id=1, replica_groups=mesh['member'=2,'gx'=16] {'gx'}, dimensions={2}, use_global_device_ids=true | all-gather | bytes 139264 | tf_op jit(solution)/shard_map/all_gather | solution.py:221
  115.5 19.5 %all_gather.37 = f32[3,4,4096]{2,0,1:T(4,128)S(1)} all-gather(f32[3,4,256]{2,0,1:T(4,128)S(1)} %pad_maximum_fusion.31), channel_id=1, replica_groups=mesh['member'=2,'gx'=16] {'gx'}, dimensions={2}, use_global_device_ids=true | all-gather | bytes 208896 | tf_op jit(solution)/shard_map/all_gather | solution.py:185
  141.1 17.8 %all_gather.38 = f32[2,4,4096]{2,1,0:T(4,128)S(1)} all-gather(f32[2,4,256]{2,1,0:T(4,128)S(1)} %pad_maximum_fusion.35), channel_id=1, replica_groups=mesh['member'=2,'gx'=16] {'gx'}, dimensions={2}, use_global_device_ids=true | all-gather | bytes 139264 | tf_op jit(solution)/shard_map/all_gather | solution.py:221
  165.0 19.5 %all_gather.39 = f32[3,4,4096]{2,0,1:T(4,128)S(1)} all-gather(f32[3,4,256]{2,0,1:T(4,128)S(1)} %pad_maximum_fusion.32), channel_id=1, replica_groups=mesh['member'=2,'gx'=16] {'gx'}, dimensions={2}, use_global_device_ids=true | all-gather | bytes 208896 | tf_op jit(solution)/shard_map/all_gather | solution.py:185
  190.6 18.0 %all_gather.40 = f32[2,4,4096]{2,1,0:T(4,128)S(1)} all-gather(f32[2,4,256]{2,1,0:T(4,128)S(1)} %pad_maximum_fusion.36), channel_id=1, replica_groups=mesh['member'=2,'gx'=16] {'gx'}, dimensions={2}, use_global_device_ids=true | all-gather | bytes 139264 | tf_op jit(solution)/shard_map/all_gather | solution.py:221
  214.7 19.5 %all_gather.41 = f32[3,4,4096]{2,0,1:T(4,128)S(1)} all-gather(f32[3,4,256]{2,0,1:T(4,128)S(1)} %pad_maximum_fusion.33), channel_id=1, replica_groups=mesh['member'=2,'gx'=16] {'gx'}, dimensions={2}, use_global_device_ids=true | all-gather | bytes 208896 | tf_op jit(solution)/shard_map/all_gather | solution.py:185
  241.9 17.9 %all_gather.43 = f32[2,4,4096]{2,1,0:T(4,128)S(1)} all-gather(f32[2,4,256]{2,1,0:T(4,128)S(1)} %pad_maximum_fusion.37), channel_id=1, replica_groups=mesh['member'=2,'gx'=16] {'gx'}, dimensions={2}, use_global_device_ids=true | all-gather | bytes 139264 | tf_op jit(solution)/shard_map/all_gather | solution.py:221
  265.4 14.4 %all-gather.5.cloned.1.call-done = bf16[64,3,4096]{2,1,0:T(4,128)(2,1)} async-done(((bf16[4,3,4096]{2,1,0:T(4,128)(2,1)}), bf16[64,3,4096]{2,1,0:T(4,128)(2,1)}) %all-gather.5.cloned.1.call-update) | async-done | bytes 1572880 | tf_op jit(solution)/shard_map/all_gather | solution.py:266
  279.8 3.3 %fusion.5 = f32[8,3,4096]{2,0,1:T(8,128)S(1)} fusion(bf16[64,3,4096]{2,1,0:T(4,128)(2,1)} %all-gather.5.cloned.1.call-done, s32[8]{0:T(128)S(1)} %copy-done.68, pred[8]{0:T(512)(128)(4,1)S(1)} %copy-done.70), kind=kOutput, calls=%fused_computation.45 | convolution fusion | flops 12583936 | bytes 1966120 | tf_op jit(solution)/shard_map/kr,rfc->kfc/dot_general | solution.py:269
  283.5 1.2 convolution_bitcast_fusion
  285.6 2.0 reshape.468
  287.6 1.1 slice.815
  288.7 1.8 fusion.11
  290.4 3.5 %multiply_add_fusion = f32[8,64,1024]{2,1,0:T(8,128)} fusion(f32[8,64,1024]{2,1,0:T(8,128)S(1)} %copy-done, f32[8,64,1024]{2,1,0:T(8,128)} %fusion.11, f32[64,1024]{1,0:T(8,128)S(1)} %convert_element_type.42), kind=kLoop, calls=%fused_computation.43 | loop fusion | flops 1048576 | bytes 6553600 | tf_op jit(solution)/shard_map/add | solution.py:282
  293.9 2.0 fusion.10
  (477 shorter events, 66.4 us)
Async XLA Ops:
  7.2 78.3 %all-gather.3.cloned.1.call-start = ((), (), s32[]{:S(2)}) async-start(), calls=%async_computation | async-start | bytes 3342336 | tf_op jit(solution)/shard_map/all_gather | solution.py:137
  9.8 70.2 %collective-permute-start.1 = (f32[10,1,1024]{2,1,0:T(1,128)}, f32[10,1,1024]{2,1,0:T(1,128)}, u32[]{:S(2)}, u32[]{:S(2)}) collective-permute-start(f32[10,1,1024]{2,1,0:T(1,128)} %get-tuple-element.85), channel_id=1, source_target_pairs={{0,1},{1,2},{2,3},{3,4},{4,5},{5,6},{6,7},{7,8},{8,9},{9,10},{10,1... | collective-permute-start | bytes 122888 | tf_op jit(solution)/shard_map/ppermute | solution.py:34
  10.3 69.7 %collective-permute-start = (f32[10,1,1024]{2,1,0:T(1,128)}, f32[10,1,1024]{2,1,0:T(1,128)}, u32[]{:S(2)}, u32[]{:S(2)}) collective-permute-start(f32[10,1,1024]{2,1,0:T(1,128)} %get-tuple-element.84), channel_id=1, source_target_pairs={{1,0},{2,1},{3,2},{4,3},{5,4},{6,5},{7,6},{8,7},{9,8},{10,9},{11,1... | collective-permute-start | bytes 122888 | tf_op jit(solution)/shard_map/ppermute | solution.py:36
  36.0 243.8 %all-gather.5.cloned.1.call-start = ((), (), s32[]{:S(2)}) async-start(), calls=%async_computation.1 | async-start | bytes 2228224 | tf_op jit(solution)/shard_map/all_gather | solution.py:266
  42.7 29.5 %copy-start.73 = (pred[4]{0:T(512)(128)(4,1)S(1)}, pred[4]{0:T(512)(128)(4,1)}, u32[]{:S(2)}) copy-start(pred[4]{0:T(512)(128)(4,1)} %get-tuple-element.51) | copy-start | bytes 16
  43.8 31.5 %copy-start.39 = (pred[4]{0:T(512)(128)(4,1)}, pred[4]{0:T(512)(128)(4,1)S(1)}, u32[]{:S(2)}) copy-start(pred[4]{0:T(512)(128)(4,1)S(1)} %get-tuple-element.199) | copy-start | bytes 16
  43.9 31.5 %copy-start.45 = (pred[4]{0:T(512)(128)(4,1)}, pred[4]{0:T(512)(128)(4,1)S(1)}, u32[]{:S(2)}) copy-start(pred[4]{0:T(512)(128)(4,1)S(1)} %get-tuple-element.198) | copy-start | bytes 16
  45.0 29.7 %copy-start.27 = (pred[4]{0:T(512)(128)(4,1)}, pred[4]{0:T(512)(128)(4,1)S(1)}, u32[]{:S(2)}) copy-start(pred[4]{0:T(512)(128)(4,1)S(1)} %get-tuple-element.201) | copy-start | bytes 16
  45.0 30.4 %copy-start.33 = (pred[4]{0:T(512)(128)(4,1)}, pred[4]{0:T(512)(128)(4,1)S(1)}, u32[]{:S(2)}) copy-start(pred[4]{0:T(512)(128)(4,1)S(1)} %get-tuple-element.200) | copy-start | bytes 16
  45.8 26.4 %copy-start.74 = (pred[4]{0:T(512)(128)(4,1)S(1)}, pred[4]{0:T(512)(128)(4,1)}, u32[]{:S(2)}) copy-start(pred[4]{0:T(512)(128)(4,1)} %get-tuple-element.53) | copy-start | bytes 16
  45.9 27.5 %copy-start.75 = (s32[4]{0:T(128)S(1)}, s32[4]{0:T(128)}, u32[]{:S(2)}) copy-start(s32[4]{0:T(128)} %compare_select_fusion.2) | copy-start | bytes 52
  90.2 23.3 %copy-start.28 = (pred[4]{0:T(512)(128)(4,1)S(1)}, pred[4]{0:T(512)(128)(4,1)}, u32[]{:S(2)}) copy-start(pred[4]{0:T(512)(128)(4,1)} %copy-done.27) | copy-start | bytes 16
  90.2 23.3 %copy-start.52 = (f32[4]{0:T(128)S(1)}, f32[4]{0:T(128)}, u32[]{:S(2)}) copy-start(f32[4]{0:T(128)} %copy-done.51) | copy-start | bytes 52
  90.4 23.4 %copy-start.9 = (f32[4,3,4096]{2,0,1:T(4,128)S(1)}, f32[4,3,4096]{2,0,1:T(4,128)}, u32[]{:S(2)}) copy-start(f32[4,3,4096]{2,0,1:T(4,128)} %param.24) | copy-start | bytes 589828
  163.6 23.1 %copy-start.23 = (f32[4]{0:T(128)S(1)}, f32[4]{0:T(128)}, u32[]{:S(2)}) copy-start(f32[4]{0:T(128)} %copy-done.21) | copy-start | bytes 52
  163.6 23.1 %copy-start.41 = (pred[4]{0:T(512)(128)(4,1)S(1)}, pred[4]{0:T(512)(128)(4,1)}, u32[]{:S(2)}) copy-start(pred[4]{0:T(512)(128)(4,1)} %copy-done.39) | copy-start | bytes 16
  164.4 23.5 %copy-start.35 = (pred[4]{0:T(512)(128)(4,1)S(1)}, pred[4]{0:T(512)(128)(4,1)}, u32[]{:S(2)}) copy-start(pred[4]{0:T(512)(128)(4,1)} %copy-done.33) | copy-start | bytes 16
  164.4 23.5 %copy-start.59 = (f32[4]{0:T(128)S(1)}, f32[4]{0:T(128)}, u32[]{:S(2)}) copy-start(f32[4]{0:T(128)} %copy-done.57) | copy-start | bytes 52
  164.4 24.3 %copy-start.29 = (pred[4]{0:T(512)(128)(4,1)S(1)}, pred[4]{0:T(512)(128)(4,1)}, u32[]{:S(2)}) copy-start(pred[4]{0:T(512)(128)(4,1)} %copy-done.27) | copy-start | bytes 16
  164.4 24.3 %copy-start.53 = (f32[4]{0:T(128)S(1)}, f32[4]{0:T(128)}, u32[]{:S(2)}) copy-start(f32[4]{0:T(128)} %copy-done.51) | copy-start | bytes 52
  189.3 23.3 %copy-start.30 = (pred[4]{0:T(512)(128)(4,1)S(1)}, pred[4]{0:T(512)(128)(4,1)}, u32[]{:S(2)}) copy-start(pred[4]{0:T(512)(128)(4,1)} %copy-done.27) | copy-start | bytes 16
  189.3 23.3 %copy-start.54 = (f32[4]{0:T(128)S(1)}, f32[4]{0:T(128)}, u32[]{:S(2)}) copy-start(f32[4]{0:T(128)} %copy-done.51) | copy-start | bytes 52
  213.3 23.1 %copy-start.43 = (pred[4]{0:T(512)(128)(4,1)S(1)}, pred[4]{0:T(512)(128)(4,1)}, u32[]{:S(2)}) copy-start(pred[4]{0:T(512)(128)(4,1)} %copy-done.39) | copy-start | bytes 16
  214.1 23.5 %copy-start.37 = (pred[4]{0:T(512)(128)(4,1)S(1)}, pred[4]{0:T(512)(128)(4,1)}, u32[]{:S(2)}) copy-start(pred[4]{0:T(512)(128)(4,1)} %copy-done.33) | copy-start | bytes 16
  214.2 23.5 %copy-start.61 = (f32[4]{0:T(128)S(1)}, f32[4]{0:T(128)}, u32[]{:S(2)}) copy-start(f32[4]{0:T(128)} %copy-done.57) | copy-start | bytes 52
  214.2 24.3 %copy-start.31 = (pred[4]{0:T(512)(128)(4,1)S(1)}, pred[4]{0:T(512)(128)(4,1)}, u32[]{:S(2)}) copy-start(pred[4]{0:T(512)(128)(4,1)} %copy-done.27) | copy-start | bytes 16
  214.2 24.3 %copy-start.55 = (f32[4]{0:T(128)S(1)}, f32[4]{0:T(128)}, u32[]{:S(2)}) copy-start(f32[4]{0:T(128)} %copy-done.51) | copy-start | bytes 52
  239.0 22.9 %copy-start.44 = (pred[4]{0:T(512)(128)(4,1)S(1)}, pred[4]{0:T(512)(128)(4,1)}, u32[]{:S(2)}) copy-start(pred[4]{0:T(512)(128)(4,1)} %copy-done.39) | copy-start | bytes 16
  239.2 23.8 %copy-start.38 = (pred[4]{0:T(512)(128)(4,1)S(1)}, pred[4]{0:T(512)(128)(4,1)}, u32[]{:S(2)}) copy-start(pred[4]{0:T(512)(128)(4,1)} %copy-done.33) | copy-start | bytes 16
  239.3 23.8 %copy-start.62 = (f32[4]{0:T(128)S(1)}, f32[4]{0:T(128)}, u32[]{:S(2)}) copy-start(f32[4]{0:T(128)} %copy-done.57) | copy-start | bytes 52
  239.7 24.3 %copy-start.32 = (pred[4]{0:T(512)(128)(4,1)S(1)}, pred[4]{0:T(512)(128)(4,1)}, u32[]{:S(2)}) copy-start(pred[4]{0:T(512)(128)(4,1)} %copy-done.27) | copy-start | bytes 16
  239.7 24.3 %copy-start.56 = (f32[4]{0:T(128)S(1)}, f32[4]{0:T(128)}, u32[]{:S(2)}) copy-start(f32[4]{0:T(128)} %copy-done.51) | copy-start | bytes 52
  (51 other events, 515.1 us)
Sparse Core Ops, SparseCore 0:
  36.1 45.0 all-gather.2
  240.8 38.9 all-gather.4
where the time goes:
time: 304 us; the launch traced here: 303 us
  blocking collectives  161 us (53%)
  local copies, waits for them, and re-layouts  63.5 us (21%)
  other arithmetic  34.9 us (11%)
  between operations  16.5 us (5%)
  waiting for transfers between devices  14.5 us (5%)
  matrix products  7.07 us (2%)
  starting transfers between devices  5.53 us (2%)
    all_gather x4, blocking collectives, local(): stress_gathered = lax.all_gather(stress_edges, 'gx', axis=2, tiled=True)  78.7 us
    all_gather x4, blocking collectives, local(): motion_gathered = lax.all_gather(motion_edges, 'gx', axis=2, tiled=True)  71.7 us
    gather x32, local copies, waits for them, and re-layouts, pick_halos(): taken = jnp.take(rim_table[:, rim_number], row_index, axis=1)  22.6 us
    all_gather x1, waiting for transfers between devices, local(): shard_piece = lax.all_gather(flux_blocks, 'gx', axis=0, tiled=True)  14.4 us
    unnamed x1, blocking collectives  10.3 us
    unnamed x191, local copies, waits for them, and re-layouts  6.91 us
  transfers between devices with their start and end apart: 4, of which 1 were waited for; matrix products, arithmetic and copies ran while one was open for 14% of the time, Pallas kernels for 0%

commit v1 on v0

v1 whole, which is shorter than its diff:
```python
import functools

import jax
import jax.numpy as jnp
import numpy as np
from jax import lax
from jax.experimental import pallas as pl
from jax.experimental.pallas import tpu as pltpu
from jax.sharding import PartitionSpec as P

BS = 64
SUBCYCLES = 4
KMAX = 8
M = 16
W = 8
NF = 9
ROWS1 = 176
ROWS2 = 128
ROWS3 = 32
ROWS4 = 48
RIM = 48
VMEM = 48 * 2**20
f32, bf16 = jnp.float32, jnp.bfloat16


def lanes(shape):
    return lax.broadcasted_iota(jnp.int32, shape, len(shape) - 1)


def roll(x, shift, axis=-1):
    axis = axis % x.ndim
    shift = shift % x.shape[axis]
    return x if shift == 0 else pltpu.roll(x, shift, axis)


def call(kernel, out_shape, scratch=(), in_specs=None, out_specs=None, **kw):
    return pl.pallas_call(
        kernel,
        out_shape=out_shape,
        in_specs=in_specs,
        out_specs=out_specs,
        scratch_shapes=list(scratch),
        compiler_params=pltpu.CompilerParams(vmem_limit_bytes=VMEM),
        **kw,
    )


def pack_kernel(ids, temp, drift, cells, conc, vol, motion, stress, wind, out, nat, rows, rim):
    tiles = temp.shape[2] // BS
    step = 512
    for start in range(0, BS * BS, step):
        sl = pl.ds(start, step)
        ice = cells[:, sl].astype(f32)
        cover = jnp.sum(conc[:, :, sl], axis=1)
        thick = jnp.sum(vol[:, :, sl], axis=1)
        nat[0, :, sl] = thick * ice
        nat[1, :, sl] = 2.0 * thick * jnp.exp(-5.0 * (1.0 - cover))
        nat[9, :, sl] = cover
        for k in range(2):
            nat[2 + k, :, sl] = wind[:, k, sl]
            nat[4 + k, :, sl] = motion[:, k, sl]
        for k in range(3):
            nat[6 + k, :, sl] = stress[:, k, sl]
    lane = lanes((4, 128))
    low, high = (lane & 63) < W, (lane & 63) >= BS - W
    which = lax.broadcasted_iota(jnp.int32, (4, 128), 0)
    listed = jnp.zeros((4, 128), f32)
    for q in range(4):
        number = ids[q]
        column, row = number // tiles, number % tiles
        pair = jnp.where(lane < 64, column, row).astype(f32)
        listed = jnp.where(which == q, pair, listed)
    rim[:, 36:40, :] = jnp.broadcast_to(listed[None], (M, 4, 128))
    rim[:, 40:48, :] = jnp.zeros((M, 8, 128), f32)
    for f in range(NF):
        at = slice(4 * f, 4 * f + 4)
        for k in range(4):
            rim[k, at, :] = nat[f, :, 128 * k : 128 * k + 128]
            rim[4 + k, at, :] = nat[f, :, 3584 + 128 * k : 3712 + 128 * k]
            first = jnp.zeros((4, 128), f32)
            last = jnp.zeros((4, 128), f32)
            for t in range(8):
                v = nat[f, :, 128 * (8 * k + t) : 128 * (8 * k + t) + 128]
                first = first + roll(jnp.where(low, v, 0.0), 8 * t)
                last = last + roll(jnp.where(high, v, 0.0), 8 * t)
            rim[8 + k, at, :] = first
            rim[12 + k, at, :] = last
    for m in range(M):
        start = (5 * m - W) % BS
        for k in range(2):
            left = min(5, BS - start)
            rows[5 * k : 5 * k + left, :] = drift[k, start : start + left, :]
            if left < 5:
                rows[5 * k + left : 5 * k + 5, :] = drift[k, 0 : 5 - left, :]
        rows[10:14, :] = temp[0, 4 * m : 4 * m + 4, :]
        rows[14:16, :] = jnp.zeros((2, rows.shape[1]), f32)
        tile = rows[...].astype(bf16)
        for part in range(8):
            out[m, 16 * part : 16 * part + 16, :] = tile[:, 128 * part : 128 * part + 128]
        out[m, 128:ROWS1, :] = rim[m].astype(bf16)


def route_kernel(count, me, got, everyone, table, out, s_sea, s_rim, row_of, acc):
    me_now = me[0]
    m = lax.rem(me_now, M)
    first = me_now - m
    east = m < 4
    west = jnp.logical_and(m >= 4, m < 8)
    north = jnp.logical_and(m >= 8, m < 12)
    shift_c = jnp.where(east, 1, jnp.where(west, -1, 0))
    shift_r = jnp.where(north, 1, jnp.where(m >= 12, -1, 0))
    lists = got[:, 160:176, :].reshape(M * 16, 128).astype(f32)
    number = lists[:, 0:1] * 16.0 + lists[:, 64:65]
    aim = table[0:1, :]
    hit = lax.broadcasted_iota(jnp.int32, (M * 16, M * RIM), 0) == aim
    number_lane = jnp.sum(jnp.where(hit, number, 0.0), axis=0, keepdims=True).astype(jnp.int32)
    code_one = jnp.where(aim >= 0, number_lane * 16 + table[1:2, :], -100)
    code_four = jnp.where(aim >= 0, number_lane * 16 + table[2:3, :], -100)
    lane = lanes((64, 128))
    part = lax.broadcasted_iota(jnp.int32, (64, 128), 0) >> 2

    def build(o, _):
        base = pl.multiple_of(o * 64, 64)
        here = everyone[o, everyone.shape[1] - 16 :, :]
        pick = lanes((64, 16)) == 4 + (lax.broadcasted_iota(jnp.int32, (64, 16), 0) & 3)
        both = jnp.dot(pick.astype(bf16), here, preferred_element_type=f32)
        other = roll(both, 64)
        column = jnp.where(lane < 64, both, other).astype(jnp.int32)
        row = jnp.where(lane < 64, other, both).astype(jnp.int32)
        row_of[pl.ds(base, 64), :] = row
        wide = 5 * m + jnp.where(part < 5, part, part - 5)
        delta = jnp.where(wide < W, -1, jnp.where(wide >= BS + W, 1, 0))
        delta = jnp.where(part >= 10, 0, delta)
        source = column + delta
        source = jnp.where(source < 0, source + count, source)
        source = jnp.where(source >= count, source - count, source) - first
        code = jnp.where((source >= 0) & (source < M) & (part < 14), source * 16 + part, -1)
        for k in range(2):
            s_sea[pl.ds(base, 64), 128 * k : 128 * k + 128] = (
                (lane + 128 * k) == code
            ).astype(bf16)
        tc = column + shift_c
        tc = jnp.where(tc < 0, tc + count, tc)
        tc = jnp.where(tc >= count, tc - count, tc)
        tr = row + shift_r
        one = jnp.where((tr >= 0) & (tr < 16) & (part < NF), (tc * 16 + tr) * 16 + part, -1)
        corner = (part >= NF) & (part < NF + 3)
        before = jnp.where(corner & (tr >= 1), (tc * 16 + tr - 1) * 16 + part - NF, -1)
        after = jnp.where(corner & (tr < 15), (tc * 16 + tr + 1) * 16 + part - NF, -1)
        span = M * RIM
        for k in range(span // 128):
            cut = slice(128 * k, 128 * k + 128)
            s_rim[pl.ds(base, 64), cut] = (code_one[:, cut] == one).astype(bf16)
            s_rim[pl.ds(base, 64), span + 128 * k : span + 128 * k + 128] = (
                code_four[:, cut] == before
            ).astype(bf16)
            s_rim[pl.ds(base, 64), 2 * span + 128 * k : 2 * span + 128 * k + 128] = (
                code_four[:, cut] == after
            ).astype(bf16)
        return 0

    lax.fori_loop(0, count, build, 0)

    rims = got[:, 128:ROWS1, :]
    wide_rims = rims.astype(f32)
    lane3 = lanes(wide_rims.shape)
    quarter = (lax.broadcasted_iota(jnp.int32, wide_rims.shape, 1) >> 2) & 3
    halves = []
    for mask in ((lane3 & 63) >= BS - W, (lane3 & 63) < W):
        kept = jnp.where(mask, wide_rims, 0.0)
        moved = kept
        for i in range(1, 4):
            moved = jnp.where(quarter == i, roll(kept, 16 * i), moved)
        halves.append(moved.astype(bf16).reshape(M * RIM, 128))
    span = M * RIM
    total = jnp.dot(s_rim[:, :span], rims.reshape(span, 128), preferred_element_type=f32)
    total = total + jnp.dot(s_rim[:, span : 2 * span], halves[0], preferred_element_type=f32)
    total = total + jnp.dot(s_rim[:, 2 * span :], halves[1], preferred_element_type=f32)
    out[:, 64:128, :] = total.astype(bf16).reshape(count, 64, 128)

    for k in range(8):
        sea = got[:, 16 * k : 16 * k + 16, :].reshape(M * 16, 128)
        value = jnp.dot(s_sea[...], sea, preferred_element_type=f32)
        place = 128 * k + lanes(value.shape) - row_of[...] * BS + W
        value = jnp.where((place >= 0) & (place < BS + 2 * W), value, 0.0)
        if k == 0:
            acc[...] = value
        else:
            acc[...] += value
    value = acc[...]
    value = jnp.where((row_of[...] & 1) == 1, roll(value, W + 64), roll(value, W))
    out[:, 0:64, :] = value.astype(bf16).reshape(count, 64, 128)


def ice_kernel(got, nat, conc, vol, motion, stress, grown, out, wide, ext, temp, flux):
    for m in range(M):
        wide[m] = got[m].astype(f32)
    lane = lanes((8, 128))
    lane4 = lanes((4, 128))

    def rim(m, j):
        return wide[m, 4 * j : 4 * j + 4, :]

    def two(a, b):
        return jnp.concatenate([a, b], axis=0)

    def natural(f, r):
        return two(
            nat[f, :, 128 * r : 128 * r + 128], nat[f, :, 128 * (r + 16) : 128 * (r + 16) + 128]
        )

    for f in range(11):
        ext[f, 0] = jnp.zeros((8, 128), f32)
        ext[f, 49] = jnp.zeros((8, 128), f32)
    for f in range(NF):
        for r in range(16):
            t = r % 8
            v = natural(f, r)
            north = two(rim(8 + r // 8, 16 + f), rim(10 + r // 8, 16 + f))
            south = two(rim(12 + r // 8, 16 + f), rim(14 + r // 8, 16 + f))
            for p in range(2):
                value = jnp.where(lane < 72, roll(v, 8 - 64 * p), roll(north, 72 - 64 * p - 8 * t))
                value = jnp.where(lane < 8, roll(south, -(56 + 64 * p + 8 * t)), value)
                ext[f, 1 + 8 + 2 * r + p] = value
        for y in range(8):
            p, i = y % 2, f % 4
            centre = two(rim(4 + y // 2, 16 + f), rim(y // 2, 16 + f))
            corner = two(
                rim(4 + y // 2, 16 + NF + f // 4), rim(y // 2, 16 + NF + f // 4)
            )
            value = jnp.where(
                lane < 72, roll(centre, 8 - 64 * p), roll(corner, 72 - 64 * p - 16 * i)
            )
            value = jnp.where(lane < 8, roll(corner, -(56 + 64 * p + 16 * i)), value)
            ext[f, 1 + y] = two(value[0:4], ext[f, 33 + y, 0:4, :])
            ext[f, 41 + y] = two(ext[f, 9 + y, 4:8, :], value[4:8])
    for y in range(48):
        for k in range(2):
            a, b = y, y + 32
            value = two(rim(a // 5, 5 * k + a % 5), rim(b // 5, 5 * k + b % 5))
            ext[9 + k, 1 + y] = value
            ext[2 + k, 1 + y] = ext[2 + k, 1 + y] + value
    thick = ext[0, 1:49]
    ext[11, 1:49] = jnp.where(thick > 0.0, 1.0 / (thick + 1.0), 0.0)
    ext[1, 1:49] = jnp.where(thick > 0.0, 0.5 * ext[1, 1:49], 0.0)

    step = 8

    def speed(i, _):
        at = pl.ds(1 + i * step, step)
        full = pl.ds(i * step, step + 2)
        one, two_, shear = ext[6, full], ext[7, full], ext[8, full]
        add = one + two_
        sub = one[1:-1] - two_[1:-1]
        mid = shear[1:-1]
        fx = 0.25 * (add[2:] - add[:-2]) + 0.5 * (roll(mid, -1) - roll(mid, 1))
        fy = 0.5 * (shear[2:] - shear[:-2]) + 0.25 * (roll(sub, -1) - roll(sub, 1))
        thick, inverse = ext[0, at], ext[11, at]
        u, v = ext[4, at], ext[5, at]
        half = 0.5 * thick
        ext[4, at] = (thick * u + fx + ext[2, at] + half * v) * inverse
        ext[5, at] = (thick * v + fy + ext[3, at] - half * u) * inverse
        return 0

    def strain(i, _):
        at = pl.ds(1 + i * step, step)
        full = pl.ds(i * step, step + 2)
        uu, vv = ext[4, full], ext[5, full]
        u, v = uu[1:-1], vv[1:-1]
        ux = uu[2:] - uu[:-2]
        vx = vv[2:] - vv[:-2]
        uy = roll(u, -1) - roll(u, 1)
        vy = roll(v, -1) - roll(v, 1)
        divergence = 0.5 * (ux + vy)
        tension = 0.5 * (ux - vy)
        shearing = 0.5 * (uy + vx)
        inverse = lax.rsqrt(
            divergence * divergence + 0.25 * (tension * tension + shearing * shearing) + 0.01
        )
        half = jnp.where(ext[0, at] > 0.0, 0.5, 0.0)
        strong = ext[1, at]
        scaled = strong * inverse
        ext[6, at] = half * ext[6, at] + (scaled * divergence - strong)
        ext[7, at] = half * ext[7, at] + 0.25 * scaled * tension
        ext[8, at] = half * ext[8, at] + 0.125 * scaled * shearing
        return 0

    for _ in range(SUBCYCLES):
        lax.fori_loop(0, 48 // step, speed, 0)
        lax.fori_loop(0, 48 // step, strain, 0)

    def flat(f, r):
        a, b = ext[f, 9 + 2 * r], ext[f, 10 + 2 * r]
        return jnp.where(lane < 64, roll(a, -8), roll(b, 56))

    for r in range(32):
        a, b = rim(r // 2, 10 + 2 * (r % 2)), rim(r // 2, 11 + 2 * (r % 2))
        temp[:, 128 * r : 128 * r + 128] = jnp.where(lane4 < 64, roll(a, -8), roll(b, 56))
    flux[:, 24:32, :] = jnp.zeros((M, 8, 128), f32)
    for r in range(16):
        for f in range(3):
            value = flat(6 + f, r)
            stress[:, f, 128 * r : 128 * r + 128] = value[0:4]
            stress[:, f, 128 * (r + 16) : 128 * (r + 16) + 128] = value[4:8]
        cover, ice = natural(9, r), natural(0, r) > 0.0
        for f in range(2):
            value = flat(4 + f, r)
            motion[:, f, 128 * r : 128 * r + 128] = value[0:4]
            motion[:, f, 128 * (r + 16) : 128 * (r + 16) + 128] = value[4:8]
            tau = jnp.where(ice, cover * (value - flat(9 + f, r)), 0.0)
            at = 4 * ((f + 1) * 2 + r % 2)
            flux[r // 2, at : at + 4, :] = tau[0:4]
            flux[8 + r // 2, at : at + 4, :] = tau[4:8]
    step = 512
    bias = 1.5 - 0.5 * lax.broadcasted_iota(jnp.int32, (conc.shape[1], step), 0).astype(f32)
    for q in range(4):
        for start in range(0, BS * BS, step):
            sl = pl.ds(start, step)
            volume = vol[q, :, sl]
            excess = temp[q : q + 1, sl] + 1.8
            ice = nat[0, q : q + 1, sl] > 0.0
            rate = 0.5 * conc[q, :, sl] * (bias - excess) / (1.0 + volume)
            later = jnp.maximum(volume + jnp.where(ice, rate, 0.0), 0.0)
            grown[q, :, sl] = later
            heat = jnp.sum(later - volume, axis=0, keepdims=True)
            for k in range(step // 128):
                r = start // 128 + k
                at = 4 * (r % 2) + q
                flux[r // 2, at : at + 1, :] = heat[:, 128 * k : 128 * k + 128]
    for m in range(M):
        out[m] = flux[m].astype(bf16)


def return_kernel(count, got, codes, out, pick):
    column = lax.broadcasted_iota(jnp.int32, (ROWS4, M * ROWS3), 0)
    local_code = (column & 7) * 8 + (column >> 3)
    span = codes[0:1, :]

    def build(c, _):
        base = pl.multiple_of(c * ROWS4, ROWS4)
        pick[pl.ds(base, ROWS4), :] = (span == local_code + c * 64).astype(bf16)
        return 0

    lax.fori_loop(0, count, build, 0)
    value = jnp.dot(pick[...], got[...].reshape(M * ROWS3, 128), preferred_element_type=f32)
    out[...] = value.astype(bf16).reshape(count, ROWS4, 128)


def ocean_kernel(temp, drift, wet, before, after, temp_out, drift_out):
    levels = temp.shape[0]
    shape = temp.shape[1:]
    lane = lanes(shape)
    row = lax.broadcasted_iota(jnp.int32, shape, 0)
    sea = wet[...].astype(f32)
    for k in range(levels + drift.shape[0]):
        mid = temp[k] if k < levels else drift[k - levels]
        east = jnp.where(row == shape[0] - 1, after[k], roll(mid, -1, 0))
        west = jnp.where(row == 0, before[k], roll(mid, 1, 0))
        north = jnp.where(lane == shape[1] - 1, 0.0, roll(mid, -1))
        south = jnp.where(lane == 0, 0.0, roll(mid, 1))
        change = 0.2 * (east + west + north + south - 4.0 * mid)
        if k < levels:
            vertical = jnp.zeros(shape, f32)
            if k + 1 < levels:
                vertical = vertical + (temp[k + 1] - mid)
            if k > 0:
                vertical = vertical - (mid - temp[k - 1])
            temp_out[k] = mid + sea * (change + 0.2 * vertical)
        else:
            drift_out[k - levels] = mid + sea * change


def final_kernel(rows, got, wet, temp, drift, temp_out, drift_out, wide, flux):
    for m in range(M):
        wide[pl.ds(ROWS4 * m, ROWS4), :] = got[m].astype(f32)
    flux[...] = jnp.zeros(flux.shape, f32)
    upper = lanes((M, 128)) >= 64
    for slot in range(KMAX):
        r = rows[slot]
        at = r // 2
        odd = lax.rem(r, 2) == 1
        keep = upper == odd
        for f in range(3):
            for h in range(2):
                value = wide[pl.ds(8 * (2 * f + h) + slot, M, stride=ROWS4), :]
                turned = roll(value, 64)
                for p in range(2):
                    chosen = jnp.where(odd, turned, value) if p == 0 else jnp.where(odd, value, turned)
                    to = (at, pl.ds(BS * f + 2 * h + p, M, stride=4), slice(None))
                    flux[to] = flux[to] + jnp.where(keep, chosen, 0.0)
    for part in range(flux.shape[0]):
        cut = slice(128 * part, 128 * part + 128)
        sea = wet[:, cut].astype(f32)
        temp_out[0, :, cut] = temp[0, :, cut] + sea * flux[part, 0:BS, :]
        for k in range(2):
            added = sea * flux[part, BS * (k + 1) : BS * (k + 2), :]
            drift_out[k, :, cut] = drift[k, :, cut] + added


def local(
    thermal_state,
    seawater_drift,
    sea_site_indicator,
    chosen_tile_numbers,
    chosen_floe_indicator,
    areal_fraction,
    thickness_amount,
    floe_motion,
    internal_traction,
    wind_traction,
):
    count = lax.axis_size("gx")
    groups = count // M
    me = lax.axis_index("gx")
    tiles = thermal_state.shape[2] // BS
    members = [[g * M + i for i in range(M)] for g in range(groups)]
    smem = pl.BlockSpec(memory_space=pltpu.SMEM)
    vmem = pl.BlockSpec(memory_space=pltpu.VMEM)
    depth, height = thermal_state.shape[1:]
    top = pl.BlockSpec((1, depth, height), lambda i: (0, 0, 0))

    def whole(x):
        return pl.BlockSpec(x.shape, lambda i, n=len(x.shape): (0,) * n)

    def within(x):
        if groups == 1:
            return lax.all_to_all(x, "gx", 0, 0, tiled=True)
        return lax.all_to_all(x, "gx", 0, 0, axis_index_groups=members, tiled=True)

    def across(x):
        x = lax.all_to_all(x, "gx", 0, 0, tiled=True)
        if groups == 1:
            return x
        return jnp.sum(x.reshape((groups, M) + x.shape[1:]).astype(f32), 0).astype(bf16)

    tail = jnp.concatenate([thermal_state[:, depth - 1 :], seawater_drift[:, depth - 1 :]], 0)
    head = jnp.concatenate([thermal_state[:, :1], seawater_drift[:, :1]], 0)
    before = lax.ppermute(tail, "gx", [(i, (i + 1) % count) for i in range(count)])
    after = lax.ppermute(head, "gx", [((i + 1) % count, i) for i in range(count)])

    arrays = (
        thermal_state,
        seawater_drift,
        chosen_floe_indicator,
        areal_fraction,
        thickness_amount,
        floe_motion,
        internal_traction,
        wind_traction,
    )
    nat_shape = jax.ShapeDtypeStruct((10, 4, BS * BS), f32)
    one_shape = jax.ShapeDtypeStruct((M, ROWS1, 128), bf16)
    payload, nat = call(
        pack_kernel,
        (one_shape, nat_shape),
        scratch=(pltpu.VMEM((16, height), f32), pltpu.VMEM((M, RIM, 128), f32)),
        grid=(1,),
        in_specs=[smem, top] + [whole(x) for x in arrays[1:]],
        out_specs=(whole(one_shape), whole(nat_shape)),
    )(chosen_tile_numbers, *arrays)
    got1 = within(payload)

    index = np.arange(M * RIM)
    source, place = index // RIM, index % RIM
    table = np.zeros((8, M * RIM), np.int32)
    table[0] = np.where(place < 4 * NF, source * 16 + 4 + place % 4, -1)
    table[1] = place // 4
    table[2] = place // 16
    if groups == 1:
        everyone = got1
    else:
        mine = payload[0, 160:176]
        everyone = lax.all_gather(mine, "gx", axis=0, tiled=False)
    payload2 = call(
        functools.partial(route_kernel, count),
        jax.ShapeDtypeStruct((count, ROWS2, 128), bf16),
        scratch=(
            pltpu.VMEM((count * 64, M * 16), bf16),
            pltpu.VMEM((count * 64, 3 * M * RIM), bf16),
            pltpu.VMEM((count * 64, 128), jnp.int32),
            pltpu.VMEM((count * 64, 128), f32),
        ),
        in_specs=[smem, vmem, vmem, vmem],
        out_specs=vmem,
    )(me.reshape(1).astype(jnp.int32), got1, everyone, jnp.asarray(table))
    got2 = across(payload2)

    pairs = everyone[:, everyone.shape[1] - 12 : everyone.shape[1] - 8, :].astype(f32)
    columns = pairs[:, :, 0].reshape(-1).astype(jnp.int32)
    rows = pairs[:, :, 64].reshape(-1).astype(jnp.int32)
    ranks = jnp.sum(
        ((columns[None, :] == columns[:, None]) & (rows[None, :] < rows[:, None])).astype(jnp.int32), 1
    )
    slot = jnp.arange(KMAX, dtype=jnp.int32)
    mine = (columns[None, :] == me) & (ranks[None, :] == slot[:, None])
    slot_rows = jnp.sum(jnp.where(mine, rows[None, :], 0), 1)
    code = columns * 64 + ranks * 8
    code = lax.dynamic_slice_in_dim(code, (me // M) * (M * 4), M * 4, 0)
    item = jnp.arange(8, dtype=jnp.int32)
    codes = code.reshape(M, 1, 4) + item[None, :, None]
    codes = jnp.where(item[None, :, None] < 6, codes, -1).reshape(1, M * ROWS3)

    temp_new, drift_new = call(
        ocean_kernel,
        (
            jax.ShapeDtypeStruct(thermal_state.shape, f32),
            jax.ShapeDtypeStruct(seawater_drift.shape, f32),
        ),
        in_specs=[vmem] * 5,
        out_specs=(vmem, vmem),
        cost_estimate=pl.CostEstimate(flops=10**7, bytes_accessed=6 * 10**6, transcendentals=0),
    )(thermal_state, seawater_drift, sea_site_indicator, before, after)

    motion, stress, grown, payload3 = call(
        ice_kernel,
        (
            jax.ShapeDtypeStruct(floe_motion.shape, f32),
            jax.ShapeDtypeStruct(internal_traction.shape, f32),
            jax.ShapeDtypeStruct(thickness_amount.shape, f32),
            jax.ShapeDtypeStruct((M, ROWS3, 128), bf16),
        ),
        scratch=(
            pltpu.VMEM((M, ROWS2, 128), f32),
            pltpu.VMEM((12, 50, 8, 128), f32),
            pltpu.VMEM((4, BS * BS), f32),
            pltpu.VMEM((M, ROWS3, 128), f32),
        ),
        in_specs=[vmem] * 4,
        out_specs=(vmem,) * 4,
    )(got2, nat, areal_fraction, thickness_amount)
    got3 = within(payload3)

    payload4 = call(
        functools.partial(return_kernel, count),
        jax.ShapeDtypeStruct((count, ROWS4, 128), bf16),
        scratch=(pltpu.VMEM((count * ROWS4, M * ROWS3), bf16),),
        in_specs=[vmem, vmem],
        out_specs=vmem,
    )(got3, codes)
    got4 = across(payload4)

    temp_later, drift_later = call(
        final_kernel,
        (
            jax.ShapeDtypeStruct(thermal_state.shape, f32),
            jax.ShapeDtypeStruct(seawater_drift.shape, f32),
        ),
        scratch=(pltpu.VMEM((M * ROWS4, 128), f32), pltpu.VMEM((height // 128, 3 * BS, 128), f32)),
        grid=(1,),
        in_specs=[smem, whole(got4), whole(sea_site_indicator), top, whole(drift_new)],
        out_specs=(top, whole(drift_new)),
        input_output_aliases={3: 0, 4: 1},
    )(slot_rows, got4, sea_site_indicator, temp_new, drift_new)
    return temp_later, drift_later, motion, stress, grown


def solution(mesh):
    return jax.shard_map(
        local,
        mesh=mesh,
        in_specs=(
            P("member", "gx", None),
            P("member", "gx", None),
            P("gx", None),
            P(("member", "gx")),
            P(("member", "gx"), None),
            P(("member", "gx"), None, None),
            P(("member", "gx"), None, None),
            P(("member", "gx"), None, None),
            P(("member", "gx"), None, None),
            P(("member", "gx"), None, None),
        ),
        out_specs=(
            P("member", "gx", None),
            P("member", "gx", None),
            P(("member", "gx"), None, None),
            P(("member", "gx"), None, None),
            P(("member", "gx"), None, None),
        ),
        check_vma=False,
    )
```

time: 304 us -> 108 us (0.36)
  blocking collectives: 161 us -> 0 us
  local copies, waits for them, and re-layouts: 63.5 us -> 16.7 us
  other arithmetic: 34.9 us -> 1.76 us
  Pallas kernels: 0 us -> 26.2 us
  waiting for transfers between devices: 14.5 us -> 36.2 us
  starting transfers between devices: 5.53 us -> 25.2 us
  between operations: 16.5 us -> 0.86 us
  matrix products: 7.07 us -> 0 us
    all_gather x8 -> x0, blocking collectives: 150 us -> none  [the longest x4 78.7 us: local(): stress_gathered = lax.all_gather(stress_edges, 'gx', axis=2, tiled=True)]
    all_to_all x0 -> x4, waiting for transfers between devices: none -> 36.2 us  [the longest x2 24.3 us: within(): return lax.all_to_all(x, 'gx', 0, 0, tiled=True)]
    gather x36 -> x0, local copies, waits for them, and re-layouts: 27.1 us -> none  [the longest x32 22.6 us: pick_halos(): taken = jnp.take(rim_table[:, rim_number], row_index, axis=1)]
    pallas_call x0 -> x6, Pallas kernels: none -> 26.2 us  [the longest x1 9.43 us: local(): call(ice_kernel, (jax.ShapeDtypeStruct(floe_motion.shape, f32), jax.Shape...]
    all_to_all x0 -> x4, starting transfers between devices: none -> 20.4 us  [the longest x2 11.9 us: within(): return lax.all_to_all(x, 'gx', 0, 0, tiled=True)]
    all_gather x2 -> x0, waiting for transfers between devices: 14.4 us -> none  [the longest x1 14.4 us: local(): shard_piece = lax.all_gather(flux_blocks, 'gx', axis=0, tiled=True)]
    slice x43 -> x2, local copies, waits for them, and re-layouts: 11.9 us -> 0.94 us  [local(): head = jnp.concatenate([thermal_state[:, :1], seawater_drift[:, :1]], 0)]
    unnamed x1 -> x0, blocking collectives: 10.3 us -> none
  transfers between devices with their start and end apart: 4 -> 6, of which waited for: 1 -> 4; matrix products, arithmetic and copies ran while one was open for 14% -> 5% of each run, Pallas kernels for 0% -> 21%
where the time goes in v1:
time: 108 us; the launch traced here: 107 us
  waiting for transfers between devices  36.2 us (34%)
  Pallas kernels  26.2 us (24%)
  starting transfers between devices  25.2 us (23%)
  local copies, waits for them, and re-layouts  16.7 us (15%)
  other arithmetic  1.76 us (2%)
    all_to_all x2, waiting for transfers between devices, within(): return lax.all_to_all(x, 'gx', 0, 0, tiled=True)  24.3 us
    unnamed x43, local copies, waits for them, and re-layouts  15.2 us
    all_to_all x2, starting transfers between devices, within(): return lax.all_to_all(x, 'gx', 0, 0, tiled=True)  11.9 us
    all_to_all x2, waiting for transfers between devices, across(): x = lax.all_to_all(x, 'gx', 0, 0, tiled=True)  11.9 us
    pallas_call x1, Pallas kernels, local(): call(ice_kernel, (jax.ShapeDtypeStruct(floe_motion.shape, f32), jax.Shape...  9.43 us
    all_to_all x2, starting transfers between devices, across(): x = lax.all_to_all(x, 'gx', 0, 0, tiled=True)  8.46 us
    pallas_call x1, Pallas kernels, local(): call(functools.partial(route_kernel, count), jax.ShapeDtypeStruct((count,...  8.07 us
    ppermute x1, starting transfers between devices, local(): lax.ppermute(head, 'gx', [((i + 1) % count, i) for i in range(count)])  4.33 us
  transfers between devices with their start and end apart: 6, of which 4 were waited for; matrix products, arithmetic and copies ran while one was open for 5% of the time, Pallas kernels for 21%

profile of v1, /device:TPU:0, one launch (start us, length us, event | category | flops | bytes accessed | tf_op | source)
XLA Modules:
  0.0 106.8 jit_solution(11386497219949103679)
XLA Ops:
  0.7 1.2 %copy.40.stress = f32[4,3,4096]{2,1,0:T(4,128)S(1)} copy(f32[4,3,4096]{2,0,1:T(4,128)} %param.19) | data formatting | bytes 393216 | tf_op args[8]
  1.9 1.2 %copy.38.conc = f32[4,5,4096]{2,1,0:T(8,128)S(1)} copy(f32[4,5,4096]{2,0,1:T(4,128)} %param.16) | data formatting | bytes 655360 | tf_op args[5]
  3.0 1.2 %copy.39.vol = f32[4,5,4096]{2,1,0:T(8,128)S(1)} copy(f32[4,5,4096]{2,0,1:T(4,128)} %param.17) | data formatting | bytes 655360 | tf_op args[6]
  4.3 1.0 copy-done.3
  5.3 0.9 copy-done.14
  6.2 0.9 copy-done.15
  7.1 0.8 copy-done.16
  7.9 1.8 %shard_map.146 = (bf16[16,176,128]{2,1,0:T(8,128)(2,1)S(1)}, f32[10,4,4096]{2,1,0:T(4,128)S(1)}) custom-call(s32[4]{0:T(128)S(1)} %copy-done.18, f32[8,64,1024]{2,1,0:T(8,128)S(1)} %copy-done, f32[2,64,1024]{2,1,0:T(8,128)S(1)} %copy-done.3, s32[4,4096]{1,0:T(4,128)S(1)} %copy-done.16, f32[4,5,4096]{2,1,0:T(8,128)S(1)} %copy.38.conc, ...), custom_call_target="tpu_custom_call" | custom-call | tf_op jit(solution)/shard_map/pallas_call | solution.py:453
  9.8 0.8 copy-done.7
  10.6 0.9 copy-done.8
  11.5 7.4 %all-to-all-start = ((bf16[16,176,128]{2,1,0:T(8,128)(2,1)}), bf16[16,176,128]{2,1,0:T(8,128)(2,1)S(1)}, u32[]{:S(2)}, u32[]{:S(2)}) async-start(bf16[16,176,128]{2,1,0:T(8,128)(2,1)} %copy-done.7), calls=%async_computation | async-start | bytes 1441792 | tf_op jit(solution)/shard_map/all_to_all | solution.py:427
  18.9 0.9 fusion.5
  20.3 16.6 %all-to-all-done.got.everyone = bf16[16,176,128]{2,1,0:T(8,128)(2,1)S(1)} async-done(((bf16[16,176,128]{2,1,0:T(8,128)(2,1)}), bf16[16,176,128]{2,1,0:T(8,128)(2,1)S(1)}, u32[]{:S(2)}, u32[]{:S(2)}) %all-to-all-start) | async-done | bytes 720928 | tf_op jit(solution)/shard_map/all_to_all | solution.py:427
  37.0 8.1 %shard_map.147 = bf16[16,128,128]{2,1,0:T(8,128)(2,1)S(1)} custom-call(s32[1]{0:T(128)} %bitcast.me, bf16[16,176,128]{2,1,0:T(8,128)(2,1)S(1)} %all-to-all-done.got.everyone, bf16[16,176,128]{2,1,0:T(8,128)(2,1)S(1)} %all-to-all-done.got.everyone, s32[8,768]{1,0:T(8,128)S(1)} %copy-done.17), custom_call_target="tpu_custom_call" | custom-call | tf_op jit(solution)/shard_map/pallas_call | solution.py:474
  45.1 0.8 copy-done.5
  45.8 4.8 %all-to-all-start.1 = ((bf16[16,128,128]{2,1,0:T(8,128)(2,1)}), bf16[16,128,128]{2,1,0:T(8,128)(2,1)}, u32[]{:S(2)}, u32[]{:S(2)}) async-start(bf16[16,128,128]{2,1,0:T(8,128)(2,1)} %copy-done.5), calls=%async_computation.1 | async-start | bytes 1048576 | tf_op jit(solution)/shard_map/all_to_all | solution.py:431
  51.3 4.3 %collective-permute-start.1 = (f32[10,1,1024]{2,1,0:T(1,128)}, f32[10,1,1024]{2,1,0:T(1,128)S(1)}, u32[]{:S(2)}, u32[]{:S(2)}) collective-permute-start(f32[10,1,1024]{2,1,0:T(1,128)} %pad_maximum_fusion.1), channel_id=1, source_target_pairs={{1,0},{2,1},{3,2},{4,3},{5,4},{6,5},{7,6},{8,7},{9,8},{10,9},{11,1... | collective-permute-start | bytes 122888 | tf_op jit(solution)/shard_map/ppermute | solution.py:439
  56.9 8.2 %all-to-all-done.1.got = bf16[16,128,128]{2,1,0:T(8,128)(2,1)} async-done(((bf16[16,128,128]{2,1,0:T(8,128)(2,1)}), bf16[16,128,128]{2,1,0:T(8,128)(2,1)}, u32[]{:S(2)}, u32[]{:S(2)}) %all-to-all-start.1) | async-done | bytes 524320 | tf_op jit(solution)/shard_map/all_to_all | solution.py:431
  65.1 1.0 copy-done.2
  66.2 1.1 %copy-done.9 = f32[10,4,4096]{2,1,0:T(4,128)S(1)} copy-done((f32[10,4,4096]{2,1,0:T(4,128)S(1)}, f32[10,4,4096]{2,1,0:T(4,128)}, u32[]{:S(2)}) %copy-start.9) | copy-done | bytes 655384
  67.3 9.4 %shard_map.148 = (f32[4,2,4096]{2,1,0:T(2,128)}, f32[4,3,4096]{2,1,0:T(4,128)S(1)}, f32[4,5,4096]{2,1,0:T(8,128)S(1)}, bf16[16,32,128]{2,1,0:T(8,128)(2,1)}) custom-call(bf16[16,128,128]{2,1,0:T(8,128)(2,1)} %all-to-all-done.1.got, f32[10,4,4096]{2,1,0:T(4,128)S(1)} %copy-done.9, f32[4,5,4096]{2,1,0:T(8,128)S(1)} %copy.38.conc, f32[4,5,4096]{2,1,0:T(8,128)S(1)} %copy-done.2), custom_call_target="tpu_custom_call" | custom-call | tf_op jit(solution)/shard_map/pallas_call | solution.py:514
  76.7 0.8 copy-done.10
  77.5 0.7 copy-done.12
  78.2 4.5 %all-to-all-start.2 = ((bf16[16,32,128]{2,1,0:T(8,128)(2,1)}), bf16[16,32,128]{2,1,0:T(8,128)(2,1)S(1)}, u32[]{:S(2)}, u32[]{:S(2)}) async-start(bf16[16,32,128]{2,1,0:T(8,128)(2,1)} %get-tuple-element.17), calls=%async_computation.2 | async-start | bytes 262144 | tf_op jit(solution)/shard_map/all_to_all | solution.py:427
  83.0 7.7 %all-to-all-done.2.got = bf16[16,32,128]{2,1,0:T(8,128)(2,1)S(1)} async-done(((bf16[16,32,128]{2,1,0:T(8,128)(2,1)}), bf16[16,32,128]{2,1,0:T(8,128)(2,1)S(1)}, u32[]{:S(2)}, u32[]{:S(2)}) %all-to-all-start.2) | async-done | bytes 131104 | tf_op jit(solution)/shard_map/all_to_all | solution.py:427
  90.7 1.2 %shard_map.149 = bf16[16,48,128]{2,1,0:T(8,128)(2,1)} custom-call(bf16[16,32,128]{2,1,0:T(8,128)(2,1)S(1)} %all-to-all-done.2.got, s32[1,512]{1,0:T(1,128)S(1)} %select_n.24.codes), custom_call_target="tpu_custom_call" | custom-call | tf_op jit(solution)/shard_map/pallas_call | solution.py:533
  91.9 3.7 %all-to-all-start.3 = ((bf16[16,48,128]{2,1,0:T(8,128)(2,1)}), bf16[16,48,128]{2,1,0:T(8,128)(2,1)S(1)}, u32[]{:S(2)}, u32[]{:S(2)}) async-start(bf16[16,48,128]{2,1,0:T(8,128)(2,1)} %shard_map.149), calls=%async_computation.3 | async-start | bytes 393216 | tf_op jit(solution)/shard_map/all_to_all | solution.py:431
  95.7 3.2 %shard_map.150 = (f32[8,64,1024]{2,1,0:T(8,128)}, f32[2,64,1024]{2,1,0:T(8,128)}) custom-call(f32[8,64,1024]{2,1,0:T(8,128)S(1)} %copy-done, f32[2,64,1024]{2,1,0:T(8,128)S(1)} %copy-done.4, s32[64,1024]{1,0:T(8,128)S(1)} %copy-done.6, f32[10,1,1024]{2,1,0:T(1,128)S(1)} %collective-permute-done.before, f32[10,1,1024]{2,1,0:T(1,128)S(1)} %collective-permute-done.1.after), custom_call_target="tpu_custom_call" | custom-call | flops 10000000 | bytes 6000000 | tf_op jit(solution)/shard_map/pallas_call | solution.py:503
  99.0 0.8 copy.46
  99.8 0.9 copy.47
  100.8 3.6 %all-to-all-done.3.got = bf16[16,48,128]{2,1,0:T(8,128)(2,1)S(1)} async-done(((bf16[16,48,128]{2,1,0:T(8,128)(2,1)}), bf16[16,48,128]{2,1,0:T(8,128)(2,1)S(1)}, u32[]{:S(2)}, u32[]{:S(2)}) %all-to-all-start.3) | async-done | bytes 196640 | tf_op jit(solution)/shard_map/all_to_all | solution.py:431
  104.4 2.4 %shard_map.151 = (f32[8,64,1024]{2,1,0:T(8,128)}, f32[2,64,1024]{2,1,0:T(8,128)}) custom-call(s32[8]{0:T(128)S(1)} %select_reduce_fusion.rows, bf16[16,48,128]{2,1,0:T(8,128)(2,1)S(1)} %all-to-all-done.3.got, s32[64,1024]{1,0:T(8,128)S(1)} %copy-done.6, f32[8,64,1024]{2,1,0:T(8,128)} %get-tuple-element.18.temp, ...), custom_call_target="tpu_custom_call", output_to_operand_aliasing={{0}: (3, {}), {1}: (4, {})} | custom-call | tf_op jit(solution)/shard_map/pallas_call | solution.py:542
  (49 shorter events, 3.0 us)
Async XLA Ops:
  0.6 3.6 %copy-start = (f32[8,64,1024]{2,1,0:T(8,128)S(1)}, f32[8,64,1024]{2,1,0:T(8,128)}, u32[]{:S(2)}) copy-start(f32[8,64,1024]{2,1,0:T(8,128)} %temp.3) | copy-start | bytes 6291460
  0.6 3.6 %copy-start.18 = (s32[4]{0:T(128)S(1)}, s32[4]{0:T(128)}, u32[]{:S(2)}) copy-start(s32[4]{0:T(128)} %ids.1) | copy-start | bytes 52
  4.2 1.0 copy-start.3
  5.3 0.9 copy-start.14
  6.2 0.9 copy-start.15
  7.1 0.8 copy-start.16
  7.9 1.8 %copy-start.1 = (f32[4,5,4096]{2,1,0:T(8,128)}, f32[4,5,4096]{2,1,0:T(8,128)S(1)}, u32[]{:S(2)}) copy-start(f32[4,5,4096]{2,1,0:T(8,128)S(1)} %copy.39.vol) | copy-start | bytes 983044
  7.9 29.0 %copy-start.17 = (s32[8,768]{1,0:T(8,128)S(1)}, s32[8,768]{1,0:T(8,128)}, u32[]{:S(2)}) copy-start(s32[8,768]{1,0:T(8,128)} %constant.26.clone.table) | copy-start | bytes 73732
  9.8 0.9 copy-start.7
  10.6 0.9 copy-start.8
  11.5 25.5 %all-to-all-start = ((bf16[16,176,128]{2,1,0:T(8,128)(2,1)}), bf16[16,176,128]{2,1,0:T(8,128)(2,1)S(1)}, u32[]{:S(2)}, u32[]{:S(2)}) async-start(bf16[16,176,128]{2,1,0:T(8,128)(2,1)} %copy-done.7), calls=%async_computation | async-start | bytes 1441792 | tf_op jit(solution)/shard_map/all_to_all | solution.py:427
  19.9 75.8 %collective-permute-start = (f32[10,1,1024]{2,1,0:T(1,128)S(1)}, f32[10,1,1024]{2,1,0:T(1,128)S(1)}, u32[]{:S(2)}, u32[]{:S(2)}) collective-permute-start(f32[10,1,1024]{2,1,0:T(1,128)S(1)} %pad_maximum_fusion), channel_id=1, source_target_pairs={{0,1},{1,2},{2,3},{3,4},{4,5},{5,6},{6,7},{7,8},{8,9},{9,10},{10,1... | collective-permute-start | bytes 122888 | tf_op jit(solution)/shard_map/ppermute | solution.py:438
  45.0 0.8 copy-start.5
  45.8 19.3 %all-to-all-start.1 = ((bf16[16,128,128]{2,1,0:T(8,128)(2,1)}), bf16[16,128,128]{2,1,0:T(8,128)(2,1)}, u32[]{:S(2)}, u32[]{:S(2)}) async-start(bf16[16,128,128]{2,1,0:T(8,128)(2,1)} %copy-done.5), calls=%async_computation.1 | async-start | bytes 1048576 | tf_op jit(solution)/shard_map/all_to_all | solution.py:431
  51.3 44.4 %collective-permute-start.1 = (f32[10,1,1024]{2,1,0:T(1,128)}, f32[10,1,1024]{2,1,0:T(1,128)S(1)}, u32[]{:S(2)}, u32[]{:S(2)}) collective-permute-start(f32[10,1,1024]{2,1,0:T(1,128)} %pad_maximum_fusion.1), channel_id=1, source_target_pairs={{1,0},{2,1},{3,2},{4,3},{5,4},{6,5},{7,6},{8,7},{9,8},{10,9},{11,1... | collective-permute-start | bytes 122888 | tf_op jit(solution)/shard_map/ppermute | solution.py:439
  65.1 1.0 copy-start.2
  66.2 1.1 %copy-start.9 = (f32[10,4,4096]{2,1,0:T(4,128)S(1)}, f32[10,4,4096]{2,1,0:T(4,128)}, u32[]{:S(2)}) copy-start(f32[10,4,4096]{2,1,0:T(4,128)} %copy-done.8) | copy-start | bytes 1966084
  67.3 28.4 %copy-start.4 = (f32[2,64,1024]{2,1,0:T(8,128)S(1)}, f32[2,64,1024]{2,1,0:T(8,128)}, u32[]{:S(2)}) copy-start(f32[2,64,1024]{2,1,0:T(8,128)} %drift.3) | copy-start | bytes 1572868
  67.3 28.4 %copy-start.6 = (s32[64,1024]{1,0:T(8,128)S(1)}, s32[64,1024]{1,0:T(8,128)}, u32[]{:S(2)}) copy-start(s32[64,1024]{1,0:T(8,128)} %wet.3) | copy-start | bytes 786436
  76.7 0.8 copy-start.10
  77.5 0.7 copy-start.12
  78.2 12.5 %all-to-all-start.2 = ((bf16[16,32,128]{2,1,0:T(8,128)(2,1)}), bf16[16,32,128]{2,1,0:T(8,128)(2,1)S(1)}, u32[]{:S(2)}, u32[]{:S(2)}) async-start(bf16[16,32,128]{2,1,0:T(8,128)(2,1)} %get-tuple-element.17), calls=%async_computation.2 | async-start | bytes 262144 | tf_op jit(solution)/shard_map/all_to_all | solution.py:427
  91.9 12.5 %all-to-all-start.3 = ((bf16[16,48,128]{2,1,0:T(8,128)(2,1)}), bf16[16,48,128]{2,1,0:T(8,128)(2,1)S(1)}, u32[]{:S(2)}, u32[]{:S(2)}) async-start(bf16[16,48,128]{2,1,0:T(8,128)(2,1)} %shard_map.149), calls=%async_computation.3 | async-start | bytes 393216 | tf_op jit(solution)/shard_map/all_to_all | solution.py:431
  95.6 3.4 %copy-start.13 = (f32[4,3,4096]{2,1,0:T(4,128)S(1)}, f32[4,3,4096]{2,1,0:T(4,128)}, u32[]{:S(2)}) copy-start(f32[4,3,4096]{2,1,0:T(4,128)} %copy-done.12) | copy-start | bytes 589828
  95.6 4.2 %copy-start.11 = (f32[4,5,4096]{2,1,0:T(8,128)S(1)}, f32[4,5,4096]{2,1,0:T(8,128)}, u32[]{:S(2)}) copy-start(f32[4,5,4096]{2,1,0:T(8,128)} %copy-done.10) | copy-start | bytes 983044

commit v2 on v1

--- a/solution.py
+++ b/solution.py
@@ -2,7 +2,6 @@
 
 import jax
 import jax.numpy as jnp
-import numpy as np
 from jax import lax
 from jax.experimental import pallas as pl
 from jax.experimental.pallas import tpu as pltpu
@@ -14,12 +13,12 @@
 M = 16
 W = 8
 NF = 9
-ROWS1 = 176
-ROWS2 = 128
+ROWS1 = 160
+ROWS2 = 96
 ROWS3 = 32
 ROWS4 = 48
-RIM = 48
-VMEM = 48 * 2**20
+VMEM = 60 * 2**20
+ROOM = 40 * 2**20
 f32, bf16 = jnp.float32, jnp.bfloat16
 
 
@@ -33,26 +32,26 @@
     return x if shift == 0 else pltpu.roll(x, shift, axis)
 
 
-def call(kernel, out_shape, scratch=(), in_specs=None, out_specs=None, **kw):
+def call(kernel, out_shape, scratch=(), in_specs=None, out_specs=None, vmem=VMEM, **kw):
     return pl.pallas_call(
         kernel,
         out_shape=out_shape,
         in_specs=in_specs,
         out_specs=out_specs,
         scratch_shapes=list(scratch),
-        compiler_params=pltpu.CompilerParams(vmem_limit_bytes=VMEM),
+        compiler_params=pltpu.CompilerParams(vmem_limit_bytes=vmem),
         **kw,
     )
 
 
-def pack_kernel(ids, temp, drift, cells, conc, vol, motion, stress, wind, out, nat, rows, rim):
+def pack_kernel(ids, temp, drift, cells, conc, vol, motion, stress, wind, out, nat, big):
     tiles = temp.shape[2] // BS
     step = 512
     for start in range(0, BS * BS, step):
         sl = pl.ds(start, step)
         ice = cells[:, sl].astype(f32)
-        cover = jnp.sum(conc[:, :, sl], axis=1)
-        thick = jnp.sum(vol[:, :, sl], axis=1)
+        cover = jnp.sum(conc[:, :, sl], axis=0)
+        thick = jnp.sum(vol[:, :, sl], axis=0)
         nat[0, :, sl] = thick * ice
         nat[1, :, sl] = 2.0 * thick * jnp.exp(-5.0 * (1.0 - cover))
         nat[9, :, sl] = cover
@@ -60,143 +59,155 @@
             nat[2 + k, :, sl] = wind[:, k, sl]
             nat[4 + k, :, sl] = motion[:, k, sl]
         for k in range(3):
-            nat[6 + k, :, sl] = stress[:, k, sl]
+            nat[6 + k, :, sl] = stress[k, :, sl]
     lane = lanes((4, 128))
     low, high = (lane & 63) < W, (lane & 63) >= BS - W
-    which = lax.broadcasted_iota(jnp.int32, (4, 128), 0)
-    listed = jnp.zeros((4, 128), f32)
+    lane_all = lanes((12, 128))
+    row_all = lax.broadcasted_iota(jnp.int32, (12, 128), 0)
+    listed = jnp.zeros((12, 128), f32)
     for q in range(4):
         number = ids[q]
         column, row = number // tiles, number % tiles
-        pair = jnp.where(lane < 64, column, row).astype(f32)
-        listed = jnp.where(which == q, pair, listed)
-    rim[:, 36:40, :] = jnp.broadcast_to(listed[None], (M, 4, 128))
-    rim[:, 40:48, :] = jnp.zeros((M, 8, 128), f32)
+        listed = jnp.where(lane_all == q, column.astype(f32), listed)
+        listed = jnp.where(lane_all == 4 + q, row.astype(f32), listed)
+    listed = jnp.where(row_all == 0, listed, 0.0)
+    for m in range(M):
+        big[m, 148:160, :] = listed
+        start = (5 * m - W) % BS
+        left = min(5, BS - start)
+        for part in range(8):
+            cut = slice(128 * part, 128 * part + 128)
+            at = 14 * part
+            for k in range(2):
+                big[m, at + 5 * k : at + 5 * k + left, :] = drift[k, start : start + left, cut]
+                if left < 5:
+                    big[m, at + 5 * k + left : at + 5 * k + 5, :] = drift[k, 0 : 5 - left, cut]
+            big[m, at + 10 : at + 14, :] = temp[0, 4 * m : 4 * m + 4, cut]
     for f in range(NF):
-        at = slice(4 * f, 4 * f + 4)
+        at = slice(112 + 4 * f, 116 + 4 * f)
         for k in range(4):
-            rim[k, at, :] = nat[f, :, 128 * k : 128 * k + 128]
-            rim[4 + k, at, :] = nat[f, :, 3584 + 128 * k : 3712 + 128 * k]
+            big[k, at, :] = nat[f, :, 128 * k : 128 * k + 128]
+            big[4 + k, at, :] = nat[f, :, 3584 + 128 * k : 3712 + 128 * k]
             first = jnp.zeros((4, 128), f32)
             last = jnp.zeros((4, 128), f32)
             for t in range(8):
                 v = nat[f, :, 128 * (8 * k + t) : 128 * (8 * k + t) + 128]
                 first = first + roll(jnp.where(low, v, 0.0), 8 * t)
                 last = last + roll(jnp.where(high, v, 0.0), 8 * t)
-            rim[8 + k, at, :] = first
-            rim[12 + k, at, :] = last
+            big[8 + k, at, :] = first
+            big[12 + k, at, :] = last
     for m in range(M):
-        start = (5 * m - W) % BS
-        for k in range(2):
-            left = min(5, BS - start)
-            rows[5 * k : 5 * k + left, :] = drift[k, start : start + left, :]
-            if left < 5:
-                rows[5 * k + left : 5 * k + 5, :] = drift[k, 0 : 5 - left, :]
-        rows[10:14, :] = temp[0, 4 * m : 4 * m + 4, :]
-        rows[14:16, :] = jnp.zeros((2, rows.shape[1]), f32)
-        tile = rows[...].astype(bf16)
-        for part in range(8):
-            out[m, 16 * part : 16 * part + 16, :] = tile[:, 128 * part : 128 * part + 128]
-        out[m, 128:ROWS1, :] = rim[m].astype(bf16)
-
-
-def route_kernel(count, me, got, everyone, table, out, s_sea, s_rim, row_of, acc):
+        out[m] = big[m].astype(bf16)
+
+
+def route_kernel(count, me, got, everyone, out, wide, sea, listed, numbers, collect, sem):
+    listed[...] = everyone[:, everyone.shape[1] - 16 :, :].astype(f32)[:, 4, :].astype(jnp.int32)
+    copy = pltpu.make_async_copy(listed, numbers, sem)
+    copy.start()
     me_now = me[0]
     m = lax.rem(me_now, M)
     first = me_now - m
+    for s in range(M):
+        wide[s] = got[s].astype(f32)
+        for part in range(8):
+            sea[s, part, 0:14, :] = wide[s, 14 * part : 14 * part + 14, :]
+
     east = m < 4
     west = jnp.logical_and(m >= 4, m < 8)
     north = jnp.logical_and(m >= 8, m < 12)
     shift_c = jnp.where(east, 1, jnp.where(west, -1, 0))
     shift_r = jnp.where(north, 1, jnp.where(m >= 12, -1, 0))
-    lists = got[:, 160:176, :].reshape(M * 16, 128).astype(f32)
-    number = lists[:, 0:1] * 16.0 + lists[:, 64:65]
-    aim = table[0:1, :]
-    hit = lax.broadcasted_iota(jnp.int32, (M * 16, M * RIM), 0) == aim
-    number_lane = jnp.sum(jnp.where(hit, number, 0.0), axis=0, keepdims=True).astype(jnp.int32)
-    code_one = jnp.where(aim >= 0, number_lane * 16 + table[1:2, :], -100)
-    code_four = jnp.where(aim >= 0, number_lane * 16 + table[2:3, :], -100)
+    size = count * 4
+
+    def by_row(values, owners):
+        n = owners * 4
+        spread = jnp.broadcast_to(values[:, None, :], (owners, 4, 128)).reshape(n, 128)
+        q = lax.broadcasted_iota(jnp.int32, (n, 128), 0) & 3
+        lane = lanes((n, 128))
+        column = jnp.sum(jnp.where(lane == q, spread, 0.0), axis=1, keepdims=True)
+        row = jnp.sum(jnp.where(lane == q + 4, spread, 0.0), axis=1, keepdims=True)
+        return column, row
+
+    column, row = by_row(listed[...].astype(f32), count)
+    own = wide[:, 148, :]
+    own_column, own_row = by_row(own, M)
+    own_number = own_column * 16.0 + own_row
+    eye = lax.broadcasted_iota(jnp.int32, (64, 64), 0) == lanes((64, 64))
+    number = jnp.sum(jnp.where(eye, own_number, 0.0), axis=0, keepdims=True)
+    tc = column + shift_c.astype(f32)
+    tc = jnp.where(tc < 0, tc + count, tc)
+    tc = jnp.where(tc >= count, tc - count, tc)
+    tr = row + shift_r.astype(f32)
+
+    def one_hot(r):
+        code = jnp.where((r >= 0) & (r < 16), tc * 16.0 + r, -1.0)
+        return (code == number).astype(bf16)
+
+    centre = one_hot(tr)
+    before = one_hot(jnp.where(tr >= 0, tr - 1.0, -1.0))
+    after = one_hot(jnp.where(tr < 16, tr + 1.0, 16.0))
     lane = lanes((64, 128))
-    part = lax.broadcasted_iota(jnp.int32, (64, 128), 0) >> 2
-
-    def build(o, _):
-        base = pl.multiple_of(o * 64, 64)
-        here = everyone[o, everyone.shape[1] - 16 :, :]
-        pick = lanes((64, 16)) == 4 + (lax.broadcasted_iota(jnp.int32, (64, 16), 0) & 3)
-        both = jnp.dot(pick.astype(bf16), here, preferred_element_type=f32)
-        other = roll(both, 64)
-        column = jnp.where(lane < 64, both, other).astype(jnp.int32)
-        row = jnp.where(lane < 64, other, both).astype(jnp.int32)
-        row_of[pl.ds(base, 64), :] = row
-        wide = 5 * m + jnp.where(part < 5, part, part - 5)
-        delta = jnp.where(wide < W, -1, jnp.where(wide >= BS + W, 1, 0))
-        delta = jnp.where(part >= 10, 0, delta)
-        source = column + delta
-        source = jnp.where(source < 0, source + count, source)
-        source = jnp.where(source >= count, source - count, source) - first
-        code = jnp.where((source >= 0) & (source < M) & (part < 14), source * 16 + part, -1)
-        for k in range(2):
-            s_sea[pl.ds(base, 64), 128 * k : 128 * k + 128] = (
-                (lane + 128 * k) == code
-            ).astype(bf16)
-        tc = column + shift_c
-        tc = jnp.where(tc < 0, tc + count, tc)
-        tc = jnp.where(tc >= count, tc - count, tc)
-        tr = row + shift_r
-        one = jnp.where((tr >= 0) & (tr < 16) & (part < NF), (tc * 16 + tr) * 16 + part, -1)
-        corner = (part >= NF) & (part < NF + 3)
-        before = jnp.where(corner & (tr >= 1), (tc * 16 + tr - 1) * 16 + part - NF, -1)
-        after = jnp.where(corner & (tr < 15), (tc * 16 + tr + 1) * 16 + part - NF, -1)
-        span = M * RIM
-        for k in range(span // 128):
-            cut = slice(128 * k, 128 * k + 128)
-            s_rim[pl.ds(base, 64), cut] = (code_one[:, cut] == one).astype(bf16)
-            s_rim[pl.ds(base, 64), span + 128 * k : span + 128 * k + 128] = (
-                code_four[:, cut] == before
-            ).astype(bf16)
-            s_rim[pl.ds(base, 64), 2 * span + 128 * k : 2 * span + 128 * k + 128] = (
-                code_four[:, cut] == after
-            ).astype(bf16)
+    low, high = (lane & 63) < W, (lane & 63) >= BS - W
+    for jj in range(3):
+        first_part = jnp.zeros((64, 128), f32)
+        last_part = jnp.zeros((64, 128), f32)
+        for i in range(min(4, NF - 4 * jj)):
+            f = 4 * jj + i
+            field = wide[:, 112 + 4 * f : 116 + 4 * f, :].reshape(64, 128)
+            value = jnp.dot(centre, field.astype(bf16), preferred_element_type=f32)
+            collect[:, 60 + 4 * f : 64 + 4 * f, :] = value.reshape(count, 4, 128)
+            last_part = last_part + roll(jnp.where(high, field, 0.0), 16 * i)
+            first_part = first_part + roll(jnp.where(low, field, 0.0), 16 * i)
+        value = jnp.dot(before, last_part.astype(bf16), preferred_element_type=f32)
+        value = value + jnp.dot(after, first_part.astype(bf16), preferred_element_type=f32)
+        collect[:, 48 + 4 * jj : 52 + 4 * jj, :] = value.reshape(count, 4, 128)
+
+    copy.wait()
+    lane = lanes((10, 128))
+    k = lax.broadcasted_iota(jnp.int32, (10, 128), 0)
+    wide_row = 5 * m + jnp.where(k < 5, k, k - 5)
+    beside = jnp.where(wide_row < W, 1, jnp.where(wide_row >= BS + W, 1, 0)) == 1
+    step = jnp.where(m < 8, -1, 1)
+    lane2 = lanes((1, 128))
+
+    def cut(o, _):
+        for q in range(4):
+            c, r = numbers[o, q], numbers[o, 4 + q]
+            other = c + step
+            other = jnp.where(other < 0, other + count, jnp.where(other >= count, other - count, other))
+            c, other = c - first, other - first
+            c_in = jnp.logical_and(c >= 0, c < M).astype(jnp.int32)
+            o_in = jnp.logical_and(other >= 0, other < M).astype(jnp.int32)
+            c, other = jnp.clip(c, 0, M - 1), jnp.clip(other, 0, M - 1)
+            half, odd = r >> 1, r & 1
+            near = half + 2 * odd - 1
+            near_in = jnp.logical_and(near >= 0, near < 8).astype(jnp.int32)
+            near = jnp.clip(near, 0, 7)
+            a = jnp.where(beside, sea[other, half, 0:10, :], sea[c, half, 0:10, :])
+            b = jnp.where(beside, sea[other, near, 0:10, :], sea[c, near, 0:10, :])
+            inside = jnp.where(odd == 1, (lane >= 56).astype(jnp.int32), (lane < 72).astype(jnp.int32))
+            edge = jnp.where(odd == 1, (lane < W).astype(jnp.int32), (lane >= 128 - W).astype(jnp.int32))
+            known = jnp.where(beside, o_in, c_in)
+            value = jnp.where(inside * known == 1, a, jnp.where(edge * near_in * known == 1, b, 0.0))
+            collect[o, pl.ds(q, 10, stride=4), :] = pltpu.roll(value, W + 64 * odd, 1)
+            warm = sea[c, half, 10:14, :] * c_in.astype(f32)
+            turn = pltpu.roll(warm, 64, 1)
+            straight = jnp.where(odd == 1, turn, warm)
+            crossed = jnp.where(odd == 1, warm, turn)
+            for i in range(2):
+                pair = jnp.where(lane2 < 64, straight[2 * i : 2 * i + 1], crossed[2 * i + 1 : 2 * i + 2])
+                collect[o, 40 + 4 * i + q : 41 + 4 * i + q, :] = pair
         return 0
 
-    lax.fori_loop(0, count, build, 0)
-
-    rims = got[:, 128:ROWS1, :]
-    wide_rims = rims.astype(f32)
-    lane3 = lanes(wide_rims.shape)
-    quarter = (lax.broadcasted_iota(jnp.int32, wide_rims.shape, 1) >> 2) & 3
-    halves = []
-    for mask in ((lane3 & 63) >= BS - W, (lane3 & 63) < W):
-        kept = jnp.where(mask, wide_rims, 0.0)
-        moved = kept
-        for i in range(1, 4):
-            moved = jnp.where(quarter == i, roll(kept, 16 * i), moved)
-        halves.append(moved.astype(bf16).reshape(M * RIM, 128))
-    span = M * RIM
-    total = jnp.dot(s_rim[:, :span], rims.reshape(span, 128), preferred_element_type=f32)
-    total = total + jnp.dot(s_rim[:, span : 2 * span], halves[0], preferred_element_type=f32)
-    total = total + jnp.dot(s_rim[:, 2 * span :], halves[1], preferred_element_type=f32)
-    out[:, 64:128, :] = total.astype(bf16).reshape(count, 64, 128)
-
-    for k in range(8):
-        sea = got[:, 16 * k : 16 * k + 16, :].reshape(M * 16, 128)
-        value = jnp.dot(s_sea[...], sea, preferred_element_type=f32)
-        place = 128 * k + lanes(value.shape) - row_of[...] * BS + W
-        value = jnp.where((place >= 0) & (place < BS + 2 * W), value, 0.0)
-        if k == 0:
-            acc[...] = value
-        else:
-            acc[...] += value
-    value = acc[...]
-    value = jnp.where((row_of[...] & 1) == 1, roll(value, W + 64), roll(value, W))
-    out[:, 0:64, :] = value.astype(bf16).reshape(count, 64, 128)
+    lax.fori_loop(0, count, cut, 0)
+    for o in range(count):
+        out[o] = collect[o].astype(bf16)
 
 
 def ice_kernel(got, nat, conc, vol, motion, stress, grown, out, wide, ext, temp, flux):
     for m in range(M):
         wide[m] = got[m].astype(f32)
     lane = lanes((8, 128))
-    lane4 = lanes((4, 128))
 
     def rim(m, j):
         return wide[m, 4 * j : 4 * j + 4, :]
@@ -216,17 +227,17 @@
         for r in range(16):
             t = r % 8
             v = natural(f, r)
-            north = two(rim(8 + r // 8, 16 + f), rim(10 + r // 8, 16 + f))
-            south = two(rim(12 + r // 8, 16 + f), rim(14 + r // 8, 16 + f))
+            north = two(rim(8 + r // 8, 15 + f), rim(10 + r // 8, 15 + f))
+            south = two(rim(12 + r // 8, 15 + f), rim(14 + r // 8, 15 + f))
             for p in range(2):
                 value = jnp.where(lane < 72, roll(v, 8 - 64 * p), roll(north, 72 - 64 * p - 8 * t))
                 value = jnp.where(lane < 8, roll(south, -(56 + 64 * p + 8 * t)), value)
                 ext[f, 1 + 8 + 2 * r + p] = value
         for y in range(8):
             p, i = y % 2, f % 4
-            centre = two(rim(4 + y // 2, 16 + f), rim(y // 2, 16 + f))
+            centre = two(rim(4 + y // 2, 15 + f), rim(y // 2, 15 + f))
             corner = two(
-                rim(4 + y // 2, 16 + NF + f // 4), rim(y // 2, 16 + NF + f // 4)
+                rim(4 + y // 2, 12 + f // 4), rim(y // 2, 12 + f // 4)
             )
             value = jnp.where(
                 lane < 72, roll(centre, 8 - 64 * p), roll(corner, 72 - 64 * p - 16 * i)
@@ -286,22 +297,23 @@
         return 0
 
     for _ in range(SUBCYCLES):
-        lax.fori_loop(0, 48 // step, speed, 0)
-        lax.fori_loop(0, 48 // step, strain, 0)
+        for i in range(48 // step):
+            speed(i, 0)
+        for i in range(48 // step):
+            strain(i, 0)
 
     def flat(f, r):
         a, b = ext[f, 9 + 2 * r], ext[f, 10 + 2 * r]
         return jnp.where(lane < 64, roll(a, -8), roll(b, 56))
 
     for r in range(32):
-        a, b = rim(r // 2, 10 + 2 * (r % 2)), rim(r // 2, 11 + 2 * (r % 2))
-        temp[:, 128 * r : 128 * r + 128] = jnp.where(lane4 < 64, roll(a, -8), roll(b, 56))
+        temp[:, 128 * r : 128 * r + 128] = rim(r // 2, 10 + r % 2)
     flux[:, 24:32, :] = jnp.zeros((M, 8, 128), f32)
     for r in range(16):
         for f in range(3):
             value = flat(6 + f, r)
-            stress[:, f, 128 * r : 128 * r + 128] = value[0:4]
-            stress[:, f, 128 * (r + 16) : 128 * (r + 16) + 128] = value[4:8]
+            stress[f, :, 128 * r : 128 * r + 128] = value[0:4]
+            stress[f, :, 128 * (r + 16) : 128 * (r + 16) + 128] = value[4:8]
         cover, ice = natural(9, r), natural(0, r) > 0.0
         for f in range(2):
             value = flat(4 + f, r)
@@ -312,21 +324,21 @@
             flux[r // 2, at : at + 4, :] = tau[0:4]
             flux[8 + r // 2, at : at + 4, :] = tau[4:8]
     step = 512
-    bias = 1.5 - 0.5 * lax.broadcasted_iota(jnp.int32, (conc.shape[1], step), 0).astype(f32)
-    for q in range(4):
-        for start in range(0, BS * BS, step):
-            sl = pl.ds(start, step)
-            volume = vol[q, :, sl]
-            excess = temp[q : q + 1, sl] + 1.8
-            ice = nat[0, q : q + 1, sl] > 0.0
-            rate = 0.5 * conc[q, :, sl] * (bias - excess) / (1.0 + volume)
-            later = jnp.maximum(volume + jnp.where(ice, rate, 0.0), 0.0)
-            grown[q, :, sl] = later
-            heat = jnp.sum(later - volume, axis=0, keepdims=True)
-            for k in range(step // 128):
-                r = start // 128 + k
-                at = 4 * (r % 2) + q
-                flux[r // 2, at : at + 1, :] = heat[:, 128 * k : 128 * k + 128]
+    for start in range(0, BS * BS, step):
+        sl = pl.ds(start, step)
+        excess = temp[:, sl] + 1.8
+        half = jnp.where(nat[0, :, sl] > 0.0, 0.5, 0.0)
+        heat = jnp.zeros((4, step), f32)
+        for n in range(conc.shape[0]):
+            volume = vol[n, :, sl]
+            rate = half * conc[n, :, sl] * ((1.5 - 0.5 * n) - excess) / (1.0 + volume)
+            later = jnp.maximum(volume + rate, 0.0)
+            grown[n, :, sl] = later
+            heat = heat + (later - volume)
+        for k in range(step // 128):
+            r = start // 128 + k
+            at = 4 * (r % 2)
+            flux[r // 2, at : at + 4, :] = heat[:, 128 * k : 128 * k + 128]
     for m in range(M):
         out[m] = flux[m].astype(bf16)
 
@@ -438,14 +450,16 @@
     before = lax.ppermute(tail, "gx", [(i, (i + 1) % count) for i in range(count)])
     after = lax.ppermute(head, "gx", [((i + 1) % count, i) for i in range(count)])
 
+    conc = jnp.transpose(areal_fraction, (1, 0, 2))
+    vol = jnp.transpose(thickness_amount, (1, 0, 2))
     arrays = (
         thermal_state,
         seawater_drift,
         chosen_floe_indicator,
-        areal_fraction,
-        thickness_amount,
+        conc,
+        vol,
         floe_motion,
-        internal_traction,
+        jnp.transpose(internal_traction, (1, 0, 2)),
         wind_traction,
     )
     nat_shape = jax.ShapeDtypeStruct((10, 4, BS * BS), f32)
@@ -453,41 +467,37 @@
     payload, nat = call(
         pack_kernel,
         (one_shape, nat_shape),
-        scratch=(pltpu.VMEM((16, height), f32), pltpu.VMEM((M, RIM, 128), f32)),
+        scratch=(pltpu.VMEM((M, ROWS1, 128), f32),),
         grid=(1,),
         in_specs=[smem, top] + [whole(x) for x in arrays[1:]],
         out_specs=(whole(one_shape), whole(nat_shape)),
     )(chosen_tile_numbers, *arrays)
     got1 = within(payload)
 
-    index = np.arange(M * RIM)
-    source, place = index // RIM, index % RIM
-    table = np.zeros((8, M * RIM), np.int32)
-    table[0] = np.where(place < 4 * NF, source * 16 + 4 + place % 4, -1)
-    table[1] = place // 4
-    table[2] = place // 16
     if groups == 1:
         everyone = got1
     else:
-        mine = payload[0, 160:176]
+        mine = payload[0, 144:160]
         everyone = lax.all_gather(mine, "gx", axis=0, tiled=False)
     payload2 = call(
         functools.partial(route_kernel, count),
         jax.ShapeDtypeStruct((count, ROWS2, 128), bf16),
         scratch=(
-            pltpu.VMEM((count * 64, M * 16), bf16),
-            pltpu.VMEM((count * 64, 3 * M * RIM), bf16),
-            pltpu.VMEM((count * 64, 128), jnp.int32),
-            pltpu.VMEM((count * 64, 128), f32),
-        ),
-        in_specs=[smem, vmem, vmem, vmem],
+            pltpu.VMEM((M, ROWS1, 128), f32),
+            pltpu.VMEM((M, 8, 16, 128), f32),
+            pltpu.VMEM((count, 128), jnp.int32),
+            pltpu.SMEM((count, 128), jnp.int32),
+            pltpu.VMEM((count, ROWS2, 128), f32),
+            pltpu.SemaphoreType.DMA,
+        ),
+        in_specs=[smem, vmem, vmem],
         out_specs=vmem,
-    )(me.reshape(1).astype(jnp.int32), got1, everyone, jnp.asarray(table))
+        vmem=ROOM,
+    )(me.reshape(1).astype(jnp.int32), got1, everyone)
     got2 = across(payload2)
 
-    pairs = everyone[:, everyone.shape[1] - 12 : everyone.shape[1] - 8, :].astype(f32)
-    columns = pairs[:, :, 0].reshape(-1).astype(jnp.int32)
-    rows = pairs[:, :, 64].reshape(-1).astype(jnp.int32)
+    pairs = everyone[:, everyone.shape[1] - 12, 0:8].astype(jnp.int32)
+    columns, rows = pairs[:, :4].reshape(-1), pairs[:, 4:].reshape(-1)
     ranks = jnp.sum(
         ((columns[None, :] == columns[:, None]) & (rows[None, :] < rows[:, None])).astype(jnp.int32), 1
     )
@@ -515,8 +525,8 @@
         ice_kernel,
         (
             jax.ShapeDtypeStruct(floe_motion.shape, f32),
-            jax.ShapeDtypeStruct(internal_traction.shape, f32),
-            jax.ShapeDtypeStruct(thickness_amount.shape, f32),
+            jax.ShapeDtypeStruct(arrays[6].shape, f32),
+            jax.ShapeDtypeStruct(vol.shape, f32),
             jax.ShapeDtypeStruct((M, ROWS3, 128), bf16),
         ),
         scratch=(
@@ -527,7 +537,10 @@
         ),
         in_specs=[vmem] * 4,
         out_specs=(vmem,) * 4,
-    )(got2, nat, areal_fraction, thickness_amount)
+        vmem=ROOM,
+    )(got2, nat, conc, vol)
+    stress = jnp.transpose(stress, (1, 0, 2))
+    grown = jnp.transpose(grown, (1, 0, 2))
     got3 = within(payload3)
 
     payload4 = call(
@@ -536,6 +549,7 @@
         scratch=(pltpu.VMEM((count * ROWS4, M * ROWS3), bf16),),
         in_specs=[vmem, vmem],
         out_specs=vmem,
+        vmem=ROOM,
     )(got3, codes)
     got4 = across(payload4)
 
@@ -550,6 +564,7 @@
         in_specs=[smem, whole(got4), whole(sea_site_indicator), top, whole(drift_new)],
         out_specs=(top, whole(drift_new)),
         input_output_aliases={3: 0, 4: 1},
+        vmem=ROOM,
     )(slot_rows, got4, sea_site_indicator, temp_new, drift_new)
     return temp_later, drift_later, motion, stress, grown
 

time: 108 us -> 81.4 us (0.75)
  local copies, waits for them, and re-layouts: 16.7 us -> 3.96 us
  Pallas kernels: 26.2 us -> 19.2 us
  waiting for transfers between devices: 36.2 us -> 32.3 us
  other arithmetic: 1.76 us -> 0.5 us
  starting transfers between devices: 25.2 us -> 24 us
    unnamed x43 -> x12, local copies, waits for them, and re-layouts: 15.2 us -> 1.22 us
    all_to_all x2, waiting for transfers between devices: 24.3 us -> 18.1 us  [within(): return lax.all_to_all(x, 'gx', 0, 0, tiled=True)]
    pallas_call x1, Pallas kernels: 9.43 us -> 3.83 us  [local(): call(ice_kernel, (jax.ShapeDtypeStruct(floe_motion.shape, f32), jax.Shape...]
    pallas_call x1, Pallas kernels: 8.07 us -> 3.76 us  [local(): call(functools.partial(route_kernel, count), jax.ShapeDtypeStruct((count,...]
    all_to_all x2, waiting for transfers between devices: 11.9 us -> 14.2 us  [across(): x = lax.all_to_all(x, 'gx', 0, 0, tiled=True)]
    pallas_call x1, Pallas kernels: 3.2 us -> 4.76 us  [local(): call(ocean_kernel, (jax.ShapeDtypeStruct(thermal_state.shape, f32), jax.S...]
    pallas_call x1, Pallas kernels: 1.79 us -> 3.22 us  [local(): call(pack_kernel, (one_shape, nat_shape), scratch=(pltpu.VMEM((M, ROWS1,...]
  transfers between devices with their start and end apart: 6 -> 6, of which waited for: 4 -> 4; matrix products, arithmetic and copies ran while one was open for 5% -> 4% of each run, Pallas kernels for 21% -> 17%
where the time goes in v2:
time: 81.4 us; the launch traced here: 80.8 us
  waiting for transfers between devices  32.3 us (40%)
  starting transfers between devices  24 us (29%)
  Pallas kernels  19.2 us (24%)
  local copies, waits for them, and re-layouts  3.96 us (5%)
    all_to_all x2, waiting for transfers between devices, within(): return lax.all_to_all(x, 'gx', 0, 0, tiled=True)  18.1 us
    all_to_all x2, waiting for transfers between devices, across(): x = lax.all_to_all(x, 'gx', 0, 0, tiled=True)  14.2 us
    all_to_all x2, starting transfers between devices, within(): return lax.all_to_all(x, 'gx', 0, 0, tiled=True)  11.2 us
    all_to_all x2, starting transfers between devices, across(): x = lax.all_to_all(x, 'gx', 0, 0, tiled=True)  8.31 us
    pallas_call x1, Pallas kernels, local(): call(ocean_kernel, (jax.ShapeDtypeStruct(thermal_state.shape, f32), jax.S...  4.76 us
    ppermute x1, starting transfers between devices, local(): lax.ppermute(head, 'gx', [((i + 1) % count, i) for i in range(count)])  4.09 us
    pallas_call x1, Pallas kernels, local(): call(ice_kernel, (jax.ShapeDtypeStruct(floe_motion.shape, f32), jax.Shape...  3.83 us
    pallas_call x1, Pallas kernels, local(): call(functools.partial(route_kernel, count), jax.ShapeDtypeStruct((count,...  3.76 us
  transfers between devices with their start and end apart: 6, of which 4 were waited for; matrix products, arithmetic and copies ran while one was open for 4% of the time, Pallas kernels for 17%

profile of v2, /device:TPU:0, one launch (start us, length us, event | category | flops | bytes accessed | tf_op | source)
XLA Modules:
  0.0 80.8 jit_solution(2342549835801198357)
XLA Ops:
  0.6 3.2 %shard_map.137 = (bf16[16,160,128]{2,1,0:T(8,128)(2,1)}, f32[10,4,4096]{2,1,0:T(4,128)}) custom-call(s32[4]{0:T(128)} %ids.1, f32[8,64,1024]{2,1,0:T(8,128)} %temp.3, f32[2,64,1024]{2,1,0:T(8,128)} %drift.3, s32[4,4096]{1,0:T(4,128)} %cells.1, f32[5,4,4096]{2,1,0:T(4,128)} %bitcast.7, f32[5,4,4096]{2,1,0:T(4,128)} %bitcast.9, f32[4,2,4096]{2,1,0:T(2,128)} %motion.1, ...), custom_call_target="tpu_custom_call" | custom-call | tf_op jit(solution)/shard_map/pallas_call | solution.py:467
  3.9 7.5 %all-to-all-start = ((bf16[16,160,128]{2,1,0:T(8,128)(2,1)}), bf16[16,160,128]{2,1,0:T(8,128)(2,1)S(1)}, u32[]{:S(2)}, u32[]{:S(2)}) async-start(bf16[16,160,128]{2,1,0:T(8,128)(2,1)} %get-tuple-element.15), calls=%async_computation | async-start | bytes 1310720 | tf_op jit(solution)/shard_map/all_to_all | solution.py:439
  11.4 0.9 %fusion.2 = (f32[2,1,1024]{2,1,0:T(1,128)S(1)}, f32[2,1,1024]{2,1,0:T(1,128)S(1)}) fusion(f32[2,64,1024]{2,1,0:T(8,128)} %drift.3), kind=kLoop, calls=%fused_computation.13 | loop fusion | bytes 32768 | tf_op jit(solution)/shard_map/slice | solution.py:449
  12.3 1.1 %fusion.1 = (f32[8,1,1024]{2,1,0:T(1,128)S(1)}, f32[8,1,1024]{2,1,0:T(1,128)S(1)}) fusion(f32[8,64,1024]{2,1,0:T(8,128)} %temp.3), kind=kLoop, calls=%fused_computation.12 | loop fusion | bytes 131072 | tf_op jit(solution)/shard_map/slice | solution.py:449
  13.4 0.5 collective-permute-start
  13.9 4.1 %collective-permute-start.1 = (f32[10,1,1024]{2,1,0:T(1,128)S(1)}, f32[10,1,1024]{2,1,0:T(1,128)S(1)}, u32[]{:S(2)}, u32[]{:S(2)}) collective-permute-start(f32[10,1,1024]{2,1,0:T(1,128)S(1)} %pad_maximum_fusion.1), channel_id=1, source_target_pairs={{1,0},{2,1},{3,2},{4,3},{5,4},{6,5},{7,6},{8,7},{9,8},{10,9},{11,1... | collective-permute-start | bytes 122888 | tf_op jit(solution)/shard_map/ppermute | solution.py:451
  18.0 10.4 %all-to-all-done.got.everyone = bf16[16,160,128]{2,1,0:T(8,128)(2,1)S(1)} async-done(((bf16[16,160,128]{2,1,0:T(8,128)(2,1)}), bf16[16,160,128]{2,1,0:T(8,128)(2,1)S(1)}, u32[]{:S(2)}, u32[]{:S(2)}) %all-to-all-start) | async-done | bytes 655392 | tf_op jit(solution)/shard_map/all_to_all | solution.py:439
  28.4 3.8 %shard_map.138 = bf16[16,96,128]{2,1,0:T(8,128)(2,1)} custom-call(s32[1]{0:T(128)} %bitcast.4.me, bf16[16,160,128]{2,1,0:T(8,128)(2,1)S(1)} %all-to-all-done.got.everyone, bf16[16,160,128]{2,1,0:T(8,128)(2,1)S(1)} %all-to-all-done.got.everyone), custom_call_target="tpu_custom_call" | custom-call | tf_op jit(solution)/shard_map/pallas_call | solution.py:482
  32.2 4.8 %all-to-all-start.1 = ((bf16[16,96,128]{2,1,0:T(8,128)(2,1)}), bf16[16,96,128]{2,1,0:T(8,128)(2,1)S(1)}, u32[]{:S(2)}, u32[]{:S(2)}) async-start(bf16[16,96,128]{2,1,0:T(8,128)(2,1)} %shard_map.138), calls=%async_computation.1 | async-start | bytes 786432 | tf_op jit(solution)/shard_map/all_to_all | solution.py:443
  37.0 0.1 copy.32
  37.1 0.1 copy.33
  37.2 0.1 broadcast_in_dim_reshape.2
  37.3 0.1 copy.34
  37.4 0.1 lt.24
  37.5 0.2 convert_reduce_fusion
  37.7 0.1 mul.24
  37.7 0.1 copy.35
  37.8 11.4 %all-to-all-done.1.got = bf16[16,96,128]{2,1,0:T(8,128)(2,1)S(1)} async-done(((bf16[16,96,128]{2,1,0:T(8,128)(2,1)}), bf16[16,96,128]{2,1,0:T(8,128)(2,1)S(1)}, u32[]{:S(2)}, u32[]{:S(2)}) %all-to-all-start.1) | async-done | bytes 393248 | tf_op jit(solution)/shard_map/all_to_all | solution.py:443
  49.2 3.8 %shard_map.139 = (f32[4,2,4096]{2,1,0:T(2,128)}, f32[3,4,4096]{2,1,0:T(4,128)}, f32[5,4,4096]{2,1,0:T(4,128)}, bf16[16,32,128]{2,1,0:T(8,128)(2,1)}) custom-call(bf16[16,96,128]{2,1,0:T(8,128)(2,1)S(1)} %all-to-all-done.1.got, f32[10,4,4096]{2,1,0:T(4,128)S(1)} %copy-done.3, f32[5,4,4096]{2,1,0:T(4,128)S(1)} %bitcast.8, f32[5,4,4096]{2,1,0:T(4,128)S(1)} %bitcast.10), custom_call_target="tpu_custom_call" | custom-call | tf_op jit(solution)/shard_map/pallas_call | solution.py:524
  53.0 3.7 %all-to-all-start.2 = ((bf16[16,32,128]{2,1,0:T(8,128)(2,1)}), bf16[16,32,128]{2,1,0:T(8,128)(2,1)S(1)}, u32[]{:S(2)}, u32[]{:S(2)}) async-start(bf16[16,32,128]{2,1,0:T(8,128)(2,1)} %get-tuple-element.17), calls=%async_computation.2 | async-start | bytes 262144 | tf_op jit(solution)/shard_map/all_to_all | solution.py:439
  56.7 0.1 copy.36
  56.8 0.1 add_select_fusion
  56.9 0.1 select_n.24.codes
  57.0 7.6 %all-to-all-done.2.got = bf16[16,32,128]{2,1,0:T(8,128)(2,1)S(1)} async-done(((bf16[16,32,128]{2,1,0:T(8,128)(2,1)}), bf16[16,32,128]{2,1,0:T(8,128)(2,1)S(1)}, u32[]{:S(2)}, u32[]{:S(2)}) %all-to-all-start.2) | async-done | bytes 131104 | tf_op jit(solution)/shard_map/all_to_all | solution.py:439
  64.6 1.2 %shard_map.140 = bf16[16,48,128]{2,1,0:T(8,128)(2,1)} custom-call(bf16[16,32,128]{2,1,0:T(8,128)(2,1)S(1)} %all-to-all-done.2.got, s32[1,512]{1,0:T(1,128)S(1)} %select_n.24.codes), custom_call_target="tpu_custom_call" | custom-call | tf_op jit(solution)/shard_map/pallas_call | solution.py:546
  65.9 3.5 %all-to-all-start.3 = ((bf16[16,48,128]{2,1,0:T(8,128)(2,1)}), bf16[16,48,128]{2,1,0:T(8,128)(2,1)S(1)}, u32[]{:S(2)}, u32[]{:S(2)}) async-start(bf16[16,48,128]{2,1,0:T(8,128)(2,1)} %shard_map.140), calls=%async_computation.3 | async-start | bytes 393216 | tf_op jit(solution)/shard_map/all_to_all | solution.py:443
  69.4 0.6 copy-done.4
  70.0 0.6 copy-done.5
  70.6 4.8 %shard_map.141 = (f32[8,64,1024]{2,1,0:T(8,128)}, f32[2,64,1024]{2,1,0:T(8,128)}) custom-call(f32[8,64,1024]{2,1,0:T(8,128)} %temp.3, f32[2,64,1024]{2,1,0:T(8,128)} %drift.3, s32[64,1024]{1,0:T(8,128)} %wet.3, f32[10,1,1024]{2,1,0:T(1,128)} %copy-done.4, f32[10,1,1024]{2,1,0:T(1,128)} %copy-done.5), custom_call_target="tpu_custom_call" | custom-call | flops 10000000 | bytes 6000000 | tf_op jit(solution)/shard_map/pallas_call | solution.py:513
  75.4 0.1 select_reduce_fusion.rows
  75.5 2.8 %all-to-all-done.3.got = bf16[16,48,128]{2,1,0:T(8,128)(2,1)S(1)} async-done(((bf16[16,48,128]{2,1,0:T(8,128)(2,1)}), bf16[16,48,128]{2,1,0:T(8,128)(2,1)S(1)}, u32[]{:S(2)}, u32[]{:S(2)}) %all-to-all-start.3) | async-done | bytes 196640 | tf_op jit(solution)/shard_map/all_to_all | solution.py:443
  78.4 2.4 %shard_map.142 = (f32[8,64,1024]{2,1,0:T(8,128)}, f32[2,64,1024]{2,1,0:T(8,128)}) custom-call(s32[8]{0:T(128)S(1)} %select_reduce_fusion.rows, bf16[16,48,128]{2,1,0:T(8,128)(2,1)S(1)} %all-to-all-done.3.got, s32[64,1024]{1,0:T(8,128)S(1)} %copy-done.2, f32[8,64,1024]{2,1,0:T(8,128)} %get-tuple-element.18.temp, ...), custom_call_target="tpu_custom_call", output_to_operand_aliasing={{0}: (3, {}), {1}: (4, {})} | custom-call | tf_op jit(solution)/shard_map/pallas_call | solution.py:556
  (20 shorter events, 0.1 us)
Async XLA Ops:
  3.8 45.4 %copy-start = (f32[4,5,4096]{2,0,1:T(4,128)S(1)}, f32[4,5,4096]{2,0,1:T(4,128)}, u32[]{:S(2)}) copy-start(f32[4,5,4096]{2,0,1:T(4,128)} %param.15) | copy-start | bytes 983044
  3.9 45.4 %copy-start.1 = (f32[4,5,4096]{2,0,1:T(4,128)S(1)}, f32[4,5,4096]{2,0,1:T(4,128)}, u32[]{:S(2)}) copy-start(f32[4,5,4096]{2,0,1:T(4,128)} %param.16) | copy-start | bytes 983044
  3.9 45.4 %copy-start.3 = (f32[10,4,4096]{2,1,0:T(4,128)S(1)}, f32[10,4,4096]{2,1,0:T(4,128)}, u32[]{:S(2)}) copy-start(f32[10,4,4096]{2,1,0:T(4,128)} %get-tuple-element.16.nat) | copy-start | bytes 1966084
  3.9 24.6 %all-to-all-start = ((bf16[16,160,128]{2,1,0:T(8,128)(2,1)}), bf16[16,160,128]{2,1,0:T(8,128)(2,1)S(1)}, u32[]{:S(2)}, u32[]{:S(2)}) async-start(bf16[16,160,128]{2,1,0:T(8,128)(2,1)} %get-tuple-element.15), calls=%async_computation | async-start | bytes 1310720 | tf_op jit(solution)/shard_map/all_to_all | solution.py:439
  13.4 56.0 %collective-permute-start = (f32[10,1,1024]{2,1,0:T(1,128)S(1)}, f32[10,1,1024]{2,1,0:T(1,128)S(1)}, u32[]{:S(2)}, u32[]{:S(2)}) collective-permute-start(f32[10,1,1024]{2,1,0:T(1,128)S(1)} %pad_maximum_fusion), channel_id=1, source_target_pairs={{0,1},{1,2},{2,3},{3,4},{4,5},{5,6},{6,7},{7,8},{8,9},{9,10},{10,1... | collective-permute-start | bytes 122888 | tf_op jit(solution)/shard_map/ppermute | solution.py:450
  13.9 55.5 %collective-permute-start.1 = (f32[10,1,1024]{2,1,0:T(1,128)S(1)}, f32[10,1,1024]{2,1,0:T(1,128)S(1)}, u32[]{:S(2)}, u32[]{:S(2)}) collective-permute-start(f32[10,1,1024]{2,1,0:T(1,128)S(1)} %pad_maximum_fusion.1), channel_id=1, source_target_pairs={{1,0},{2,1},{3,2},{4,3},{5,4},{6,5},{7,6},{8,7},{9,8},{10,9},{11,1... | collective-permute-start | bytes 122888 | tf_op jit(solution)/shard_map/ppermute | solution.py:451
  32.2 17.0 %all-to-all-start.1 = ((bf16[16,96,128]{2,1,0:T(8,128)(2,1)}), bf16[16,96,128]{2,1,0:T(8,128)(2,1)S(1)}, u32[]{:S(2)}, u32[]{:S(2)}) async-start(bf16[16,96,128]{2,1,0:T(8,128)(2,1)} %shard_map.138), calls=%async_computation.1 | async-start | bytes 786432 | tf_op jit(solution)/shard_map/all_to_all | solution.py:443
  53.0 25.3 %copy-start.2 = (s32[64,1024]{1,0:T(8,128)S(1)}, s32[64,1024]{1,0:T(8,128)}, u32[]{:S(2)}) copy-start(s32[64,1024]{1,0:T(8,128)} %wet.3) | copy-start | bytes 786436
  53.0 11.6 %all-to-all-start.2 = ((bf16[16,32,128]{2,1,0:T(8,128)(2,1)}), bf16[16,32,128]{2,1,0:T(8,128)(2,1)S(1)}, u32[]{:S(2)}, u32[]{:S(2)}) async-start(bf16[16,32,128]{2,1,0:T(8,128)(2,1)} %get-tuple-element.17), calls=%async_computation.2 | async-start | bytes 262144 | tf_op jit(solution)/shard_map/all_to_all | solution.py:439
  65.9 12.5 %all-to-all-start.3 = ((bf16[16,48,128]{2,1,0:T(8,128)(2,1)}), bf16[16,48,128]{2,1,0:T(8,128)(2,1)S(1)}, u32[]{:S(2)}, u32[]{:S(2)}) async-start(bf16[16,48,128]{2,1,0:T(8,128)(2,1)} %shard_map.140), calls=%async_computation.3 | async-start | bytes 393216 | tf_op jit(solution)/shard_map/all_to_all | solution.py:443
  69.4 0.6 copy-start.4
  70.0 0.6 copy-start.5

commit v3 on v2

--- a/solution.py
+++ b/solution.py
@@ -13,9 +13,9 @@
 M = 16
 W = 8
 NF = 9
-ROWS1 = 160
+ROWS1 = 152
 ROWS2 = 96
-ROWS3 = 32
+ROWS3 = 24
 ROWS4 = 48
 VMEM = 60 * 2**20
 ROOM = 40 * 2**20
@@ -62,9 +62,9 @@
             nat[6 + k, :, sl] = stress[k, :, sl]
     lane = lanes((4, 128))
     low, high = (lane & 63) < W, (lane & 63) >= BS - W
-    lane_all = lanes((12, 128))
-    row_all = lax.broadcasted_iota(jnp.int32, (12, 128), 0)
-    listed = jnp.zeros((12, 128), f32)
+    lane_all = lanes((4, 128))
+    row_all = lax.broadcasted_iota(jnp.int32, (4, 128), 0)
+    listed = jnp.zeros((4, 128), f32)
     for q in range(4):
         number = ids[q]
         column, row = number // tiles, number % tiles
@@ -72,7 +72,7 @@
         listed = jnp.where(lane_all == 4 + q, row.astype(f32), listed)
     listed = jnp.where(row_all == 0, listed, 0.0)
     for m in range(M):
-        big[m, 148:160, :] = listed
+        big[m, 148:152, :] = listed
         start = (5 * m - W) % BS
         left = min(5, BS - start)
         for part in range(8):
@@ -101,14 +101,18 @@
 
 
 def route_kernel(count, me, got, everyone, out, wide, sea, listed, numbers, collect, sem):
-    listed[...] = everyone[:, everyone.shape[1] - 16 :, :].astype(f32)[:, 4, :].astype(jnp.int32)
+    for s in range(M):
+        wide[s] = got[s].astype(f32)
+    if count == M:
+        listed[...] = wide[:, 148, :].astype(jnp.int32)
+    else:
+        listed[...] = everyone[...].astype(f32)[:, 4, :].astype(jnp.int32)
     copy = pltpu.make_async_copy(listed, numbers, sem)
     copy.start()
     me_now = me[0]
     m = lax.rem(me_now, M)
     first = me_now - m
     for s in range(M):
-        wide[s] = got[s].astype(f32)
         for part in range(8):
             sea[s, part, 0:14, :] = wide[s, 14 * part : 14 * part + 14, :]
 
@@ -199,7 +203,7 @@
                 collect[o, 40 + 4 * i + q : 41 + 4 * i + q, :] = pair
         return 0
 
-    lax.fori_loop(0, count, cut, 0)
+    lax.fori_loop(0, count, cut, 0, unroll=M)
     for o in range(count):
         out[o] = collect[o].astype(bf16)
 
@@ -223,26 +227,24 @@
     for f in range(11):
         ext[f, 0] = jnp.zeros((8, 128), f32)
         ext[f, 49] = jnp.zeros((8, 128), f32)
+    inside = (lane >= W) & (lane < W + BS)
+    for r in range(16):
+        t = r % 8
+        for p in range(2):
+            own = (lane >> 3) == 8 * p + t
+            for f in range(NF):
+                north = two(rim(8 + r // 8, 15 + f), rim(10 + r // 8, 15 + f))
+                south = two(rim(12 + r // 8, 15 + f), rim(14 + r // 8, 15 + f))
+                sides = roll(jnp.where(own, north, south), -(56 + 64 * p + 8 * t))
+                ext[f, 9 + 2 * r + p] = jnp.where(inside, roll(natural(f, r), 8 - 64 * p), sides)
     for f in range(NF):
-        for r in range(16):
-            t = r % 8
-            v = natural(f, r)
-            north = two(rim(8 + r // 8, 15 + f), rim(10 + r // 8, 15 + f))
-            south = two(rim(12 + r // 8, 15 + f), rim(14 + r // 8, 15 + f))
-            for p in range(2):
-                value = jnp.where(lane < 72, roll(v, 8 - 64 * p), roll(north, 72 - 64 * p - 8 * t))
-                value = jnp.where(lane < 8, roll(south, -(56 + 64 * p + 8 * t)), value)
-                ext[f, 1 + 8 + 2 * r + p] = value
         for y in range(8):
             p, i = y % 2, f % 4
             centre = two(rim(4 + y // 2, 15 + f), rim(y // 2, 15 + f))
-            corner = two(
-                rim(4 + y // 2, 12 + f // 4), rim(y // 2, 12 + f // 4)
+            corner = two(rim(4 + y // 2, 12 + f // 4), rim(y // 2, 12 + f // 4))
+            value = jnp.where(
+                inside, roll(centre, 8 - 64 * p), roll(corner, -(56 + 64 * p + 16 * i))
             )
-            value = jnp.where(
-                lane < 72, roll(centre, 8 - 64 * p), roll(corner, 72 - 64 * p - 16 * i)
-            )
-            value = jnp.where(lane < 8, roll(corner, -(56 + 64 * p + 16 * i)), value)
             ext[f, 1 + y] = two(value[0:4], ext[f, 33 + y, 0:4, :])
             ext[f, 41 + y] = two(ext[f, 9 + y, 4:8, :], value[4:8])
     for y in range(48):
@@ -308,7 +310,6 @@
 
     for r in range(32):
         temp[:, 128 * r : 128 * r + 128] = rim(r // 2, 10 + r % 2)
-    flux[:, 24:32, :] = jnp.zeros((M, 8, 128), f32)
     for r in range(16):
         for f in range(3):
             value = flat(6 + f, r)
@@ -343,7 +344,9 @@
         out[m] = flux[m].astype(bf16)
 
 
-def return_kernel(count, got, codes, out, pick):
+def return_kernel(count, got, codes, out, pick, wide):
+    for s in range(M):
+        wide[ROWS3 * s : ROWS3 * s + ROWS3, :] = got[s].astype(f32)
     column = lax.broadcasted_iota(jnp.int32, (ROWS4, M * ROWS3), 0)
     local_code = (column & 7) * 8 + (column >> 3)
     span = codes[0:1, :]
@@ -354,7 +357,7 @@
         return 0
 
     lax.fori_loop(0, count, build, 0)
-    value = jnp.dot(pick[...], got[...].reshape(M * ROWS3, 128), preferred_element_type=f32)
+    value = jnp.dot(pick[...], wide[...].astype(bf16), preferred_element_type=f32)
     out[...] = value.astype(bf16).reshape(count, ROWS4, 128)
 
 
@@ -382,7 +385,14 @@
             drift_out[k - levels] = mid + sea * change
 
 
-def final_kernel(rows, got, wet, temp, drift, temp_out, drift_out, wide, flux):
+def final_kernel(
+    rows, got, wet, temp, drift, temp_out, drift_out, wide, flux, held, arrive, leave
+):
+    arrivals = []
+    for k in range(3):
+        place = temp.at[0] if k == 0 else drift.at[k - 1]
+        arrivals.append(pltpu.make_async_copy(place, held.at[k], arrive.at[k]))
+        arrivals[-1].start()
     for m in range(M):
         wide[pl.ds(ROWS4 * m, ROWS4), :] = got[m].astype(f32)
     flux[...] = jnp.zeros(flux.shape, f32)
@@ -400,13 +410,18 @@
                     chosen = jnp.where(odd, turned, value) if p == 0 else jnp.where(odd, value, turned)
                     to = (at, pl.ds(BS * f + 2 * h + p, M, stride=4), slice(None))
                     flux[to] = flux[to] + jnp.where(keep, chosen, 0.0)
-    for part in range(flux.shape[0]):
-        cut = slice(128 * part, 128 * part + 128)
-        sea = wet[:, cut].astype(f32)
-        temp_out[0, :, cut] = temp[0, :, cut] + sea * flux[part, 0:BS, :]
-        for k in range(2):
-            added = sea * flux[part, BS * (k + 1) : BS * (k + 2), :]
-            drift_out[k, :, cut] = drift[k, :, cut] + added
+    copies = []
+    for k in range(3):
+        arrivals[k].wait()
+        for part in range(flux.shape[0]):
+            cut = slice(128 * part, 128 * part + 128)
+            added = wet[:, cut].astype(f32) * flux[part, BS * k : BS * (k + 1), :]
+            held[k, :, cut] = held[k, :, cut] + added
+        place = temp_out.at[0] if k == 0 else drift_out.at[k - 1]
+        copies.append(pltpu.make_async_copy(held.at[k], place, leave.at[k]))
+        copies[-1].start()
+    for copy in copies:
+        copy.wait()
 
 
 def local(
@@ -429,6 +444,7 @@
     smem = pl.BlockSpec(memory_space=pltpu.SMEM)
     vmem = pl.BlockSpec(memory_space=pltpu.VMEM)
     depth, height = thermal_state.shape[1:]
+    anywhere = pl.BlockSpec(memory_space=pl.ANY)
     top = pl.BlockSpec((1, depth, height), lambda i: (0, 0, 0))
 
     def whole(x):
@@ -477,11 +493,11 @@
     if groups == 1:
         everyone = got1
     else:
-        mine = payload[0, 144:160]
+        mine = payload[0, 144:152]
         everyone = lax.all_gather(mine, "gx", axis=0, tiled=False)
     payload2 = call(
         functools.partial(route_kernel, count),
-        jax.ShapeDtypeStruct((count, ROWS2, 128), bf16),
+        pltpu.HBM((count, ROWS2, 128), bf16),
         scratch=(
             pltpu.VMEM((M, ROWS1, 128), f32),
             pltpu.VMEM((M, 8, 16, 128), f32),
@@ -496,7 +512,7 @@
     )(me.reshape(1).astype(jnp.int32), got1, everyone)
     got2 = across(payload2)
 
-    pairs = everyone[:, everyone.shape[1] - 12, 0:8].astype(jnp.int32)
+    pairs = everyone[:, everyone.shape[1] - 4, 0:8].astype(jnp.int32)
     columns, rows = pairs[:, :4].reshape(-1), pairs[:, 4:].reshape(-1)
     ranks = jnp.sum(
         ((columns[None, :] == columns[:, None]) & (rows[None, :] < rows[:, None])).astype(jnp.int32), 1
@@ -506,9 +522,8 @@
     slot_rows = jnp.sum(jnp.where(mine, rows[None, :], 0), 1)
     code = columns * 64 + ranks * 8
     code = lax.dynamic_slice_in_dim(code, (me // M) * (M * 4), M * 4, 0)
-    item = jnp.arange(8, dtype=jnp.int32)
-    codes = code.reshape(M, 1, 4) + item[None, :, None]
-    codes = jnp.where(item[None, :, None] < 6, codes, -1).reshape(1, M * ROWS3)
+    item = jnp.arange(6, dtype=jnp.int32)
+    codes = (code.reshape(M, 1, 4) + item[None, :, None]).reshape(1, M * ROWS3)
 
     temp_new, drift_new = call(
         ocean_kernel,
@@ -527,7 +542,7 @@
             jax.ShapeDtypeStruct(floe_motion.shape, f32),
             jax.ShapeDtypeStruct(arrays[6].shape, f32),
             jax.ShapeDtypeStruct(vol.shape, f32),
-            jax.ShapeDtypeStruct((M, ROWS3, 128), bf16),
+            pltpu.HBM((M, ROWS3, 128), bf16),
         ),
         scratch=(
             pltpu.VMEM((M, ROWS2, 128), f32),
@@ -545,8 +560,11 @@
 
     payload4 = call(
         functools.partial(return_kernel, count),
-        jax.ShapeDtypeStruct((count, ROWS4, 128), bf16),
-        scratch=(pltpu.VMEM((count * ROWS4, M * ROWS3), bf16),),
+        pltpu.HBM((count, ROWS4, 128), bf16),
+        scratch=(
+            pltpu.VMEM((count * ROWS4, M * ROWS3), bf16),
+            pltpu.VMEM((M * ROWS3, 128), f32),
+        ),
         in_specs=[vmem, vmem],
         out_specs=vmem,
         vmem=ROOM,
@@ -559,10 +577,15 @@
             jax.ShapeDtypeStruct(thermal_state.shape, f32),
             jax.ShapeDtypeStruct(seawater_drift.shape, f32),
         ),
-        scratch=(pltpu.VMEM((M * ROWS4, 128), f32), pltpu.VMEM((height // 128, 3 * BS, 128), f32)),
-        grid=(1,),
-        in_specs=[smem, whole(got4), whole(sea_site_indicator), top, whole(drift_new)],
-        out_specs=(top, whole(drift_new)),
+        scratch=(
+            pltpu.VMEM((M * ROWS4, 128), f32),
+            pltpu.VMEM((height // 128, 3 * BS, 128), f32),
+            pltpu.VMEM((3, depth, height), f32),
+            pltpu.SemaphoreType.DMA((3,)),
+            pltpu.SemaphoreType.DMA((3,)),
+        ),
+        in_specs=[smem, vmem, vmem, anywhere, anywhere],
+        out_specs=(anywhere, anywhere),
         input_output_aliases={3: 0, 4: 1},
         vmem=ROOM,
     )(slot_rows, got4, sea_site_indicator, temp_new, drift_new)

time: 81.4 us -> 79.1 us (0.972)
  Pallas kernels: 19.2 us -> 18 us
  waiting for transfers between devices: 32.3 us -> 31.4 us
    pallas_call x2, Pallas kernels: 4.98 us -> 3.79 us  [the longest x1 2.63 us: local(): call(functools.partial(route_kernel, count), pltpu.HBM((count, ROWS2, 128...]
    all_to_all x2, waiting for transfers between devices: 18.1 us -> 17.2 us  [within(): return lax.all_to_all(x, 'gx', 0, 0, tiled=True)]
  transfers between devices with their start and end apart: 6 -> 6, of which waited for: 4 -> 4; matrix products, arithmetic and copies ran while one was open for 4% -> 4% of each run, Pallas kernels for 17% -> 15%
where the time goes in v3:
time: 79.1 us; the launch traced here: 78.5 us
  waiting for transfers between devices  31.4 us (40%)
  starting transfers between devices  23.9 us (30%)
  Pallas kernels  18 us (23%)
  local copies, waits for them, and re-layouts  3.96 us (5%)
    all_to_all x2, waiting for transfers between devices, within(): return lax.all_to_all(x, 'gx', 0, 0, tiled=True)  17.2 us
    all_to_all x2, waiting for transfers between devices, across(): x = lax.all_to_all(x, 'gx', 0, 0, tiled=True)  14.2 us
    all_to_all x2, starting transfers between devices, within(): return lax.all_to_all(x, 'gx', 0, 0, tiled=True)  11.2 us
    all_to_all x2, starting transfers between devices, across(): x = lax.all_to_all(x, 'gx', 0, 0, tiled=True)  8.13 us
    pallas_call x1, Pallas kernels, local(): call(ocean_kernel, (jax.ShapeDtypeStruct(thermal_state.shape, f32), jax.S...  4.76 us
    ppermute x1, starting transfers between devices, local(): lax.ppermute(head, 'gx', [((i + 1) % count, i) for i in range(count)])  4.09 us
    pallas_call x1, Pallas kernels, local(): call(ice_kernel, (jax.ShapeDtypeStruct(floe_motion.shape, f32), jax.Shape...  3.61 us
    pallas_call x1, Pallas kernels, local(): call(pack_kernel, (one_shape, nat_shape), scratch=(pltpu.VMEM((M, ROWS1,...  3.18 us
  transfers between devices with their start and end apart: 6, of which 4 were waited for; matrix products, arithmetic and copies ran while one was open for 4% of the time, Pallas kernels for 15%

profile of v3, /device:TPU:0, one launch (start us, length us, event | category | flops | bytes accessed | tf_op | source)
XLA Modules:
  0.0 78.5 jit_solution(16953557948704822213)
XLA Ops:
  0.6 3.2 %shard_map.137 = (bf16[16,152,128]{2,1,0:T(8,128)(2,1)}, f32[10,4,4096]{2,1,0:T(4,128)}) custom-call(s32[4]{0:T(128)} %ids.1, f32[8,64,1024]{2,1,0:T(8,128)} %temp.3, f32[2,64,1024]{2,1,0:T(8,128)} %drift.3, s32[4,4096]{1,0:T(4,128)} %cells.1, f32[5,4,4096]{2,1,0:T(4,128)} %bitcast.7, f32[5,4,4096]{2,1,0:T(4,128)} %bitcast.9, f32[4,2,4096]{2,1,0:T(2,128)} %motion.1, ...), custom_call_target="tpu_custom_call" | custom-call | tf_op jit(solution)/shard_map/pallas_call | solution.py:483
  3.8 0.0 copy-start.3
  3.8 7.5 %all-to-all-start = ((bf16[16,152,128]{2,1,0:T(8,128)(2,1)}), bf16[16,152,128]{2,1,0:T(8,128)(2,1)S(1)}, u32[]{:S(2)}, u32[]{:S(2)}) async-start(bf16[16,152,128]{2,1,0:T(8,128)(2,1)} %get-tuple-element.15), calls=%async_computation | async-start | bytes 1245184 | tf_op jit(solution)/shard_map/all_to_all | solution.py:455
  11.4 0.9 %fusion.2 = (f32[2,1,1024]{2,1,0:T(1,128)S(1)}, f32[2,1,1024]{2,1,0:T(1,128)S(1)}) fusion(f32[2,64,1024]{2,1,0:T(8,128)} %drift.3), kind=kLoop, calls=%fused_computation.12 | loop fusion | bytes 32768 | tf_op jit(solution)/shard_map/slice | solution.py:465
  12.3 1.1 %fusion.1 = (f32[8,1,1024]{2,1,0:T(1,128)S(1)}, f32[8,1,1024]{2,1,0:T(1,128)S(1)}) fusion(f32[8,64,1024]{2,1,0:T(8,128)} %temp.3), kind=kLoop, calls=%fused_computation.11 | loop fusion | bytes 131072 | tf_op jit(solution)/shard_map/slice | solution.py:465
  13.4 0.5 collective-permute-start
  13.9 4.1 %collective-permute-start.1 = (f32[10,1,1024]{2,1,0:T(1,128)S(1)}, f32[10,1,1024]{2,1,0:T(1,128)S(1)}, u32[]{:S(2)}, u32[]{:S(2)}) collective-permute-start(f32[10,1,1024]{2,1,0:T(1,128)S(1)} %pad_maximum_fusion.1), channel_id=1, source_target_pairs={{1,0},{2,1},{3,2},{4,3},{5,4},{6,5},{7,6},{8,7},{9,8},{10,9},{11,1... | collective-permute-start | bytes 122888 | tf_op jit(solution)/shard_map/ppermute | solution.py:467
  18.0 9.9 %all-to-all-done.got.everyone = bf16[16,152,128]{2,1,0:T(8,128)(2,1)S(1)} async-done(((bf16[16,152,128]{2,1,0:T(8,128)(2,1)}), bf16[16,152,128]{2,1,0:T(8,128)(2,1)S(1)}, u32[]{:S(2)}, u32[]{:S(2)}) %all-to-all-start) | async-done | bytes 622624 | tf_op jit(solution)/shard_map/all_to_all | solution.py:455
  27.9 0.1 copy.32
  28.0 2.6 %shard_map.138 = bf16[16,96,128]{2,1,0:T(8,128)(2,1)} custom-call(s32[1]{0:T(128)} %bitcast.4.me, bf16[16,152,128]{2,1,0:T(8,128)(2,1)S(1)} %all-to-all-done.got.everyone, bf16[16,152,128]{2,1,0:T(8,128)(2,1)S(1)} %all-to-all-done.got.everyone), custom_call_target="tpu_custom_call" | custom-call | tf_op jit(solution)/shard_map/pallas_call | solution.py:498
  30.6 4.6 %all-to-all-start.1 = ((bf16[16,96,128]{2,1,0:T(8,128)(2,1)}), bf16[16,96,128]{2,1,0:T(8,128)(2,1)S(1)}, u32[]{:S(2)}, u32[]{:S(2)}) async-start(bf16[16,96,128]{2,1,0:T(8,128)(2,1)} %shard_map.138), calls=%async_computation.1 | async-start | bytes 786432 | tf_op jit(solution)/shard_map/all_to_all | solution.py:459
  35.2 0.1 copy.33
  35.3 0.1 broadcast_in_dim_reshape.2
  35.4 0.1 copy.34
  35.5 0.1 lt.16
  35.6 0.2 convert_reduce_fusion
  35.8 0.1 mul.24
  35.9 0.1 copy.35
  36.0 0.1 copy.36
  36.0 11.4 %all-to-all-done.1.got = bf16[16,96,128]{2,1,0:T(8,128)(2,1)S(1)} async-done(((bf16[16,96,128]{2,1,0:T(8,128)(2,1)}), bf16[16,96,128]{2,1,0:T(8,128)(2,1)S(1)}, u32[]{:S(2)}, u32[]{:S(2)}) %all-to-all-start.1) | async-done | bytes 393248 | tf_op jit(solution)/shard_map/all_to_all | solution.py:459
  47.4 3.6 %shard_map.139 = (f32[4,2,4096]{2,1,0:T(2,128)}, f32[3,4,4096]{2,1,0:T(4,128)}, f32[5,4,4096]{2,1,0:T(4,128)}, bf16[16,24,128]{2,1,0:T(8,128)(2,1)}) custom-call(bf16[16,96,128]{2,1,0:T(8,128)(2,1)S(1)} %all-to-all-done.1.got, f32[10,4,4096]{2,1,0:T(4,128)S(1)} %copy-done.3, f32[5,4,4096]{2,1,0:T(4,128)S(1)} %bitcast.8, f32[5,4,4096]{2,1,0:T(4,128)S(1)} %bitcast.10), custom_call_target="tpu_custom_call" | custom-call | tf_op jit(solution)/shard_map/pallas_call | solution.py:539
  51.0 3.7 %all-to-all-start.2 = ((bf16[16,24,128]{2,1,0:T(8,128)(2,1)}), bf16[16,24,128]{2,1,0:T(8,128)(2,1)S(1)}, u32[]{:S(2)}, u32[]{:S(2)}) async-start(bf16[16,24,128]{2,1,0:T(8,128)(2,1)} %get-tuple-element.17), calls=%async_computation.2 | async-start | bytes 196608 | tf_op jit(solution)/shard_map/all_to_all | solution.py:455
  54.7 0.1 add.34.codes
  54.8 7.3 %all-to-all-done.2.got = bf16[16,24,128]{2,1,0:T(8,128)(2,1)S(1)} async-done(((bf16[16,24,128]{2,1,0:T(8,128)(2,1)}), bf16[16,24,128]{2,1,0:T(8,128)(2,1)S(1)}, u32[]{:S(2)}, u32[]{:S(2)}) %all-to-all-start.2) | async-done | bytes 98336 | tf_op jit(solution)/shard_map/all_to_all | solution.py:455
  62.1 1.2 %shard_map.140 = bf16[16,48,128]{2,1,0:T(8,128)(2,1)} custom-call(bf16[16,24,128]{2,1,0:T(8,128)(2,1)S(1)} %all-to-all-done.2.got, s32[1,384]{1,0:T(1,128)S(1)} %add.34.codes), custom_call_target="tpu_custom_call" | custom-call | tf_op jit(solution)/shard_map/pallas_call | solution.py:561
  63.3 3.5 %all-to-all-start.3 = ((bf16[16,48,128]{2,1,0:T(8,128)(2,1)}), bf16[16,48,128]{2,1,0:T(8,128)(2,1)S(1)}, u32[]{:S(2)}, u32[]{:S(2)}) async-start(bf16[16,48,128]{2,1,0:T(8,128)(2,1)} %shard_map.140), calls=%async_computation.3 | async-start | bytes 393216 | tf_op jit(solution)/shard_map/all_to_all | solution.py:459
  66.8 0.6 copy-done.4
  67.4 0.6 copy-done.5
  68.0 4.8 %shard_map.141 = (f32[8,64,1024]{2,1,0:T(8,128)}, f32[2,64,1024]{2,1,0:T(8,128)}) custom-call(f32[8,64,1024]{2,1,0:T(8,128)} %temp.3, f32[2,64,1024]{2,1,0:T(8,128)} %drift.3, s32[64,1024]{1,0:T(8,128)} %wet.3, f32[10,1,1024]{2,1,0:T(1,128)} %copy-done.4, f32[10,1,1024]{2,1,0:T(1,128)} %copy-done.5), custom_call_target="tpu_custom_call" | custom-call | flops 10000000 | bytes 6000000 | tf_op jit(solution)/shard_map/pallas_call | solution.py:528
  72.8 0.1 select_reduce_fusion.rows
  72.9 2.8 %all-to-all-done.3.got = bf16[16,48,128]{2,1,0:T(8,128)(2,1)S(1)} async-done(((bf16[16,48,128]{2,1,0:T(8,128)(2,1)}), bf16[16,48,128]{2,1,0:T(8,128)(2,1)S(1)}, u32[]{:S(2)}, u32[]{:S(2)}) %all-to-all-start.3) | async-done | bytes 196640 | tf_op jit(solution)/shard_map/all_to_all | solution.py:459
  75.8 2.7 %shard_map.142 = (f32[8,64,1024]{2,1,0:T(8,128)}, f32[2,64,1024]{2,1,0:T(8,128)}) custom-call(s32[8]{0:T(128)S(1)} %select_reduce_fusion.rows, bf16[16,48,128]{2,1,0:T(8,128)(2,1)S(1)} %all-to-all-done.3.got, s32[64,1024]{1,0:T(8,128)S(1)} %copy-done.2, f32[8,64,1024]{2,1,0:T(8,128)} %get-tuple-element.18.temp, ...), custom_call_target="tpu_custom_call", output_to_operand_aliasing={{0}: (3, {}), {1}: (4, {})} | custom-call | tf_op jit(solution)/shard_map/pallas_call | solution.py:574
  (19 shorter events, 0.1 us)
Async XLA Ops:
  3.8 43.6 %copy-start = (f32[4,5,4096]{2,0,1:T(4,128)S(1)}, f32[4,5,4096]{2,0,1:T(4,128)}, u32[]{:S(2)}) copy-start(f32[4,5,4096]{2,0,1:T(4,128)} %param.15) | copy-start | bytes 983044
  3.8 43.6 %copy-start.1 = (f32[4,5,4096]{2,0,1:T(4,128)S(1)}, f32[4,5,4096]{2,0,1:T(4,128)}, u32[]{:S(2)}) copy-start(f32[4,5,4096]{2,0,1:T(4,128)} %param.16) | copy-start | bytes 983044
  3.8 43.6 %copy-start.3 = (f32[10,4,4096]{2,1,0:T(4,128)S(1)}, f32[10,4,4096]{2,1,0:T(4,128)}, u32[]{:S(2)}) copy-start(f32[10,4,4096]{2,1,0:T(4,128)} %get-tuple-element.16.nat) | copy-start | bytes 1966084
  3.8 24.1 %all-to-all-start = ((bf16[16,152,128]{2,1,0:T(8,128)(2,1)}), bf16[16,152,128]{2,1,0:T(8,128)(2,1)S(1)}, u32[]{:S(2)}, u32[]{:S(2)}) async-start(bf16[16,152,128]{2,1,0:T(8,128)(2,1)} %get-tuple-element.15), calls=%async_computation | async-start | bytes 1245184 | tf_op jit(solution)/shard_map/all_to_all | solution.py:455
  13.4 53.4 %collective-permute-start = (f32[10,1,1024]{2,1,0:T(1,128)S(1)}, f32[10,1,1024]{2,1,0:T(1,128)S(1)}, u32[]{:S(2)}, u32[]{:S(2)}) collective-permute-start(f32[10,1,1024]{2,1,0:T(1,128)S(1)} %pad_maximum_fusion), channel_id=1, source_target_pairs={{0,1},{1,2},{2,3},{3,4},{4,5},{5,6},{6,7},{7,8},{8,9},{9,10},{10,1... | collective-permute-start | bytes 122888 | tf_op jit(solution)/shard_map/ppermute | solution.py:466
  13.9 52.9 %collective-permute-start.1 = (f32[10,1,1024]{2,1,0:T(1,128)S(1)}, f32[10,1,1024]{2,1,0:T(1,128)S(1)}, u32[]{:S(2)}, u32[]{:S(2)}) collective-permute-start(f32[10,1,1024]{2,1,0:T(1,128)S(1)} %pad_maximum_fusion.1), channel_id=1, source_target_pairs={{1,0},{2,1},{3,2},{4,3},{5,4},{6,5},{7,6},{8,7},{9,8},{10,9},{11,1... | collective-permute-start | bytes 122888 | tf_op jit(solution)/shard_map/ppermute | solution.py:467
  30.6 16.8 %all-to-all-start.1 = ((bf16[16,96,128]{2,1,0:T(8,128)(2,1)}), bf16[16,96,128]{2,1,0:T(8,128)(2,1)S(1)}, u32[]{:S(2)}, u32[]{:S(2)}) async-start(bf16[16,96,128]{2,1,0:T(8,128)(2,1)} %shard_map.138), calls=%async_computation.1 | async-start | bytes 786432 | tf_op jit(solution)/shard_map/all_to_all | solution.py:459
  51.0 24.7 %copy-start.2 = (s32[64,1024]{1,0:T(8,128)S(1)}, s32[64,1024]{1,0:T(8,128)}, u32[]{:S(2)}) copy-start(s32[64,1024]{1,0:T(8,128)} %wet.3) | copy-start | bytes 786436
  51.0 11.1 %all-to-all-start.2 = ((bf16[16,24,128]{2,1,0:T(8,128)(2,1)}), bf16[16,24,128]{2,1,0:T(8,128)(2,1)S(1)}, u32[]{:S(2)}, u32[]{:S(2)}) async-start(bf16[16,24,128]{2,1,0:T(8,128)(2,1)} %get-tuple-element.17), calls=%async_computation.2 | async-start | bytes 196608 | tf_op jit(solution)/shard_map/all_to_all | solution.py:455
  63.3 12.5 %all-to-all-start.3 = ((bf16[16,48,128]{2,1,0:T(8,128)(2,1)}), bf16[16,48,128]{2,1,0:T(8,128)(2,1)S(1)}, u32[]{:S(2)}, u32[]{:S(2)}) async-start(bf16[16,48,128]{2,1,0:T(8,128)(2,1)} %shard_map.140), calls=%async_computation.3 | async-start | bytes 393216 | tf_op jit(solution)/shard_map/all_to_all | solution.py:459
  66.8 0.6 copy-start.4
  67.4 0.6 copy-start.5

commit v4 on v3

--- a/solution.py
+++ b/solution.py
@@ -13,10 +13,11 @@
 M = 16
 W = 8
 NF = 9
-ROWS1 = 152
-ROWS2 = 96
+ROWS1 = 136
+ROWS2 = 88
 ROWS3 = 24
 ROWS4 = 48
+SEA = 12
 VMEM = 60 * 2**20
 ROOM = 40 * 2**20
 f32, bf16 = jnp.float32, jnp.bfloat16
@@ -42,6 +43,12 @@
         compiler_params=pltpu.CompilerParams(vmem_limit_bytes=vmem),
         **kw,
     )
+
+
+def sea_rows(m):
+    if m >= 8:
+        return [(24 + 4 * (m - 8), 4)]
+    return [(2 * m if m < 4 else 48 + 2 * m, 2), (8 + 2 * m, 2)]
 
 
 def pack_kernel(ids, temp, drift, cells, conc, vol, motion, stress, wind, out, nat, big):
@@ -72,19 +79,18 @@
         listed = jnp.where(lane_all == 4 + q, row.astype(f32), listed)
     listed = jnp.where(row_all == 0, listed, 0.0)
     for m in range(M):
-        big[m, 148:152, :] = listed
-        start = (5 * m - W) % BS
-        left = min(5, BS - start)
+        big[m, 132:136, :] = listed
         for part in range(8):
             cut = slice(128 * part, 128 * part + 128)
-            at = 14 * part
+            at = SEA * part
             for k in range(2):
-                big[m, at + 5 * k : at + 5 * k + left, :] = drift[k, start : start + left, cut]
-                if left < 5:
-                    big[m, at + 5 * k + left : at + 5 * k + 5, :] = drift[k, 0 : 5 - left, cut]
-            big[m, at + 10 : at + 14, :] = temp[0, 4 * m : 4 * m + 4, cut]
+                place = at + 4 * k
+                for start, size in sea_rows(m):
+                    big[m, place : place + size, :] = drift[k, start : start + size, cut]
+                    place += size
+            big[m, at + 8 : at + 12, :] = temp[0, 4 * m : 4 * m + 4, cut]
     for f in range(NF):
-        at = slice(112 + 4 * f, 116 + 4 * f)
+        at = slice(96 + 4 * f, 100 + 4 * f)
         for k in range(4):
             big[k, at, :] = nat[f, :, 128 * k : 128 * k + 128]
             big[4 + k, at, :] = nat[f, :, 3584 + 128 * k : 3712 + 128 * k]
@@ -100,11 +106,11 @@
         out[m] = big[m].astype(bf16)
 
 
-def route_kernel(count, me, got, everyone, out, wide, sea, listed, numbers, collect, sem):
+def route_kernel(count, me, got, everyone, out, wide, sea, listed, numbers, collect, field, sem):
     for s in range(M):
         wide[s] = got[s].astype(f32)
     if count == M:
-        listed[...] = wide[:, 148, :].astype(jnp.int32)
+        listed[...] = wide[:, 132, :].astype(jnp.int32)
     else:
         listed[...] = everyone[...].astype(f32)[:, 4, :].astype(jnp.int32)
     copy = pltpu.make_async_copy(listed, numbers, sem)
@@ -114,7 +120,7 @@
     first = me_now - m
     for s in range(M):
         for part in range(8):
-            sea[s, part, 0:14, :] = wide[s, 14 * part : 14 * part + 14, :]
+            sea[s, part, 0:SEA, :] = wide[s, SEA * part : SEA * part + SEA, :]
 
     east = m < 4
     west = jnp.logical_and(m >= 4, m < 8)
@@ -122,22 +128,14 @@
     shift_c = jnp.where(east, 1, jnp.where(west, -1, 0))
     shift_r = jnp.where(north, 1, jnp.where(m >= 12, -1, 0))
     size = count * 4
-
-    def by_row(values, owners):
-        n = owners * 4
-        spread = jnp.broadcast_to(values[:, None, :], (owners, 4, 128)).reshape(n, 128)
-        q = lax.broadcasted_iota(jnp.int32, (n, 128), 0) & 3
-        lane = lanes((n, 128))
-        column = jnp.sum(jnp.where(lane == q, spread, 0.0), axis=1, keepdims=True)
-        row = jnp.sum(jnp.where(lane == q + 4, spread, 0.0), axis=1, keepdims=True)
-        return column, row
-
-    column, row = by_row(listed[...].astype(f32), count)
-    own = wide[:, 148, :]
-    own_column, own_row = by_row(own, M)
-    own_number = own_column * 16.0 + own_row
-    eye = lax.broadcasted_iota(jnp.int32, (64, 64), 0) == lanes((64, 64))
-    number = jnp.sum(jnp.where(eye, own_number, 0.0), axis=0, keepdims=True)
+    spread = jnp.broadcast_to(listed[...].astype(f32)[:, None, :], (count, 4, 128))
+    spread = spread.reshape(size, 128)
+    q_of = lax.broadcasted_iota(jnp.int32, (size, 128), 0) & 3
+    lane_of = lanes((size, 128))
+    column = jnp.sum(jnp.where(lane_of == q_of, spread, 0.0), axis=1, keepdims=True)
+    row = jnp.sum(jnp.where(lane_of == q_of + 4, spread, 0.0), axis=1, keepdims=True)
+    eye = lax.broadcasted_iota(jnp.int32, (size, size), 0) == lanes((size, size))
+    number = jnp.sum(jnp.where(eye, column * 16.0 + row, 0.0), axis=0, keepdims=True)
     tc = column + shift_c.astype(f32)
     tc = jnp.where(tc < 0, tc + count, tc)
     tc = jnp.where(tc >= count, tc - count, tc)
@@ -150,60 +148,62 @@
     centre = one_hot(tr)
     before = one_hot(jnp.where(tr >= 0, tr - 1.0, -1.0))
     after = one_hot(jnp.where(tr < 16, tr + 1.0, 16.0))
-    lane = lanes((64, 128))
-    low, high = (lane & 63) < W, (lane & 63) >= BS - W
-    for jj in range(3):
-        first_part = jnp.zeros((64, 128), f32)
-        last_part = jnp.zeros((64, 128), f32)
-        for i in range(min(4, NF - 4 * jj)):
-            f = 4 * jj + i
-            field = wide[:, 112 + 4 * f : 116 + 4 * f, :].reshape(64, 128)
-            value = jnp.dot(centre, field.astype(bf16), preferred_element_type=f32)
-            collect[:, 60 + 4 * f : 64 + 4 * f, :] = value.reshape(count, 4, 128)
-            last_part = last_part + roll(jnp.where(high, field, 0.0), 16 * i)
-            first_part = first_part + roll(jnp.where(low, field, 0.0), 16 * i)
-        value = jnp.dot(before, last_part.astype(bf16), preferred_element_type=f32)
-        value = value + jnp.dot(after, first_part.astype(bf16), preferred_element_type=f32)
-        collect[:, 48 + 4 * jj : 52 + 4 * jj, :] = value.reshape(count, 4, 128)
 
     copy.wait()
-    lane = lanes((10, 128))
-    k = lax.broadcasted_iota(jnp.int32, (10, 128), 0)
-    wide_row = 5 * m + jnp.where(k < 5, k, k - 5)
-    beside = jnp.where(wide_row < W, 1, jnp.where(wide_row >= BS + W, 1, 0)) == 1
-    step = jnp.where(m < 8, -1, 1)
+    lane = lanes((8, 128))
     lane2 = lanes((1, 128))
 
     def cut(o, _):
         for q in range(4):
-            c, r = numbers[o, q], numbers[o, 4 + q]
-            other = c + step
-            other = jnp.where(other < 0, other + count, jnp.where(other >= count, other - count, other))
-            c, other = c - first, other - first
-            c_in = jnp.logical_and(c >= 0, c < M).astype(jnp.int32)
-            o_in = jnp.logical_and(other >= 0, other < M).astype(jnp.int32)
-            c, other = jnp.clip(c, 0, M - 1), jnp.clip(other, 0, M - 1)
+            c, r = numbers[o, q] - first, numbers[o, 4 + q]
+            known = jnp.logical_and(c >= 0, c < M).astype(jnp.int32)
+            c = jnp.clip(c, 0, M - 1)
             half, odd = r >> 1, r & 1
             near = half + 2 * odd - 1
             near_in = jnp.logical_and(near >= 0, near < 8).astype(jnp.int32)
             near = jnp.clip(near, 0, 7)
-            a = jnp.where(beside, sea[other, half, 0:10, :], sea[c, half, 0:10, :])
-            b = jnp.where(beside, sea[other, near, 0:10, :], sea[c, near, 0:10, :])
+            a, b = sea[c, half, 0:8, :], sea[c, near, 0:8, :]
             inside = jnp.where(odd == 1, (lane >= 56).astype(jnp.int32), (lane < 72).astype(jnp.int32))
             edge = jnp.where(odd == 1, (lane < W).astype(jnp.int32), (lane >= 128 - W).astype(jnp.int32))
-            known = jnp.where(beside, o_in, c_in)
             value = jnp.where(inside * known == 1, a, jnp.where(edge * near_in * known == 1, b, 0.0))
-            collect[o, pl.ds(q, 10, stride=4), :] = pltpu.roll(value, W + 64 * odd, 1)
-            warm = sea[c, half, 10:14, :] * c_in.astype(f32)
+            collect[o, pl.ds(q, 8, stride=4), :] = pltpu.roll(value, W + 64 * odd, 1)
+            warm = sea[c, half, 8:12, :] * known.astype(f32)
             turn = pltpu.roll(warm, 64, 1)
             straight = jnp.where(odd == 1, turn, warm)
             crossed = jnp.where(odd == 1, warm, turn)
             for i in range(2):
                 pair = jnp.where(lane2 < 64, straight[2 * i : 2 * i + 1], crossed[2 * i + 1 : 2 * i + 2])
-                collect[o, 40 + 4 * i + q : 41 + 4 * i + q, :] = pair
+                collect[o, 32 + 4 * i + q : 33 + 4 * i + q, :] = pair
         return 0
 
     lax.fori_loop(0, count, cut, 0, unroll=M)
+
+    lane = lanes((size, 128))
+    low, high = (lane & 63) < W, (lane & 63) >= BS - W
+    rim = (m < 8).astype(f32)
+    for jj in range(3):
+        first_part = jnp.zeros((size, 128), f32)
+        last_part = jnp.zeros((size, 128), f32)
+        for i in range(min(4, NF - 4 * jj)):
+            f = 4 * jj + i
+            own = wide[:, 96 + 4 * f : 100 + 4 * f, :]
+            if count > M:
+                field[...] = jnp.zeros(field.shape, f32)
+                field[pl.ds(first, M)] = own
+                own = field[...]
+            own = own.reshape(size, 128)
+            if f in (2, 3):
+                at = 16 * (f - 2)
+                one = roll(collect[:, at : at + 4, :], -W).reshape(size, 128)
+                two = roll(collect[:, at + 4 : at + 8, :], 64 - W).reshape(size, 128)
+                own = own + rim * jnp.where(lane < 64, one, two)
+            value = jnp.dot(centre, own.astype(bf16), preferred_element_type=f32)
+            collect[:, 52 + 4 * f : 56 + 4 * f, :] = value.reshape(count, 4, 128)
+            last_part = last_part + roll(jnp.where(high, own, 0.0), 16 * i)
+            first_part = first_part + roll(jnp.where(low, own, 0.0), 16 * i)
+        value = jnp.dot(before, last_part.astype(bf16), preferred_element_type=f32)
+        value = value + jnp.dot(after, first_part.astype(bf16), preferred_element_type=f32)
+        collect[:, 40 + 4 * jj : 44 + 4 * jj, :] = value.reshape(count, 4, 128)
     for o in range(count):
         out[o] = collect[o].astype(bf16)
 
@@ -233,24 +233,31 @@
         for p in range(2):
             own = (lane >> 3) == 8 * p + t
             for f in range(NF):
-                north = two(rim(8 + r // 8, 15 + f), rim(10 + r // 8, 15 + f))
-                south = two(rim(12 + r // 8, 15 + f), rim(14 + r // 8, 15 + f))
+                north = two(rim(8 + r // 8, 13 + f), rim(10 + r // 8, 13 + f))
+                south = two(rim(12 + r // 8, 13 + f), rim(14 + r // 8, 13 + f))
                 sides = roll(jnp.where(own, north, south), -(56 + 64 * p + 8 * t))
                 ext[f, 9 + 2 * r + p] = jnp.where(inside, roll(natural(f, r), 8 - 64 * p), sides)
     for f in range(NF):
         for y in range(8):
             p, i = y % 2, f % 4
-            centre = two(rim(4 + y // 2, 15 + f), rim(y // 2, 15 + f))
-            corner = two(rim(4 + y // 2, 12 + f // 4), rim(y // 2, 12 + f // 4))
+            centre = two(rim(4 + y // 2, 13 + f), rim(y // 2, 13 + f))
+            corner = two(rim(4 + y // 2, 10 + f // 4), rim(y // 2, 10 + f // 4))
             value = jnp.where(
                 inside, roll(centre, 8 - 64 * p), roll(corner, -(56 + 64 * p + 16 * i))
             )
             ext[f, 1 + y] = two(value[0:4], ext[f, 33 + y, 0:4, :])
             ext[f, 41 + y] = two(ext[f, 9 + y, 4:8, :], value[4:8])
+    where = {}
+    for m in range(M):
+        listed = [start + i for start, size in sea_rows(m) for i in range(size)]
+        for k, row in enumerate(listed):
+            where[row + W] = (m, k)
+    blank = jnp.zeros((4, 128), f32)
     for y in range(48):
         for k in range(2):
-            a, b = y, y + 32
-            value = two(rim(a // 5, 5 * k + a % 5), rim(b // 5, 5 * k + b % 5))
+            halves = [where.get(x) for x in (y, y + 32)]
+            halves = [blank if at is None else rim(at[0], 4 * k + at[1]) for at in halves]
+            value = two(*halves)
             ext[9 + k, 1 + y] = value
             ext[2 + k, 1 + y] = ext[2 + k, 1 + y] + value
     thick = ext[0, 1:49]
@@ -309,7 +316,7 @@
         return jnp.where(lane < 64, roll(a, -8), roll(b, 56))
 
     for r in range(32):
-        temp[:, 128 * r : 128 * r + 128] = rim(r // 2, 10 + r % 2)
+        temp[:, 128 * r : 128 * r + 128] = rim(r // 2, 8 + r % 2)
     for r in range(16):
         for f in range(3):
             value = flat(6 + f, r)
@@ -361,7 +368,7 @@
     out[...] = value.astype(bf16).reshape(count, ROWS4, 128)
 
 
-def ocean_kernel(temp, drift, wet, before, after, temp_out, drift_out):
+def ocean_kernel(temp, drift, wet, before, after, _, temp_out, drift_out):
     levels = temp.shape[0]
     shape = temp.shape[1:]
     lane = lanes(shape)
@@ -395,27 +402,23 @@
         arrivals[-1].start()
     for m in range(M):
         wide[pl.ds(ROWS4 * m, ROWS4), :] = got[m].astype(f32)
-    flux[...] = jnp.zeros(flux.shape, f32)
-    upper = lanes((M, 128)) >= 64
+    flux[0:16] = jnp.zeros((16,) + flux.shape[1:], f32)
     for slot in range(KMAX):
         r = rows[slot]
-        at = r // 2
-        odd = lax.rem(r, 2) == 1
-        keep = upper == odd
         for f in range(3):
             for h in range(2):
                 value = wide[pl.ds(8 * (2 * f + h) + slot, M, stride=ROWS4), :]
-                turned = roll(value, 64)
-                for p in range(2):
-                    chosen = jnp.where(odd, turned, value) if p == 0 else jnp.where(odd, value, turned)
-                    to = (at, pl.ds(BS * f + 2 * h + p, M, stride=4), slice(None))
-                    flux[to] = flux[to] + jnp.where(keep, chosen, 0.0)
+                flux[r, pl.ds(BS * f + 2 * h, M, stride=4), :] = value
+                flux[r, pl.ds(BS * f + 2 * h + 1, M, stride=4), :] = roll(value, 64)
+    left = lanes((BS, 128)) < 64
     copies = []
     for k in range(3):
         arrivals[k].wait()
-        for part in range(flux.shape[0]):
+        for part in range(8):
             cut = slice(128 * part, 128 * part + 128)
-            added = wet[:, cut].astype(f32) * flux[part, BS * k : BS * (k + 1), :]
+            rows_of = slice(BS * k, BS * (k + 1))
+            pair = jnp.where(left, flux[2 * part, rows_of, :], roll(flux[2 * part + 1, rows_of, :], 64))
+            added = wet[:, cut].astype(f32) * pair
             held[k, :, cut] = held[k, :, cut] + added
         place = temp_out.at[0] if k == 0 else drift_out.at[k - 1]
         copies.append(pltpu.make_async_copy(held.at[k], place, leave.at[k]))
@@ -493,7 +496,7 @@
     if groups == 1:
         everyone = got1
     else:
-        mine = payload[0, 144:152]
+        mine = payload[0, 128:136]
         everyone = lax.all_gather(mine, "gx", axis=0, tiled=False)
     payload2 = call(
         functools.partial(route_kernel, count),
@@ -504,6 +507,7 @@
             pltpu.VMEM((count, 128), jnp.int32),
             pltpu.SMEM((count, 128), jnp.int32),
             pltpu.VMEM((count, ROWS2, 128), f32),
+            pltpu.VMEM((count, 4, 128), f32),
             pltpu.SemaphoreType.DMA,
         ),
         in_specs=[smem, vmem, vmem],
@@ -519,22 +523,11 @@
     )
     slot = jnp.arange(KMAX, dtype=jnp.int32)
     mine = (columns[None, :] == me) & (ranks[None, :] == slot[:, None])
-    slot_rows = jnp.sum(jnp.where(mine, rows[None, :], 0), 1)
+    slot_rows = 16 + jnp.sum(jnp.where(mine, rows[None, :] - 16, 0), 1)
     code = columns * 64 + ranks * 8
     code = lax.dynamic_slice_in_dim(code, (me // M) * (M * 4), M * 4, 0)
     item = jnp.arange(6, dtype=jnp.int32)
     codes = (code.reshape(M, 1, 4) + item[None, :, None]).reshape(1, M * ROWS3)
-
-    temp_new, drift_new = call(
-        ocean_kernel,
-        (
-            jax.ShapeDtypeStruct(thermal_state.shape, f32),
-            jax.ShapeDtypeStruct(seawater_drift.shape, f32),
-        ),
-        in_specs=[vmem] * 5,
-        out_specs=(vmem, vmem),
-        cost_estimate=pl.CostEstimate(flops=10**7, bytes_accessed=6 * 10**6, transcendentals=0),
-    )(thermal_state, seawater_drift, sea_site_indicator, before, after)
 
     motion, stress, grown, payload3 = call(
         ice_kernel,
@@ -556,6 +549,17 @@
     )(got2, nat, conc, vol)
     stress = jnp.transpose(stress, (1, 0, 2))
     grown = jnp.transpose(grown, (1, 0, 2))
+    temp_new, drift_new = call(
+        ocean_kernel,
+        (
+            jax.ShapeDtypeStruct(thermal_state.shape, f32),
+            jax.ShapeDtypeStruct(seawater_drift.shape, f32),
+        ),
+        in_specs=[vmem] * 5 + [anywhere],
+        out_specs=(vmem, vmem),
+        cost_estimate=pl.CostEstimate(flops=10**7, bytes_accessed=6 * 10**6, transcendentals=0),
+    )(thermal_state, seawater_drift, sea_site_indicator, before, after, payload3)
+
     got3 = within(payload3)
 
     payload4 = call(
@@ -579,7 +583,7 @@
         ),
         scratch=(
             pltpu.VMEM((M * ROWS4, 128), f32),
-            pltpu.VMEM((height // 128, 3 * BS, 128), f32),
+            pltpu.VMEM((17, 3 * BS, 128), f32),
             pltpu.VMEM((3, depth, height), f32),
             pltpu.SemaphoreType.DMA((3,)),
             pltpu.SemaphoreType.DMA((3,)),

time: 79.1 us -> 77.4 us (0.979)
  waiting for transfers between devices: 31.4 us -> 30.1 us
    all_to_all x2, waiting for transfers between devices: 17.2 us -> 16.2 us  [within(): return lax.all_to_all(x, 'gx', 0, 0, tiled=True)]
  transfers between devices with their start and end apart: 6 -> 6, of which waited for: 4 -> 4; matrix products, arithmetic and copies ran while one was open for 4% -> 4% of each run, Pallas kernels for 15% -> 16%
where the time goes in v4:
time: 77.4 us; the launch traced here: 76.7 us
  waiting for transfers between devices  30.1 us (39%)
  starting transfers between devices  23.5 us (30%)
  Pallas kernels  17.9 us (23%)
  local copies, waits for them, and re-layouts  3.96 us (5%)
  between operations  0.78 us (1%)
    all_to_all x2, waiting for transfers between devices, within(): return lax.all_to_all(x, 'gx', 0, 0, tiled=True)  16.2 us
    all_to_all x2, waiting for transfers between devices, across(): x = lax.all_to_all(x, 'gx', 0, 0, tiled=True)  13.9 us
    all_to_all x2, starting transfers between devices, within(): return lax.all_to_all(x, 'gx', 0, 0, tiled=True)  11.2 us
    all_to_all x2, starting transfers between devices, across(): x = lax.all_to_all(x, 'gx', 0, 0, tiled=True)  7.78 us
    pallas_call x1, Pallas kernels, local(): call(ocean_kernel, (jax.ShapeDtypeStruct(thermal_state.shape, f32), jax.S...  4.76 us
    ppermute x1, starting transfers between devices, local(): lax.ppermute(head, 'gx', [((i + 1) % count, i) for i in range(count)])  4.09 us
    pallas_call x1, Pallas kernels, local(): call(ice_kernel, (jax.ShapeDtypeStruct(floe_motion.shape, f32), jax.Shape...  3.61 us
    pallas_call x1, Pallas kernels, local(): call(pack_kernel, (one_shape, nat_shape), scratch=(pltpu.VMEM((M, ROWS1,...  3.16 us
  transfers between devices with their start and end apart: 6, of which 4 were waited for; matrix products, arithmetic and copies ran while one was open for 4% of the time, Pallas kernels for 16%

profile of v4, /device:TPU:0, one launch (start us, length us, event | category | flops | bytes accessed | tf_op | source)
XLA Modules:
  0.0 76.7 jit_solution(17732324656754984357)
XLA Ops:
  0.6 3.2 %shard_map.137 = (bf16[16,136,128]{2,1,0:T(8,128)(2,1)}, f32[10,4,4096]{2,1,0:T(4,128)}) custom-call(s32[4]{0:T(128)} %ids.1, f32[8,64,1024]{2,1,0:T(8,128)} %temp.3, f32[2,64,1024]{2,1,0:T(8,128)} %drift.3, s32[4,4096]{1,0:T(4,128)} %cells.1, f32[5,4,4096]{2,1,0:T(4,128)} %bitcast.7, f32[5,4,4096]{2,1,0:T(4,128)} %bitcast.9, f32[4,2,4096]{2,1,0:T(2,128)} %motion.1, ...), custom_call_target="tpu_custom_call" | custom-call | tf_op jit(solution)/shard_map/pallas_call | solution.py:486
  3.8 0.0 copy-start.3
  3.8 7.5 %all-to-all-start = ((bf16[16,136,128]{2,1,0:T(8,128)(2,1)}), bf16[16,136,128]{2,1,0:T(8,128)(2,1)S(1)}, u32[]{:S(2)}, u32[]{:S(2)}) async-start(bf16[16,136,128]{2,1,0:T(8,128)(2,1)} %get-tuple-element.15), calls=%async_computation | async-start | bytes 1114112 | tf_op jit(solution)/shard_map/all_to_all | solution.py:458
  11.4 0.9 %fusion.2 = (f32[2,1,1024]{2,1,0:T(1,128)S(1)}, f32[2,1,1024]{2,1,0:T(1,128)S(1)}) fusion(f32[2,64,1024]{2,1,0:T(8,128)} %drift.3), kind=kLoop, calls=%fused_computation.14 | loop fusion | bytes 32768 | tf_op jit(solution)/shard_map/slice | solution.py:468
  12.2 1.1 %fusion.1 = (f32[8,1,1024]{2,1,0:T(1,128)S(1)}, f32[8,1,1024]{2,1,0:T(1,128)S(1)}) fusion(f32[8,64,1024]{2,1,0:T(8,128)} %temp.3), kind=kLoop, calls=%fused_computation.13 | loop fusion | bytes 131072 | tf_op jit(solution)/shard_map/slice | solution.py:468
  13.4 0.5 collective-permute-start
  13.9 4.1 %collective-permute-start.1 = (f32[10,1,1024]{2,1,0:T(1,128)S(1)}, f32[10,1,1024]{2,1,0:T(1,128)S(1)}, u32[]{:S(2)}, u32[]{:S(2)}) collective-permute-start(f32[10,1,1024]{2,1,0:T(1,128)S(1)} %pad_maximum_fusion.1), channel_id=1, source_target_pairs={{1,0},{2,1},{3,2},{4,3},{5,4},{6,5},{7,6},{8,7},{9,8},{10,9},{11,1... | collective-permute-start | bytes 122888 | tf_op jit(solution)/shard_map/ppermute | solution.py:470
  18.0 8.9 %all-to-all-done.got.everyone = bf16[16,136,128]{2,1,0:T(8,128)(2,1)S(1)} async-done(((bf16[16,136,128]{2,1,0:T(8,128)(2,1)}), bf16[16,136,128]{2,1,0:T(8,128)(2,1)S(1)}, u32[]{:S(2)}, u32[]{:S(2)}) %all-to-all-start) | async-done | bytes 557088 | tf_op jit(solution)/shard_map/all_to_all | solution.py:458
  26.8 0.1 copy.32
  26.9 0.1 copy.33
  27.0 0.1 broadcast_in_dim_reshape.2
  27.1 0.1 copy.34
  27.2 0.1 lt.16
  27.3 2.6 %shard_map.138 = bf16[16,88,128]{2,1,0:T(8,128)(2,1)} custom-call(s32[1]{0:T(128)} %bitcast.4.me, bf16[16,136,128]{2,1,0:T(8,128)(2,1)S(1)} %all-to-all-done.got.everyone, bf16[16,136,128]{2,1,0:T(8,128)(2,1)S(1)} %all-to-all-done.got.everyone), custom_call_target="tpu_custom_call" | custom-call | tf_op jit(solution)/shard_map/pallas_call | solution.py:501
  29.8 4.3 %all-to-all-start.1 = ((bf16[16,88,128]{2,1,0:T(8,128)(2,1)}), bf16[16,88,128]{2,1,0:T(8,128)(2,1)S(1)}, u32[]{:S(2)}, u32[]{:S(2)}) async-start(bf16[16,88,128]{2,1,0:T(8,128)(2,1)} %shard_map.138), calls=%async_computation.1 | async-start | bytes 720896 | tf_op jit(solution)/shard_map/all_to_all | solution.py:462
  34.1 0.2 convert_reduce_fusion
  34.3 0.1 mul.24
  34.4 0.1 copy.35
  34.5 0.1 copy.36
  34.6 0.1 add.44.codes
  34.7 11.1 %all-to-all-done.1.got = bf16[16,88,128]{2,1,0:T(8,128)(2,1)S(1)} async-done(((bf16[16,88,128]{2,1,0:T(8,128)(2,1)}), bf16[16,88,128]{2,1,0:T(8,128)(2,1)S(1)}, u32[]{:S(2)}, u32[]{:S(2)}) %all-to-all-start.1) | async-done | bytes 360480 | tf_op jit(solution)/shard_map/all_to_all | solution.py:462
  45.8 3.6 %shard_map.139 = (f32[4,2,4096]{2,1,0:T(2,128)}, f32[3,4,4096]{2,1,0:T(4,128)}, f32[5,4,4096]{2,1,0:T(4,128)}, bf16[16,24,128]{2,1,0:T(8,128)(2,1)}) custom-call(bf16[16,88,128]{2,1,0:T(8,128)(2,1)S(1)} %all-to-all-done.1.got, f32[10,4,4096]{2,1,0:T(4,128)S(1)} %copy-done.3, f32[5,4,4096]{2,1,0:T(4,128)S(1)} %bitcast.8, f32[5,4,4096]{2,1,0:T(4,128)S(1)} %bitcast.10), custom_call_target="tpu_custom_call" | custom-call | tf_op jit(solution)/shard_map/pallas_call | solution.py:532
  49.4 3.6 %all-to-all-start.2 = ((bf16[16,24,128]{2,1,0:T(8,128)(2,1)}), bf16[16,24,128]{2,1,0:T(8,128)(2,1)S(1)}, u32[]{:S(2)}, u32[]{:S(2)}) async-start(bf16[16,24,128]{2,1,0:T(8,128)(2,1)} %get-tuple-element.17._), calls=%async_computation.2 | async-start | bytes 196608 | tf_op jit(solution)/shard_map/all_to_all | solution.py:458
  53.0 7.4 %all-to-all-done.2.got = bf16[16,24,128]{2,1,0:T(8,128)(2,1)S(1)} async-done(((bf16[16,24,128]{2,1,0:T(8,128)(2,1)}), bf16[16,24,128]{2,1,0:T(8,128)(2,1)S(1)}, u32[]{:S(2)}, u32[]{:S(2)}) %all-to-all-start.2) | async-done | bytes 98336 | tf_op jit(solution)/shard_map/all_to_all | solution.py:458
  60.4 1.2 %shard_map.140 = bf16[16,48,128]{2,1,0:T(8,128)(2,1)} custom-call(bf16[16,24,128]{2,1,0:T(8,128)(2,1)S(1)} %all-to-all-done.2.got, s32[1,384]{1,0:T(1,128)S(1)} %add.44.codes), custom_call_target="tpu_custom_call" | custom-call | tf_op jit(solution)/shard_map/pallas_call | solution.py:565
  61.6 3.5 %all-to-all-start.3 = ((bf16[16,48,128]{2,1,0:T(8,128)(2,1)}), bf16[16,48,128]{2,1,0:T(8,128)(2,1)S(1)}, u32[]{:S(2)}, u32[]{:S(2)}) async-start(bf16[16,48,128]{2,1,0:T(8,128)(2,1)} %shard_map.140), calls=%async_computation.3 | async-start | bytes 393216 | tf_op jit(solution)/shard_map/all_to_all | solution.py:462
  65.1 0.1 select_reduce_fusion
  65.3 0.6 copy-done.4
  65.8 0.6 copy-done.5
  66.5 4.8 %shard_map.141 = (f32[8,64,1024]{2,1,0:T(8,128)}, f32[2,64,1024]{2,1,0:T(8,128)}) custom-call(f32[8,64,1024]{2,1,0:T(8,128)} %temp.3, f32[2,64,1024]{2,1,0:T(8,128)} %drift.3, s32[64,1024]{1,0:T(8,128)} %wet.3, f32[10,1,1024]{2,1,0:T(1,128)} %copy-done.4, f32[10,1,1024]{2,1,0:T(1,128)} %copy-done.5, bf16[16,24,128]{2,1,0:T(8,128)(2,1)} %get-tuple-element.17._), custom_call_target="tpu_custom_call" | custom-call | flops 10000000 | bytes 6000000 | tf_op jit(solution)/shard_map/pallas_call | solution.py:552
  71.2 2.8 %all-to-all-done.3.got = bf16[16,48,128]{2,1,0:T(8,128)(2,1)S(1)} async-done(((bf16[16,48,128]{2,1,0:T(8,128)(2,1)}), bf16[16,48,128]{2,1,0:T(8,128)(2,1)S(1)}, u32[]{:S(2)}, u32[]{:S(2)}) %all-to-all-start.3) | async-done | bytes 196640 | tf_op jit(solution)/shard_map/all_to_all | solution.py:462
  74.1 2.7 %shard_map.142 = (f32[8,64,1024]{2,1,0:T(8,128)}, f32[2,64,1024]{2,1,0:T(8,128)}) custom-call(s32[8]{0:T(128)S(1)} %broadcast_add_fusion.rows, bf16[16,48,128]{2,1,0:T(8,128)(2,1)S(1)} %all-to-all-done.3.got, s32[64,1024]{1,0:T(8,128)S(1)} %copy-done.2, f32[8,64,1024]{2,1,0:T(8,128)} %get-tuple-element.18.temp, ...), custom_call_target="tpu_custom_call", output_to_operand_aliasing={{0}: (3, {}), {1}: (4, {})} | custom-call | tf_op jit(solution)/shard_map/pallas_call | solution.py:578
  (21 shorter events, 0.2 us)
Async XLA Ops:
  3.8 42.0 %copy-start = (f32[4,5,4096]{2,0,1:T(4,128)S(1)}, f32[4,5,4096]{2,0,1:T(4,128)}, u32[]{:S(2)}) copy-start(f32[4,5,4096]{2,0,1:T(4,128)} %param.15) | copy-start | bytes 983044
  3.8 42.0 %copy-start.1 = (f32[4,5,4096]{2,0,1:T(4,128)S(1)}, f32[4,5,4096]{2,0,1:T(4,128)}, u32[]{:S(2)}) copy-start(f32[4,5,4096]{2,0,1:T(4,128)} %param.16) | copy-start | bytes 983044
  3.8 42.0 %copy-start.3 = (f32[10,4,4096]{2,1,0:T(4,128)S(1)}, f32[10,4,4096]{2,1,0:T(4,128)}, u32[]{:S(2)}) copy-start(f32[10,4,4096]{2,1,0:T(4,128)} %get-tuple-element.16.nat) | copy-start | bytes 1966084
  3.8 23.0 %all-to-all-start = ((bf16[16,136,128]{2,1,0:T(8,128)(2,1)}), bf16[16,136,128]{2,1,0:T(8,128)(2,1)S(1)}, u32[]{:S(2)}, u32[]{:S(2)}) async-start(bf16[16,136,128]{2,1,0:T(8,128)(2,1)} %get-tuple-element.15), calls=%async_computation | async-start | bytes 1114112 | tf_op jit(solution)/shard_map/all_to_all | solution.py:458
  13.4 51.9 %collective-permute-start = (f32[10,1,1024]{2,1,0:T(1,128)S(1)}, f32[10,1,1024]{2,1,0:T(1,128)S(1)}, u32[]{:S(2)}, u32[]{:S(2)}) collective-permute-start(f32[10,1,1024]{2,1,0:T(1,128)S(1)} %pad_maximum_fusion), channel_id=1, source_target_pairs={{0,1},{1,2},{2,3},{3,4},{4,5},{5,6},{6,7},{7,8},{8,9},{9,10},{10,1... | collective-permute-start | bytes 122888 | tf_op jit(solution)/shard_map/ppermute | solution.py:469
  13.9 51.4 %collective-permute-start.1 = (f32[10,1,1024]{2,1,0:T(1,128)S(1)}, f32[10,1,1024]{2,1,0:T(1,128)S(1)}, u32[]{:S(2)}, u32[]{:S(2)}) collective-permute-start(f32[10,1,1024]{2,1,0:T(1,128)S(1)} %pad_maximum_fusion.1), channel_id=1, source_target_pairs={{1,0},{2,1},{3,2},{4,3},{5,4},{6,5},{7,6},{8,7},{9,8},{10,9},{11,1... | collective-permute-start | bytes 122888 | tf_op jit(solution)/shard_map/ppermute | solution.py:470
  29.8 15.9 %all-to-all-start.1 = ((bf16[16,88,128]{2,1,0:T(8,128)(2,1)}), bf16[16,88,128]{2,1,0:T(8,128)(2,1)S(1)}, u32[]{:S(2)}, u32[]{:S(2)}) async-start(bf16[16,88,128]{2,1,0:T(8,128)(2,1)} %shard_map.138), calls=%async_computation.1 | async-start | bytes 720896 | tf_op jit(solution)/shard_map/all_to_all | solution.py:462
  49.4 24.7 %copy-start.2 = (s32[64,1024]{1,0:T(8,128)S(1)}, s32[64,1024]{1,0:T(8,128)}, u32[]{:S(2)}) copy-start(s32[64,1024]{1,0:T(8,128)} %wet.3) | copy-start | bytes 786436
  49.4 11.0 %all-to-all-start.2 = ((bf16[16,24,128]{2,1,0:T(8,128)(2,1)}), bf16[16,24,128]{2,1,0:T(8,128)(2,1)S(1)}, u32[]{:S(2)}, u32[]{:S(2)}) async-start(bf16[16,24,128]{2,1,0:T(8,128)(2,1)} %get-tuple-element.17._), calls=%async_computation.2 | async-start | bytes 196608 | tf_op jit(solution)/shard_map/all_to_all | solution.py:458
  61.6 12.5 %all-to-all-start.3 = ((bf16[16,48,128]{2,1,0:T(8,128)(2,1)}), bf16[16,48,128]{2,1,0:T(8,128)(2,1)S(1)}, u32[]{:S(2)}, u32[]{:S(2)}) async-start(bf16[16,48,128]{2,1,0:T(8,128)(2,1)} %shard_map.140), calls=%async_computation.3 | async-start | bytes 393216 | tf_op jit(solution)/shard_map/all_to_all | solution.py:462
  65.2 0.6 copy-start.4
  65.8 0.6 copy-start.5

commit v5 on v4

--- a/solution.py
+++ b/solution.py
@@ -14,9 +14,10 @@
 W = 8
 NF = 9
 ROWS1 = 136
-ROWS2 = 88
+ROWS2 = 80
 ROWS3 = 24
 ROWS4 = 48
+FREE = BS + 2 * W
 SEA = 12
 VMEM = 60 * 2**20
 ROOM = 40 * 2**20
@@ -181,6 +182,7 @@
     lane = lanes((size, 128))
     low, high = (lane & 63) < W, (lane & 63) >= BS - W
     rim = (m < 8).astype(f32)
+    corners = []
     for jj in range(3):
         first_part = jnp.zeros((size, 128), f32)
         last_part = jnp.zeros((size, 128), f32)
@@ -198,12 +200,22 @@
                 two = roll(collect[:, at + 4 : at + 8, :], 64 - W).reshape(size, 128)
                 own = own + rim * jnp.where(lane < 64, one, two)
             value = jnp.dot(centre, own.astype(bf16), preferred_element_type=f32)
-            collect[:, 52 + 4 * f : 56 + 4 * f, :] = value.reshape(count, 4, 128)
+            collect[:, 40 + 4 * f : 44 + 4 * f, :] = value.reshape(count, 4, 128)
             last_part = last_part + roll(jnp.where(high, own, 0.0), 16 * i)
             first_part = first_part + roll(jnp.where(low, own, 0.0), 16 * i)
         value = jnp.dot(before, last_part.astype(bf16), preferred_element_type=f32)
         value = value + jnp.dot(after, first_part.astype(bf16), preferred_element_type=f32)
-        collect[:, 40 + 4 * jj : 44 + 4 * jj, :] = value.reshape(count, 4, 128)
+        corners.append(value)
+    for g in range(8):
+        gap = jnp.zeros((size, 128), f32)
+        for jj in range(3):
+            start = 48 * g - 128 * jj
+            if -48 < start < 128:
+                place = lane + (start - FREE)
+                there = (lane >= FREE) & (place >= 0) & (place < 128)
+                gap = gap + jnp.where(there, roll(corners[jj], FREE - start), 0.0)
+        at = slice(4 * g, 4 * g + 4)
+        collect[:, at, :] = collect[:, at, :] + gap.reshape(count, 4, 128)
     for o in range(count):
         out[o] = collect[o].astype(bf16)
 
@@ -227,21 +239,32 @@
     for f in range(11):
         ext[f, 0] = jnp.zeros((8, 128), f32)
         ext[f, 49] = jnp.zeros((8, 128), f32)
+    lane4 = lanes((4, 128))
+    corners = {}
+    for m in range(8):
+        for jj in range(3):
+            value = jnp.zeros((4, 128), f32)
+            for g in range(8):
+                start = 48 * g - 128 * jj
+                if -48 < start < 128:
+                    there = (lane4 >= start) & (lane4 < start + 48)
+                    value = jnp.where(there, roll(rim(m, g), start - FREE), value)
+            corners[m, jj] = value
     inside = (lane >= W) & (lane < W + BS)
     for r in range(16):
         t = r % 8
         for p in range(2):
             own = (lane >> 3) == 8 * p + t
             for f in range(NF):
-                north = two(rim(8 + r // 8, 13 + f), rim(10 + r // 8, 13 + f))
-                south = two(rim(12 + r // 8, 13 + f), rim(14 + r // 8, 13 + f))
+                north = two(rim(8 + r // 8, 10 + f), rim(10 + r // 8, 10 + f))
+                south = two(rim(12 + r // 8, 10 + f), rim(14 + r // 8, 10 + f))
                 sides = roll(jnp.where(own, north, south), -(56 + 64 * p + 8 * t))
                 ext[f, 9 + 2 * r + p] = jnp.where(inside, roll(natural(f, r), 8 - 64 * p), sides)
     for f in range(NF):
         for y in range(8):
             p, i = y % 2, f % 4
-            centre = two(rim(4 + y // 2, 13 + f), rim(y // 2, 13 + f))
-            corner = two(rim(4 + y // 2, 10 + f // 4), rim(y // 2, 10 + f // 4))
+            centre = two(rim(4 + y // 2, 10 + f), rim(y // 2, 10 + f))
+            corner = two(corners[4 + y // 2, f // 4], corners[y // 2, f // 4])
             value = jnp.where(
                 inside, roll(centre, 8 - 64 * p), roll(corner, -(56 + 64 * p + 16 * i))
             )

time: 77.4 us -> 76.9 us (level)
  no operation moved by 1% of the time
where the time goes in v5:
time: 76.9 us; the launch traced here: 76.3 us
  waiting for transfers between devices  29.6 us (38%)
  starting transfers between devices  23.5 us (31%)
  Pallas kernels  18 us (23%)
  local copies, waits for them, and re-layouts  3.96 us (5%)
  between operations  0.78 us (1%)
    all_to_all x2, waiting for transfers between devices, within(): return lax.all_to_all(x, 'gx', 0, 0, tiled=True)  16.2 us
    all_to_all x2, waiting for transfers between devices, across(): x = lax.all_to_all(x, 'gx', 0, 0, tiled=True)  13.4 us
    all_to_all x2, starting transfers between devices, within(): return lax.all_to_all(x, 'gx', 0, 0, tiled=True)  11.2 us
    all_to_all x2, starting transfers between devices, across(): x = lax.all_to_all(x, 'gx', 0, 0, tiled=True)  7.78 us
    pallas_call x1, Pallas kernels, local(): call(ocean_kernel, (jax.ShapeDtypeStruct(thermal_state.shape, f32), jax.S...  4.76 us
    ppermute x1, starting transfers between devices, local(): lax.ppermute(head, 'gx', [((i + 1) % count, i) for i in range(count)])  4.09 us
    pallas_call x1, Pallas kernels, local(): call(ice_kernel, (jax.ShapeDtypeStruct(floe_motion.shape, f32), jax.Shape...  3.63 us
    pallas_call x1, Pallas kernels, local(): call(pack_kernel, (one_shape, nat_shape), scratch=(pltpu.VMEM((M, ROWS1,...  3.16 us
  transfers between devices with their start and end apart: 6, of which 4 were waited for; matrix products, arithmetic and copies ran while one was open for 4% of the time, Pallas kernels for 16%

profile of v5, /device:TPU:0, one launch (start us, length us, event | category | flops | bytes accessed | tf_op | source)
XLA Modules:
  0.0 76.3 jit_solution(13250351220330252307)
XLA Ops:
  0.6 3.2 %shard_map.137 = (bf16[16,136,128]{2,1,0:T(8,128)(2,1)}, f32[10,4,4096]{2,1,0:T(4,128)}) custom-call(s32[4]{0:T(128)} %ids.1, f32[8,64,1024]{2,1,0:T(8,128)} %temp.3, f32[2,64,1024]{2,1,0:T(8,128)} %drift.3, s32[4,4096]{1,0:T(4,128)} %cells.1, f32[5,4,4096]{2,1,0:T(4,128)} %bitcast.7, f32[5,4,4096]{2,1,0:T(4,128)} %bitcast.9, f32[4,2,4096]{2,1,0:T(2,128)} %motion.1, ...), custom_call_target="tpu_custom_call" | custom-call | tf_op jit(solution)/shard_map/pallas_call | solution.py:509
  3.8 0.0 copy-start.3
  3.8 7.5 %all-to-all-start = ((bf16[16,136,128]{2,1,0:T(8,128)(2,1)}), bf16[16,136,128]{2,1,0:T(8,128)(2,1)S(1)}, u32[]{:S(2)}, u32[]{:S(2)}) async-start(bf16[16,136,128]{2,1,0:T(8,128)(2,1)} %get-tuple-element.15), calls=%async_computation | async-start | bytes 1114112 | tf_op jit(solution)/shard_map/all_to_all | solution.py:481
  11.4 0.9 %fusion.2 = (f32[2,1,1024]{2,1,0:T(1,128)S(1)}, f32[2,1,1024]{2,1,0:T(1,128)S(1)}) fusion(f32[2,64,1024]{2,1,0:T(8,128)} %drift.3), kind=kLoop, calls=%fused_computation.14 | loop fusion | bytes 32768 | tf_op jit(solution)/shard_map/slice | solution.py:491
  12.2 1.1 %fusion.1 = (f32[8,1,1024]{2,1,0:T(1,128)S(1)}, f32[8,1,1024]{2,1,0:T(1,128)S(1)}) fusion(f32[8,64,1024]{2,1,0:T(8,128)} %temp.3), kind=kLoop, calls=%fused_computation.13 | loop fusion | bytes 131072 | tf_op jit(solution)/shard_map/slice | solution.py:491
  13.4 0.5 collective-permute-start
  13.9 4.1 %collective-permute-start.1 = (f32[10,1,1024]{2,1,0:T(1,128)S(1)}, f32[10,1,1024]{2,1,0:T(1,128)S(1)}, u32[]{:S(2)}, u32[]{:S(2)}) collective-permute-start(f32[10,1,1024]{2,1,0:T(1,128)S(1)} %pad_maximum_fusion.1), channel_id=1, source_target_pairs={{1,0},{2,1},{3,2},{4,3},{5,4},{6,5},{7,6},{8,7},{9,8},{10,9},{11,1... | collective-permute-start | bytes 122888 | tf_op jit(solution)/shard_map/ppermute | solution.py:493
  18.0 8.9 %all-to-all-done.got.everyone = bf16[16,136,128]{2,1,0:T(8,128)(2,1)S(1)} async-done(((bf16[16,136,128]{2,1,0:T(8,128)(2,1)}), bf16[16,136,128]{2,1,0:T(8,128)(2,1)S(1)}, u32[]{:S(2)}, u32[]{:S(2)}) %all-to-all-start) | async-done | bytes 557088 | tf_op jit(solution)/shard_map/all_to_all | solution.py:481
  26.8 0.1 copy.32
  26.9 0.1 copy.33
  27.0 0.1 broadcast_in_dim_reshape.2
  27.1 0.1 copy.34
  27.2 0.1 lt.16
  27.3 2.6 %shard_map.138 = bf16[16,80,128]{2,1,0:T(8,128)(2,1)} custom-call(s32[1]{0:T(128)} %bitcast.4.me, bf16[16,136,128]{2,1,0:T(8,128)(2,1)S(1)} %all-to-all-done.got.everyone, bf16[16,136,128]{2,1,0:T(8,128)(2,1)S(1)} %all-to-all-done.got.everyone), custom_call_target="tpu_custom_call" | custom-call | tf_op jit(solution)/shard_map/pallas_call | solution.py:524
  29.9 4.3 %all-to-all-start.1 = ((bf16[16,80,128]{2,1,0:T(8,128)(2,1)}), bf16[16,80,128]{2,1,0:T(8,128)(2,1)S(1)}, u32[]{:S(2)}, u32[]{:S(2)}) async-start(bf16[16,80,128]{2,1,0:T(8,128)(2,1)} %shard_map.138), calls=%async_computation.1 | async-start | bytes 655360 | tf_op jit(solution)/shard_map/all_to_all | solution.py:485
  34.2 0.2 convert_reduce_fusion
  34.4 0.1 mul.24
  34.4 0.1 copy.35
  34.5 0.1 copy.36
  34.6 0.1 add.44.codes
  34.8 10.5 %all-to-all-done.1.got = bf16[16,80,128]{2,1,0:T(8,128)(2,1)S(1)} async-done(((bf16[16,80,128]{2,1,0:T(8,128)(2,1)}), bf16[16,80,128]{2,1,0:T(8,128)(2,1)S(1)}, u32[]{:S(2)}, u32[]{:S(2)}) %all-to-all-start.1) | async-done | bytes 327712 | tf_op jit(solution)/shard_map/all_to_all | solution.py:485
  45.3 3.6 %shard_map.139 = (f32[4,2,4096]{2,1,0:T(2,128)}, f32[3,4,4096]{2,1,0:T(4,128)}, f32[5,4,4096]{2,1,0:T(4,128)}, bf16[16,24,128]{2,1,0:T(8,128)(2,1)}) custom-call(bf16[16,80,128]{2,1,0:T(8,128)(2,1)S(1)} %all-to-all-done.1.got, f32[10,4,4096]{2,1,0:T(4,128)S(1)} %copy-done.3, f32[5,4,4096]{2,1,0:T(4,128)S(1)} %bitcast.8, f32[5,4,4096]{2,1,0:T(4,128)S(1)} %bitcast.10), custom_call_target="tpu_custom_call" | custom-call | tf_op jit(solution)/shard_map/pallas_call | solution.py:555
  48.9 3.6 %all-to-all-start.2 = ((bf16[16,24,128]{2,1,0:T(8,128)(2,1)}), bf16[16,24,128]{2,1,0:T(8,128)(2,1)S(1)}, u32[]{:S(2)}, u32[]{:S(2)}) async-start(bf16[16,24,128]{2,1,0:T(8,128)(2,1)} %get-tuple-element.17._), calls=%async_computation.2 | async-start | bytes 196608 | tf_op jit(solution)/shard_map/all_to_all | solution.py:481
  52.6 7.4 %all-to-all-done.2.got = bf16[16,24,128]{2,1,0:T(8,128)(2,1)S(1)} async-done(((bf16[16,24,128]{2,1,0:T(8,128)(2,1)}), bf16[16,24,128]{2,1,0:T(8,128)(2,1)S(1)}, u32[]{:S(2)}, u32[]{:S(2)}) %all-to-all-start.2) | async-done | bytes 98336 | tf_op jit(solution)/shard_map/all_to_all | solution.py:481
  59.9 1.2 %shard_map.140 = bf16[16,48,128]{2,1,0:T(8,128)(2,1)} custom-call(bf16[16,24,128]{2,1,0:T(8,128)(2,1)S(1)} %all-to-all-done.2.got, s32[1,384]{1,0:T(1,128)S(1)} %add.44.codes), custom_call_target="tpu_custom_call" | custom-call | tf_op jit(solution)/shard_map/pallas_call | solution.py:588
  61.1 3.5 %all-to-all-start.3 = ((bf16[16,48,128]{2,1,0:T(8,128)(2,1)}), bf16[16,48,128]{2,1,0:T(8,128)(2,1)S(1)}, u32[]{:S(2)}, u32[]{:S(2)}) async-start(bf16[16,48,128]{2,1,0:T(8,128)(2,1)} %shard_map.140), calls=%async_computation.3 | async-start | bytes 393216 | tf_op jit(solution)/shard_map/all_to_all | solution.py:485
  64.6 0.1 select_reduce_fusion
  64.8 0.6 copy-done.4
  65.4 0.6 copy-done.5
  66.0 4.8 %shard_map.141 = (f32[8,64,1024]{2,1,0:T(8,128)}, f32[2,64,1024]{2,1,0:T(8,128)}) custom-call(f32[8,64,1024]{2,1,0:T(8,128)} %temp.3, f32[2,64,1024]{2,1,0:T(8,128)} %drift.3, s32[64,1024]{1,0:T(8,128)} %wet.3, f32[10,1,1024]{2,1,0:T(1,128)} %copy-done.4, f32[10,1,1024]{2,1,0:T(1,128)} %copy-done.5, bf16[16,24,128]{2,1,0:T(8,128)(2,1)} %get-tuple-element.17._), custom_call_target="tpu_custom_call" | custom-call | flops 10000000 | bytes 6000000 | tf_op jit(solution)/shard_map/pallas_call | solution.py:575
  70.8 2.8 %all-to-all-done.3.got = bf16[16,48,128]{2,1,0:T(8,128)(2,1)S(1)} async-done(((bf16[16,48,128]{2,1,0:T(8,128)(2,1)}), bf16[16,48,128]{2,1,0:T(8,128)(2,1)S(1)}, u32[]{:S(2)}, u32[]{:S(2)}) %all-to-all-start.3) | async-done | bytes 196640 | tf_op jit(solution)/shard_map/all_to_all | solution.py:485
  73.6 2.7 %shard_map.142 = (f32[8,64,1024]{2,1,0:T(8,128)}, f32[2,64,1024]{2,1,0:T(8,128)}) custom-call(s32[8]{0:T(128)S(1)} %broadcast_add_fusion.rows, bf16[16,48,128]{2,1,0:T(8,128)(2,1)S(1)} %all-to-all-done.3.got, s32[64,1024]{1,0:T(8,128)S(1)} %copy-done.2, f32[8,64,1024]{2,1,0:T(8,128)} %get-tuple-element.18.temp, ...), custom_call_target="tpu_custom_call", output_to_operand_aliasing={{0}: (3, {}), {1}: (4, {})} | custom-call | tf_op jit(solution)/shard_map/pallas_call | solution.py:601
  (21 shorter events, 0.2 us)
Async XLA Ops:
  3.8 41.5 %copy-start = (f32[4,5,4096]{2,0,1:T(4,128)S(1)}, f32[4,5,4096]{2,0,1:T(4,128)}, u32[]{:S(2)}) copy-start(f32[4,5,4096]{2,0,1:T(4,128)} %param.15) | copy-start | bytes 983044
  3.8 41.5 %copy-start.1 = (f32[4,5,4096]{2,0,1:T(4,128)S(1)}, f32[4,5,4096]{2,0,1:T(4,128)}, u32[]{:S(2)}) copy-start(f32[4,5,4096]{2,0,1:T(4,128)} %param.16) | copy-start | bytes 983044
  3.8 41.5 %copy-start.3 = (f32[10,4,4096]{2,1,0:T(4,128)S(1)}, f32[10,4,4096]{2,1,0:T(4,128)}, u32[]{:S(2)}) copy-start(f32[10,4,4096]{2,1,0:T(4,128)} %get-tuple-element.16.nat) | copy-start | bytes 1966084
  3.8 23.0 %all-to-all-start = ((bf16[16,136,128]{2,1,0:T(8,128)(2,1)}), bf16[16,136,128]{2,1,0:T(8,128)(2,1)S(1)}, u32[]{:S(2)}, u32[]{:S(2)}) async-start(bf16[16,136,128]{2,1,0:T(8,128)(2,1)} %get-tuple-element.15), calls=%async_computation | async-start | bytes 1114112 | tf_op jit(solution)/shard_map/all_to_all | solution.py:481
  13.4 51.4 %collective-permute-start = (f32[10,1,1024]{2,1,0:T(1,128)S(1)}, f32[10,1,1024]{2,1,0:T(1,128)S(1)}, u32[]{:S(2)}, u32[]{:S(2)}) collective-permute-start(f32[10,1,1024]{2,1,0:T(1,128)S(1)} %pad_maximum_fusion), channel_id=1, source_target_pairs={{0,1},{1,2},{2,3},{3,4},{4,5},{5,6},{6,7},{7,8},{8,9},{9,10},{10,1... | collective-permute-start | bytes 122888 | tf_op jit(solution)/shard_map/ppermute | solution.py:492
  13.9 50.9 %collective-permute-start.1 = (f32[10,1,1024]{2,1,0:T(1,128)S(1)}, f32[10,1,1024]{2,1,0:T(1,128)S(1)}, u32[]{:S(2)}, u32[]{:S(2)}) collective-permute-start(f32[10,1,1024]{2,1,0:T(1,128)S(1)} %pad_maximum_fusion.1), channel_id=1, source_target_pairs={{1,0},{2,1},{3,2},{4,3},{5,4},{6,5},{7,6},{8,7},{9,8},{10,9},{11,1... | collective-permute-start | bytes 122888 | tf_op jit(solution)/shard_map/ppermute | solution.py:493
  29.9 15.4 %all-to-all-start.1 = ((bf16[16,80,128]{2,1,0:T(8,128)(2,1)}), bf16[16,80,128]{2,1,0:T(8,128)(2,1)S(1)}, u32[]{:S(2)}, u32[]{:S(2)}) async-start(bf16[16,80,128]{2,1,0:T(8,128)(2,1)} %shard_map.138), calls=%async_computation.1 | async-start | bytes 655360 | tf_op jit(solution)/shard_map/all_to_all | solution.py:485
  48.9 24.7 %copy-start.2 = (s32[64,1024]{1,0:T(8,128)S(1)}, s32[64,1024]{1,0:T(8,128)}, u32[]{:S(2)}) copy-start(s32[64,1024]{1,0:T(8,128)} %wet.3) | copy-start | bytes 786436
  48.9 11.0 %all-to-all-start.2 = ((bf16[16,24,128]{2,1,0:T(8,128)(2,1)}), bf16[16,24,128]{2,1,0:T(8,128)(2,1)S(1)}, u32[]{:S(2)}, u32[]{:S(2)}) async-start(bf16[16,24,128]{2,1,0:T(8,128)(2,1)} %get-tuple-element.17._), calls=%async_computation.2 | async-start | bytes 196608 | tf_op jit(solution)/shard_map/all_to_all | solution.py:481
  61.1 12.5 %all-to-all-start.3 = ((bf16[16,48,128]{2,1,0:T(8,128)(2,1)}), bf16[16,48,128]{2,1,0:T(8,128)(2,1)S(1)}, u32[]{:S(2)}, u32[]{:S(2)}) async-start(bf16[16,48,128]{2,1,0:T(8,128)(2,1)} %shard_map.140), calls=%async_computation.3 | async-start | bytes 393216 | tf_op jit(solution)/shard_map/all_to_all | solution.py:485
  64.8 0.6 copy-start.4
  65.4 0.6 copy-start.5

commit v6 on v5

--- a/solution.py
+++ b/solution.py
@@ -415,14 +415,7 @@
             drift_out[k - levels] = mid + sea * change
 
 
-def final_kernel(
-    rows, got, wet, temp, drift, temp_out, drift_out, wide, flux, held, arrive, leave
-):
-    arrivals = []
-    for k in range(3):
-        place = temp.at[0] if k == 0 else drift.at[k - 1]
-        arrivals.append(pltpu.make_async_copy(place, held.at[k], arrive.at[k]))
-        arrivals[-1].start()
+def final_kernel(rows, got, wet, temp, drift, temp_out, drift_out, wide, flux):
     for m in range(M):
         wide[pl.ds(ROWS4 * m, ROWS4), :] = got[m].astype(f32)
     flux[0:16] = jnp.zeros((16,) + flux.shape[1:], f32)
@@ -434,20 +427,16 @@
                 flux[r, pl.ds(BS * f + 2 * h, M, stride=4), :] = value
                 flux[r, pl.ds(BS * f + 2 * h + 1, M, stride=4), :] = roll(value, 64)
     left = lanes((BS, 128)) < 64
-    copies = []
     for k in range(3):
-        arrivals[k].wait()
         for part in range(8):
             cut = slice(128 * part, 128 * part + 128)
             rows_of = slice(BS * k, BS * (k + 1))
             pair = jnp.where(left, flux[2 * part, rows_of, :], roll(flux[2 * part + 1, rows_of, :], 64))
             added = wet[:, cut].astype(f32) * pair
-            held[k, :, cut] = held[k, :, cut] + added
-        place = temp_out.at[0] if k == 0 else drift_out.at[k - 1]
-        copies.append(pltpu.make_async_copy(held.at[k], place, leave.at[k]))
-        copies[-1].start()
-    for copy in copies:
-        copy.wait()
+            if k == 0:
+                temp_out[0, :, cut] = temp[0, :, cut] + added
+            else:
+                drift_out[k - 1, :, cut] = drift[k - 1, :, cut] + added
 
 
 def local(
@@ -607,12 +596,10 @@
         scratch=(
             pltpu.VMEM((M * ROWS4, 128), f32),
             pltpu.VMEM((17, 3 * BS, 128), f32),
-            pltpu.VMEM((3, depth, height), f32),
-            pltpu.SemaphoreType.DMA((3,)),
-            pltpu.SemaphoreType.DMA((3,)),
-        ),
-        in_specs=[smem, vmem, vmem, anywhere, anywhere],
-        out_specs=(anywhere, anywhere),
+        ),
+        grid=(1,),
+        in_specs=[smem, whole(got4), whole(sea_site_indicator), top, whole(drift_new)],
+        out_specs=(top, whole(drift_new)),
         input_output_aliases={3: 0, 4: 1},
         vmem=ROOM,
     )(slot_rows, got4, sea_site_indicator, temp_new, drift_new)

time: 76.9 us -> 76.7 us (level)
  no operation moved by 1% of the time
where the time goes in v6:
time: 76.7 us; the launch traced here: 76.1 us
  waiting for transfers between devices  29.6 us (39%)
  starting transfers between devices  23.5 us (31%)
  Pallas kernels  17.9 us (23%)
  local copies, waits for them, and re-layouts  3.96 us (5%)
  between operations  0.78 us (1%)
    all_to_all x2, waiting for transfers between devices, within(): return lax.all_to_all(x, 'gx', 0, 0, tiled=True)  16.2 us
    all_to_all x2, waiting for transfers between devices, across(): x = lax.all_to_all(x, 'gx', 0, 0, tiled=True)  13.4 us
    all_to_all x2, starting transfers between devices, within(): return lax.all_to_all(x, 'gx', 0, 0, tiled=True)  11.2 us
    all_to_all x2, starting transfers between devices, across(): x = lax.all_to_all(x, 'gx', 0, 0, tiled=True)  7.78 us
    pallas_call x1, Pallas kernels, local(): call(ocean_kernel, (jax.ShapeDtypeStruct(thermal_state.shape, f32), jax.S...  4.76 us
    ppermute x1, starting transfers between devices, local(): lax.ppermute(head, 'gx', [((i + 1) % count, i) for i in range(count)])  4.09 us
    pallas_call x1, Pallas kernels, local(): call(ice_kernel, (jax.ShapeDtypeStruct(floe_motion.shape, f32), jax.Shape...  3.63 us
    pallas_call x1, Pallas kernels, local(): call(pack_kernel, (one_shape, nat_shape), scratch=(pltpu.VMEM((M, ROWS1,...  3.16 us
  transfers between devices with their start and end apart: 6, of which 4 were waited for; matrix products, arithmetic and copies ran while one was open for 4% of the time, Pallas kernels for 16%

profile of v6, /device:TPU:0, one launch (start us, length us, event | category | flops | bytes accessed | tf_op | source)
XLA Modules:
  0.0 76.1 jit_solution(948629723992348501)
XLA Ops:
  0.6 3.2 %shard_map.137 = (bf16[16,136,128]{2,1,0:T(8,128)(2,1)}, f32[10,4,4096]{2,1,0:T(4,128)}) custom-call(s32[4]{0:T(128)} %ids.1, f32[8,64,1024]{2,1,0:T(8,128)} %temp.3, f32[2,64,1024]{2,1,0:T(8,128)} %drift.3, s32[4,4096]{1,0:T(4,128)} %cells.1, f32[5,4,4096]{2,1,0:T(4,128)} %bitcast.7, f32[5,4,4096]{2,1,0:T(4,128)} %bitcast.9, f32[4,2,4096]{2,1,0:T(2,128)} %motion.1, ...), custom_call_target="tpu_custom_call" | custom-call | tf_op jit(solution)/shard_map/pallas_call | solution.py:498
  3.8 0.0 copy-start.3
  3.8 7.5 %all-to-all-start = ((bf16[16,136,128]{2,1,0:T(8,128)(2,1)}), bf16[16,136,128]{2,1,0:T(8,128)(2,1)S(1)}, u32[]{:S(2)}, u32[]{:S(2)}) async-start(bf16[16,136,128]{2,1,0:T(8,128)(2,1)} %get-tuple-element.15), calls=%async_computation | async-start | bytes 1114112 | tf_op jit(solution)/shard_map/all_to_all | solution.py:470
  11.4 0.9 %fusion.2 = (f32[2,1,1024]{2,1,0:T(1,128)S(1)}, f32[2,1,1024]{2,1,0:T(1,128)S(1)}) fusion(f32[2,64,1024]{2,1,0:T(8,128)} %drift.3), kind=kLoop, calls=%fused_computation.14 | loop fusion | bytes 32768 | tf_op jit(solution)/shard_map/slice | solution.py:480
  12.2 1.1 %fusion.1 = (f32[8,1,1024]{2,1,0:T(1,128)S(1)}, f32[8,1,1024]{2,1,0:T(1,128)S(1)}) fusion(f32[8,64,1024]{2,1,0:T(8,128)} %temp.3), kind=kLoop, calls=%fused_computation.13 | loop fusion | bytes 131072 | tf_op jit(solution)/shard_map/slice | solution.py:480
  13.4 0.5 collective-permute-start
  13.9 4.1 %collective-permute-start.1 = (f32[10,1,1024]{2,1,0:T(1,128)S(1)}, f32[10,1,1024]{2,1,0:T(1,128)S(1)}, u32[]{:S(2)}, u32[]{:S(2)}) collective-permute-start(f32[10,1,1024]{2,1,0:T(1,128)S(1)} %pad_maximum_fusion.1), channel_id=1, source_target_pairs={{1,0},{2,1},{3,2},{4,3},{5,4},{6,5},{7,6},{8,7},{9,8},{10,9},{11,1... | collective-permute-start | bytes 122888 | tf_op jit(solution)/shard_map/ppermute | solution.py:482
  18.0 8.9 %all-to-all-done.got.everyone = bf16[16,136,128]{2,1,0:T(8,128)(2,1)S(1)} async-done(((bf16[16,136,128]{2,1,0:T(8,128)(2,1)}), bf16[16,136,128]{2,1,0:T(8,128)(2,1)S(1)}, u32[]{:S(2)}, u32[]{:S(2)}) %all-to-all-start) | async-done | bytes 557088 | tf_op jit(solution)/shard_map/all_to_all | solution.py:470
  26.8 0.1 copy.32
  26.9 0.1 copy.33
  27.0 0.1 broadcast_in_dim_reshape.2
  27.1 0.1 copy.34
  27.2 0.1 lt.16
  27.3 2.6 %shard_map.138 = bf16[16,80,128]{2,1,0:T(8,128)(2,1)} custom-call(s32[1]{0:T(128)} %bitcast.4.me, bf16[16,136,128]{2,1,0:T(8,128)(2,1)S(1)} %all-to-all-done.got.everyone, bf16[16,136,128]{2,1,0:T(8,128)(2,1)S(1)} %all-to-all-done.got.everyone), custom_call_target="tpu_custom_call" | custom-call | tf_op jit(solution)/shard_map/pallas_call | solution.py:513
  29.9 4.3 %all-to-all-start.1 = ((bf16[16,80,128]{2,1,0:T(8,128)(2,1)}), bf16[16,80,128]{2,1,0:T(8,128)(2,1)S(1)}, u32[]{:S(2)}, u32[]{:S(2)}) async-start(bf16[16,80,128]{2,1,0:T(8,128)(2,1)} %shard_map.138), calls=%async_computation.1 | async-start | bytes 655360 | tf_op jit(solution)/shard_map/all_to_all | solution.py:474
  34.2 0.2 convert_reduce_fusion
  34.4 0.1 mul.24
  34.4 0.1 copy.35
  34.5 0.1 copy.36
  34.6 0.1 add.44.codes
  34.8 10.5 %all-to-all-done.1.got = bf16[16,80,128]{2,1,0:T(8,128)(2,1)S(1)} async-done(((bf16[16,80,128]{2,1,0:T(8,128)(2,1)}), bf16[16,80,128]{2,1,0:T(8,128)(2,1)S(1)}, u32[]{:S(2)}, u32[]{:S(2)}) %all-to-all-start.1) | async-done | bytes 327712 | tf_op jit(solution)/shard_map/all_to_all | solution.py:474
  45.3 3.6 %shard_map.139 = (f32[4,2,4096]{2,1,0:T(2,128)}, f32[3,4,4096]{2,1,0:T(4,128)}, f32[5,4,4096]{2,1,0:T(4,128)}, bf16[16,24,128]{2,1,0:T(8,128)(2,1)}) custom-call(bf16[16,80,128]{2,1,0:T(8,128)(2,1)S(1)} %all-to-all-done.1.got, f32[10,4,4096]{2,1,0:T(4,128)S(1)} %copy-done.3, f32[5,4,4096]{2,1,0:T(4,128)S(1)} %bitcast.8, f32[5,4,4096]{2,1,0:T(4,128)S(1)} %bitcast.10), custom_call_target="tpu_custom_call" | custom-call | tf_op jit(solution)/shard_map/pallas_call | solution.py:544
  48.9 3.6 %all-to-all-start.2 = ((bf16[16,24,128]{2,1,0:T(8,128)(2,1)}), bf16[16,24,128]{2,1,0:T(8,128)(2,1)S(1)}, u32[]{:S(2)}, u32[]{:S(2)}) async-start(bf16[16,24,128]{2,1,0:T(8,128)(2,1)} %get-tuple-element.17._), calls=%async_computation.2 | async-start | bytes 196608 | tf_op jit(solution)/shard_map/all_to_all | solution.py:470
  52.6 7.4 %all-to-all-done.2.got = bf16[16,24,128]{2,1,0:T(8,128)(2,1)S(1)} async-done(((bf16[16,24,128]{2,1,0:T(8,128)(2,1)}), bf16[16,24,128]{2,1,0:T(8,128)(2,1)S(1)}, u32[]{:S(2)}, u32[]{:S(2)}) %all-to-all-start.2) | async-done | bytes 98336 | tf_op jit(solution)/shard_map/all_to_all | solution.py:470
  59.9 1.2 %shard_map.140 = bf16[16,48,128]{2,1,0:T(8,128)(2,1)} custom-call(bf16[16,24,128]{2,1,0:T(8,128)(2,1)S(1)} %all-to-all-done.2.got, s32[1,384]{1,0:T(1,128)S(1)} %add.44.codes), custom_call_target="tpu_custom_call" | custom-call | tf_op jit(solution)/shard_map/pallas_call | solution.py:577
  61.1 3.5 %all-to-all-start.3 = ((bf16[16,48,128]{2,1,0:T(8,128)(2,1)}), bf16[16,48,128]{2,1,0:T(8,128)(2,1)S(1)}, u32[]{:S(2)}, u32[]{:S(2)}) async-start(bf16[16,48,128]{2,1,0:T(8,128)(2,1)} %shard_map.140), calls=%async_computation.3 | async-start | bytes 393216 | tf_op jit(solution)/shard_map/all_to_all | solution.py:474
  64.6 0.1 select_reduce_fusion
  64.8 0.6 copy-done.4
  65.4 0.6 copy-done.5
  66.0 4.8 %shard_map.141 = (f32[8,64,1024]{2,1,0:T(8,128)}, f32[2,64,1024]{2,1,0:T(8,128)}) custom-call(f32[8,64,1024]{2,1,0:T(8,128)} %temp.3, f32[2,64,1024]{2,1,0:T(8,128)} %drift.3, s32[64,1024]{1,0:T(8,128)} %wet.3, f32[10,1,1024]{2,1,0:T(1,128)} %copy-done.4, f32[10,1,1024]{2,1,0:T(1,128)} %copy-done.5, bf16[16,24,128]{2,1,0:T(8,128)(2,1)} %get-tuple-element.17._), custom_call_target="tpu_custom_call" | custom-call | flops 10000000 | bytes 6000000 | tf_op jit(solution)/shard_map/pallas_call | solution.py:564
  70.8 2.8 %all-to-all-done.3.got = bf16[16,48,128]{2,1,0:T(8,128)(2,1)S(1)} async-done(((bf16[16,48,128]{2,1,0:T(8,128)(2,1)}), bf16[16,48,128]{2,1,0:T(8,128)(2,1)S(1)}, u32[]{:S(2)}, u32[]{:S(2)}) %all-to-all-start.3) | async-done | bytes 196640 | tf_op jit(solution)/shard_map/all_to_all | solution.py:474
  73.6 2.5 %shard_map.142 = (f32[8,64,1024]{2,1,0:T(8,128)}, f32[2,64,1024]{2,1,0:T(8,128)}) custom-call(s32[8]{0:T(128)S(1)} %broadcast_add_fusion.rows, bf16[16,48,128]{2,1,0:T(8,128)(2,1)S(1)} %all-to-all-done.3.got, s32[64,1024]{1,0:T(8,128)S(1)} %copy-done.2, f32[8,64,1024]{2,1,0:T(8,128)} %get-tuple-element.18.temp, ...), custom_call_target="tpu_custom_call", output_to_operand_aliasing={{0}: (3, {}), {1}: (4, {})} | custom-call | tf_op jit(solution)/shard_map/pallas_call | solution.py:590
  (21 shorter events, 0.2 us)
Async XLA Ops:
  3.8 41.5 %copy-start = (f32[4,5,4096]{2,0,1:T(4,128)S(1)}, f32[4,5,4096]{2,0,1:T(4,128)}, u32[]{:S(2)}) copy-start(f32[4,5,4096]{2,0,1:T(4,128)} %param.15) | copy-start | bytes 983044
  3.8 41.5 %copy-start.1 = (f32[4,5,4096]{2,0,1:T(4,128)S(1)}, f32[4,5,4096]{2,0,1:T(4,128)}, u32[]{:S(2)}) copy-start(f32[4,5,4096]{2,0,1:T(4,128)} %param.16) | copy-start | bytes 983044
  3.8 41.5 %copy-start.3 = (f32[10,4,4096]{2,1,0:T(4,128)S(1)}, f32[10,4,4096]{2,1,0:T(4,128)}, u32[]{:S(2)}) copy-start(f32[10,4,4096]{2,1,0:T(4,128)} %get-tuple-element.16.nat) | copy-start | bytes 1966084
  3.8 23.0 %all-to-all-start = ((bf16[16,136,128]{2,1,0:T(8,128)(2,1)}), bf16[16,136,128]{2,1,0:T(8,128)(2,1)S(1)}, u32[]{:S(2)}, u32[]{:S(2)}) async-start(bf16[16,136,128]{2,1,0:T(8,128)(2,1)} %get-tuple-element.15), calls=%async_computation | async-start | bytes 1114112 | tf_op jit(solution)/shard_map/all_to_all | solution.py:470
  13.4 51.4 %collective-permute-start = (f32[10,1,1024]{2,1,0:T(1,128)S(1)}, f32[10,1,1024]{2,1,0:T(1,128)S(1)}, u32[]{:S(2)}, u32[]{:S(2)}) collective-permute-start(f32[10,1,1024]{2,1,0:T(1,128)S(1)} %pad_maximum_fusion), channel_id=1, source_target_pairs={{0,1},{1,2},{2,3},{3,4},{4,5},{5,6},{6,7},{7,8},{8,9},{9,10},{10,1... | collective-permute-start | bytes 122888 | tf_op jit(solution)/shard_map/ppermute | solution.py:481
  13.9 50.9 %collective-permute-start.1 = (f32[10,1,1024]{2,1,0:T(1,128)S(1)}, f32[10,1,1024]{2,1,0:T(1,128)S(1)}, u32[]{:S(2)}, u32[]{:S(2)}) collective-permute-start(f32[10,1,1024]{2,1,0:T(1,128)S(1)} %pad_maximum_fusion.1), channel_id=1, source_target_pairs={{1,0},{2,1},{3,2},{4,3},{5,4},{6,5},{7,6},{8,7},{9,8},{10,9},{11,1... | collective-permute-start | bytes 122888 | tf_op jit(solution)/shard_map/ppermute | solution.py:482
  29.9 15.4 %all-to-all-start.1 = ((bf16[16,80,128]{2,1,0:T(8,128)(2,1)}), bf16[16,80,128]{2,1,0:T(8,128)(2,1)S(1)}, u32[]{:S(2)}, u32[]{:S(2)}) async-start(bf16[16,80,128]{2,1,0:T(8,128)(2,1)} %shard_map.138), calls=%async_computation.1 | async-start | bytes 655360 | tf_op jit(solution)/shard_map/all_to_all | solution.py:474
  48.9 24.7 %copy-start.2 = (s32[64,1024]{1,0:T(8,128)S(1)}, s32[64,1024]{1,0:T(8,128)}, u32[]{:S(2)}) copy-start(s32[64,1024]{1,0:T(8,128)} %wet.3) | copy-start | bytes 786436
  48.9 11.0 %all-to-all-start.2 = ((bf16[16,24,128]{2,1,0:T(8,128)(2,1)}), bf16[16,24,128]{2,1,0:T(8,128)(2,1)S(1)}, u32[]{:S(2)}, u32[]{:S(2)}) async-start(bf16[16,24,128]{2,1,0:T(8,128)(2,1)} %get-tuple-element.17._), calls=%async_computation.2 | async-start | bytes 196608 | tf_op jit(solution)/shard_map/all_to_all | solution.py:470
  61.1 12.5 %all-to-all-start.3 = ((bf16[16,48,128]{2,1,0:T(8,128)(2,1)}), bf16[16,48,128]{2,1,0:T(8,128)(2,1)S(1)}, u32[]{:S(2)}, u32[]{:S(2)}) async-start(bf16[16,48,128]{2,1,0:T(8,128)(2,1)} %shard_map.140), calls=%async_computation.3 | async-start | bytes 393216 | tf_op jit(solution)/shard_map/all_to_all | solution.py:474
  64.8 0.6 copy-start.4
  65.4 0.6 copy-start.5
